TPU v7x, 128 devices: a whole 4x4x4 slice. The times are simulated.
128 devices in a mesh: col: 8 (over y_hi, x), ex: 16 (over z, y_lo, core).
Axes of the slice: x: 4, y: 4 (y_hi: 2, y_lo: 2; y = y_hi * 2 + y_lo), z: 4, core: 2. Of those that a mesh axis runs over, the one named last changes fastest.
Arguments:
- features: bfloat16 [8192, 8192], P('ex', 'col'), as said below
Outputs:
- gram: float32 [8192, 8192], P(('col', 'ex'))
Inputs may be any that keep to these rules, and one draw needn't show every extreme that they name: `features`: Real-valued projected gradients.
All inputs are finite; a program needn't handle non-finite values.
Results may differ from a plain program's by a relative error of at most 0.0003.
Values may be sent and summed in bfloat16 or wider, within the bound.
No kernel may reach another device: no remote copies, remote signals or barrier semaphores. Data moves between devices by JAX's collectives and lax.ppermute only.
A program may use at most 192 MiB of HBM per device.

v0:
```python
import jax
import jax.numpy as jnp
from jax import lax
from jax.sharding import PartitionSpec as P

damping = 0.5


def from_behind(shard, axis, by):
    peers = lax.axis_size(axis)
    return lax.ppermute(shard, axis, [(i, (i + by) % peers) for i in range(peers)])


def local_tile(left, right):
    return lax.dot_general(
        left, right, (((0,), (0,)), ((), ())), preferred_element_type=jnp.float32
    )


def add_damping(result):
    strip = result.shape[0]
    owner = lax.axis_index("col") * lax.axis_size("ex") + lax.axis_index("ex")
    row_ids = owner * strip + lax.broadcasted_iota(jnp.int32, result.shape, 0)
    col_ids = lax.broadcasted_iota(jnp.int32, result.shape, 1)
    return result + jnp.where(row_ids == col_ids, jnp.float32(damping), jnp.float32(0.0))


def per_device(features):
    ncols = lax.axis_size("col")
    index = lax.axis_index("col")
    current = features
    pieces = []
    for offset in range(ncols):
        pieces.append(local_tile(features, current))
        if offset + 1 < ncols:
            current = from_behind(current, "col", 1)
    ordered = [pieces[0]] + pieces[1:][::-1]
    stacked = jnp.stack(ordered, 1)
    reduced = lax.psum_scatter(stacked, "ex", scatter_dimension=0, tiled=True)
    rolled = jnp.roll(reduced, index, axis=1)
    result = rolled.reshape(rolled.shape[0], ncols * rolled.shape[2])
    return add_damping(result)


def solution(mesh):
    placed = (P("ex", "col"),)
    return jax.shard_map(
        per_device, mesh=mesh, in_specs=placed, out_specs=P(("col", "ex"), None), check_vma=False
    )
```

profile of v0, /device:TPU:0, one launch (start us, length us, event | category | flops | bytes accessed | tf_op | source)
XLA Modules:
  0.0 572.1 jit_solution(17941270836682666557)
XLA Ops:
  6.5 0.0 copy-start
  6.5 0.0 reduce-scatter.2.cloned.1.call-start
  6.5 1.6 collective-permute-start
  8.1 27.3 %collective-permute-done = bf16[512,1024]{1,0:T(8,128)(2,1)S(1)} collective-permute-done((bf16[512,1024]{1,0:T(8,128)(2,1)}, bf16[512,1024]{1,0:T(8,128)(2,1)S(1)}, u32[]{:S(2)}, u32[]{:S(2)}) %collective-permute-start) | collective-permute-done | bytes 1048608 | tf_op jit(solution)/shard_map/ppermute | solution.py:11
  35.4 0.0 collective-permute-start.1
  35.5 27.8 %collective-permute-done.1 = bf16[512,1024]{1,0:T(8,128)(2,1)S(1)} collective-permute-done((bf16[512,1024]{1,0:T(8,128)(2,1)S(1)}, bf16[512,1024]{1,0:T(8,128)(2,1)S(1)}, u32[]{:S(2)}, u32[]{:S(2)}) %collective-permute-start.1) | collective-permute-done | bytes 1048608 | tf_op jit(solution)/shard_map/ppermute | solution.py:11
  63.3 0.0 collective-permute-start.2
  63.3 26.9 %collective-permute-done.2 = bf16[512,1024]{1,0:T(8,128)(2,1)S(1)} collective-permute-done((bf16[512,1024]{1,0:T(8,128)(2,1)S(1)}, bf16[512,1024]{1,0:T(8,128)(2,1)S(1)}, u32[]{:S(2)}, u32[]{:S(2)}) %collective-permute-start.2) | collective-permute-done | bytes 1048608 | tf_op jit(solution)/shard_map/ppermute | solution.py:11
  90.2 0.0 collective-permute-start.3
  90.2 26.0 %collective-permute-done.3 = bf16[512,1024]{1,0:T(8,128)(2,1)S(1)} collective-permute-done((bf16[512,1024]{1,0:T(8,128)(2,1)S(1)}, bf16[512,1024]{1,0:T(8,128)(2,1)S(1)}, u32[]{:S(2)}, u32[]{:S(2)}) %collective-permute-start.3) | collective-permute-done | bytes 1048608 | tf_op jit(solution)/shard_map/ppermute | solution.py:11
  116.2 0.0 collective-permute-start.4
  116.2 25.1 %collective-permute-done.4 = bf16[512,1024]{1,0:T(8,128)(2,1)S(1)} collective-permute-done((bf16[512,1024]{1,0:T(8,128)(2,1)S(1)}, bf16[512,1024]{1,0:T(8,128)(2,1)S(1)}, u32[]{:S(2)}, u32[]{:S(2)}) %collective-permute-start.4) | collective-permute-done | bytes 1048608 | tf_op jit(solution)/shard_map/ppermute | solution.py:11
  141.3 0.0 collective-permute-start.5
  141.3 24.2 %collective-permute-done.5 = bf16[512,1024]{1,0:T(8,128)(2,1)S(1)} collective-permute-done((bf16[512,1024]{1,0:T(8,128)(2,1)S(1)}, bf16[512,1024]{1,0:T(8,128)(2,1)S(1)}, u32[]{:S(2)}, u32[]{:S(2)}) %collective-permute-start.5) | collective-permute-done | bytes 1048608 | tf_op jit(solution)/shard_map/ppermute | solution.py:11
  165.5 0.0 collective-permute-start.6
  165.5 4.9 bitcast_dynamic-update-slice_fusion.7
  170.4 18.4 %collective-permute-done.6 = bf16[512,1024]{1,0:T(8,128)(2,1)S(1)} collective-permute-done((bf16[512,1024]{1,0:T(8,128)(2,1)S(1)}, bf16[512,1024]{1,0:T(8,128)(2,1)S(1)}, u32[]{:S(2)}, u32[]{:S(2)}) %collective-permute-start.6) | collective-permute-done | bytes 1048608 | tf_op jit(solution)/shard_map/ppermute | solution.py:11
  188.7 0.0 copy-done
  188.7 3.3 bitcast_dynamic-update-slice_fusion.6
  192.0 3.3 bitcast_dynamic-update-slice_fusion.5
  195.3 3.2 bitcast_dynamic-update-slice_fusion.4
  198.5 3.2 bitcast_dynamic-update-slice_fusion.3
  201.8 3.3 bitcast_dynamic-update-slice_fusion.2
  205.0 3.3 bitcast_dynamic-update-slice_fusion.1
  208.3 3.2 bitcast_dynamic-update-slice_fusion
  211.5 0.0 reduce-scatter.2.cloned.1.call-update
  211.6 349.8 %reduce-scatter.2.cloned.1.call-done = f32[64,8,1024]{2,0,1:T(8,128)} async-done(((f32[1024,8,1024]{2,0,1:T(8,128)}), f32[64,8,1024]{2,0,1:T(8,128)}) %reduce-scatter.2.cloned.1.call-update) | async-done | bytes 2097168 | tf_op jit(solution)/shard_map/reduce_scatter | solution.py:39
  561.4 2.1 fusion.1
  563.4 0.2 copy.3
  563.7 1.6 select_add_fusion
  (1 shorter events, 0.0 us)
Async XLA Ops:
  6.5 182.2 %copy-start = (bf16[512,1024]{1,0:T(8,128)(2,1)S(1)}, bf16[512,1024]{1,0:T(8,128)(2,1)}, u32[]{:S(2)}) copy-start(bf16[512,1024]{1,0:T(8,128)(2,1)} %param.1) | copy-start | bytes 3145732
  6.5 554.8 %reduce-scatter.2.cloned.1.call-start = ((), (), s32[]{:S(2)}) async-start(), calls=%async_computation.1 | async-start | bytes 35651584 | tf_op jit(solution)/shard_map/reduce_scatter | solution.py:39
  6.5 28.9 %collective-permute-start = (bf16[512,1024]{1,0:T(8,128)(2,1)}, bf16[512,1024]{1,0:T(8,128)(2,1)S(1)}, u32[]{:S(2)}, u32[]{:S(2)}) collective-permute-start(bf16[512,1024]{1,0:T(8,128)(2,1)} %param.1), channel_id=1, source_target_pairs={{0,16},{16,32},{32,48},{48,64},{64,80},{80,96},{96,112},{112,0},{1... | collective-permute-start | bytes 3145736 | tf_op jit(solution)/shard_map/ppermute | solution.py:11
  35.4 27.8 %collective-permute-start.1 = (bf16[512,1024]{1,0:T(8,128)(2,1)S(1)}, bf16[512,1024]{1,0:T(8,128)(2,1)S(1)}, u32[]{:S(2)}, u32[]{:S(2)}) collective-permute-start(bf16[512,1024]{1,0:T(8,128)(2,1)S(1)} %collective-permute-done), channel_id=1, source_target_pairs={{0,16},{16,32},{32,48},{48,64},{64,80},{80,96},{96,112},{112,0},{1... | collective-permute-start | bytes 3145736 | tf_op jit(solution)/shard_map/ppermute | solution.py:11
  63.3 26.9 %collective-permute-start.2 = (bf16[512,1024]{1,0:T(8,128)(2,1)S(1)}, bf16[512,1024]{1,0:T(8,128)(2,1)S(1)}, u32[]{:S(2)}, u32[]{:S(2)}) collective-permute-start(bf16[512,1024]{1,0:T(8,128)(2,1)S(1)} %collective-permute-done.1), channel_id=1, source_target_pairs={{0,16},{16,32},{32,48},{48,64},{64,80},{80,96},{96,112},{112,0},{1... | collective-permute-start | bytes 3145736 | tf_op jit(solution)/shard_map/ppermute | solution.py:11
  90.2 26.0 %collective-permute-start.3 = (bf16[512,1024]{1,0:T(8,128)(2,1)S(1)}, bf16[512,1024]{1,0:T(8,128)(2,1)S(1)}, u32[]{:S(2)}, u32[]{:S(2)}) collective-permute-start(bf16[512,1024]{1,0:T(8,128)(2,1)S(1)} %collective-permute-done.2), channel_id=1, source_target_pairs={{0,16},{16,32},{32,48},{48,64},{64,80},{80,96},{96,112},{112,0},{1... | collective-permute-start | bytes 3145736 | tf_op jit(solution)/shard_map/ppermute | solution.py:11
  116.2 25.1 %collective-permute-start.4 = (bf16[512,1024]{1,0:T(8,128)(2,1)S(1)}, bf16[512,1024]{1,0:T(8,128)(2,1)S(1)}, u32[]{:S(2)}, u32[]{:S(2)}) collective-permute-start(bf16[512,1024]{1,0:T(8,128)(2,1)S(1)} %collective-permute-done.3), channel_id=1, source_target_pairs={{0,16},{16,32},{32,48},{48,64},{64,80},{80,96},{96,112},{112,0},{1... | collective-permute-start | bytes 3145736 | tf_op jit(solution)/shard_map/ppermute | solution.py:11
  141.3 24.2 %collective-permute-start.5 = (bf16[512,1024]{1,0:T(8,128)(2,1)S(1)}, bf16[512,1024]{1,0:T(8,128)(2,1)S(1)}, u32[]{:S(2)}, u32[]{:S(2)}) collective-permute-start(bf16[512,1024]{1,0:T(8,128)(2,1)S(1)} %collective-permute-done.4), channel_id=1, source_target_pairs={{0,16},{16,32},{32,48},{48,64},{64,80},{80,96},{96,112},{112,0},{1... | collective-permute-start | bytes 3145736 | tf_op jit(solution)/shard_map/ppermute | solution.py:11
  165.5 23.2 %collective-permute-start.6 = (bf16[512,1024]{1,0:T(8,128)(2,1)S(1)}, bf16[512,1024]{1,0:T(8,128)(2,1)S(1)}, u32[]{:S(2)}, u32[]{:S(2)}) collective-permute-start(bf16[512,1024]{1,0:T(8,128)(2,1)S(1)} %collective-permute-done.5), channel_id=1, source_target_pairs={{0,16},{16,32},{32,48},{48,64},{64,80},{80,96},{96,112},{112,0},{1... | collective-permute-start | bytes 3145736 | tf_op jit(solution)/shard_map/ppermute | solution.py:11
Sparse Core Ops, SparseCore 0:
  211.7 349.6 reduce-scatter.1
where the time goes:
time: 572 us
  waiting for transfers between devices  525 us (92%)
  matrix products  27.7 us (5%)
  between operations  13.4 us (2%)
    reduce_scatter x1, waiting for transfers between devices, per_device(): reduced = lax.psum_scatter(stacked, 'ex', scatter_dimension=0, tiled=True)  350 us
    ppermute x7, waiting for transfers between devices, from_behind(): lax.ppermute(shard, axis, [(i, (i + by) % peers) for i in range(peers)])  176 us
    dot_general x8, matrix products, local_tile(): lax.dot_general(left, right, (((0,), (0,)), ((), ())), preferred_element_...  27.7 us
  transfers between devices with their start and end apart: 8, of which 8 were waited for; matrix products, arithmetic and copies ran while one was open for 1% of the time, Pallas kernels for 0%

commit v1 on v0

v1 whole, which is shorter than its diff:
```python
import jax
import jax.numpy as jnp
from jax import lax
from jax.sharding import Mesh, PartitionSpec as P

damping = 0.5
parts = ("yh", "x", "z", "yl", "core")
sizes = (2, 4, 4, 2, 2)
ring = ("yh", "yl")


def swap(value, axis):
    return lax.ppermute(value, axis, [(0, 1), (1, 0)])


def trade(value, axis, bits):
    return lax.ppermute(value, axis, [(i, i ^ bits) for i in range(4)])


def ring_gather(value, axis):
    near = trade(value, axis, 1)
    far = trade(value, axis, 3)
    half = value.shape[0] // 2
    opposite = jnp.concatenate([trade(far[:half], axis, 1), trade(near[half:], axis, 3)], 0)
    return value, near, opposite, far


def pick(value, index, axis):
    return lax.dynamic_index_in_dim(value, index, axis, keepdims=False)


def add_damping(result):
    strip = result.shape[0]
    owner = jnp.int32(0)
    for name, size in zip(parts, sizes):
        owner = owner * size + lax.axis_index(name)
    row_ids = owner * strip + lax.broadcasted_iota(jnp.int32, result.shape, 0)
    col_ids = lax.broadcasted_iota(jnp.int32, result.shape, 1)
    return result + jnp.where(row_ids == col_ids, jnp.float32(damping), jnp.float32(0.0))


def per_device(features):
    yh, x, yl, core = (lax.axis_index(name) for name in ("yh", "x", "yl", "core"))
    rows, cols = features.shape
    strip = cols // 8

    largest = lax.pmax(jnp.max(jnp.abs(features)).astype(jnp.float32), parts)
    largest = jnp.maximum(largest, jnp.float32(1e-18))
    shrink, grow = 4.0 / largest, largest * 0.25

    split = features.reshape(rows, 4, 2, strip)
    kept = pick(split, yl, 2).reshape(rows, cols // 2)
    given = pick(split, 1 - yl, 2).reshape(rows, cols // 2)
    left = ring_gather(jnp.concatenate([kept, swap(given, "yl")], 0), "x")
    left = jnp.concatenate(left, 1)
    left = jnp.concatenate([left, swap(left, "core")], 0)

    own, near, opposite, far = ring_gather(features, ring)
    right = jnp.concatenate([jnp.concatenate([own, near], 0), jnp.concatenate([opposite, far], 0)], 1)
    right = right.reshape(2 * rows, 2, 2, cols // 2)
    kept = pick(right, core, 2).reshape(2 * rows, cols)
    given = pick(right, 1 - core, 2).reshape(2 * rows, cols)
    right = jnp.concatenate([kept, swap(given, "core")], 0)

    tile = lax.dot_general(left, right, (((0,), (0,)), ((), ())), preferred_element_type=jnp.float32)
    tile = (tile * shrink * shrink).astype(jnp.float16).reshape(4, 4, strip, cols)
    packed = jnp.stack([pick(tile, x ^ n, 0) for n in range(4)]).reshape(16, strip, cols)
    came = lax.all_to_all(packed, ("x", "z"), 0, 0, tiled=True)
    came = came.reshape(4, 4, strip, cols).astype(jnp.float32).sum(1) * grow * grow

    came = came.reshape(4, 2, strip // 2, 2, cols // 2)
    kept = pick(came, core, 1)
    got = swap(pick(came, 1 - core, 1), "core")
    low, high = jnp.where(core == 0, kept, got), jnp.where(core == 0, got, kept)
    both = jnp.stack([low, high], 3)
    both = jnp.where(yh == 0, both, both[:, :, ::-1])
    result = both.transpose(1, 2, 0, 3, 4).reshape(strip // 2, 8 * cols)
    return add_damping(result)


def solution(mesh):
    fine = Mesh(mesh.devices.reshape(sizes), parts)
    return jax.shard_map(
        per_device,
        mesh=fine,
        in_specs=(P(("z", "yl", "core"), ("yh", "x")),),
        out_specs=P(parts, None),
        check_vma=False,
    )
```

time: 572 us -> 289 us (0.51)
  waiting for transfers between devices: 525 us -> 123 us
  blocking collectives: 0 us -> 66.9 us
  other arithmetic: 3.68 us -> 34.7 us
  local copies, waits for them, and re-layouts: 0.24 us -> 17.6 us
  starting transfers between devices: 1.59 us -> 18.1 us
  between operations: 13.4 us -> 0.91 us
    reduce_scatter x1 -> x0, waiting for transfers between devices: 350 us -> none  [per_device(): reduced = lax.psum_scatter(stacked, 'ex', scatter_dimension=0, tiled=True)]
    ppermute x7 -> x12, waiting for transfers between devices: 176 us -> 59.5 us  [the longest x8 45 us: trade(): return lax.ppermute(value, axis, [(i, i ^ bits) for i in range(4)])]
    pmax x0 -> x1, blocking collectives: none -> 66.9 us  [per_device(): largest = lax.pmax(jnp.max(jnp.abs(features)).astype(jnp.float32), parts)]
    all_to_all x0 -> x1, waiting for transfers between devices: none -> 63.4 us  [per_device(): came = lax.all_to_all(packed, ('x', 'z'), 0, 0, tiled=True)]
    concatenate x0 -> x3, other arithmetic: none -> 23.2 us  [the longest x1 14.6 us: per_device(): left = jnp.concatenate(left, 1)]
    ppermute x7 -> x12, starting transfers between devices: 1.59 us -> 13.6 us  [the longest x8 11.7 us: trade(): return lax.ppermute(value, axis, [(i, i ^ bits) for i in range(4)])]
    dot_general x8 -> x1, matrix products: 27.7 us -> 24.3 us  [per_device(): lax.dot_general(left, right, (((0,), (0,)), ((), ())), preferred_element_...]
  transfers between devices with their start and end apart: 8 -> 13, of which waited for: 8 -> 9; matrix products, arithmetic and copies ran while one was open for 1% -> 10% of each run, Pallas kernels for 0% -> 0%
where the time goes in v1:
time: 289 us; the launch traced here: 285 us
  waiting for transfers between devices  123 us (43%)
  blocking collectives  66.9 us (23%)
  other arithmetic  34.7 us (12%)
  matrix products  24.3 us (8%)
  starting transfers between devices  18.1 us (6%)
  local copies, waits for them, and re-layouts  17.6 us (6%)
    pmax x1, blocking collectives, per_device(): largest = lax.pmax(jnp.max(jnp.abs(features)).astype(jnp.float32), parts)  66.9 us
    all_to_all x1, waiting for transfers between devices, per_device(): came = lax.all_to_all(packed, ('x', 'z'), 0, 0, tiled=True)  63.4 us
    ppermute x8, waiting for transfers between devices, trade(): return lax.ppermute(value, axis, [(i, i ^ bits) for i in range(4)])  45 us
    dot_general x1, matrix products, per_device(): lax.dot_general(left, right, (((0,), (0,)), ((), ())), preferred_element_...  24.3 us
    concatenate x1, other arithmetic, per_device(): left = jnp.concatenate(left, 1)  14.6 us
    ppermute x4, waiting for transfers between devices, swap(): return lax.ppermute(value, axis, [(0, 1), (1, 0)])  14.5 us
    ppermute x8, starting transfers between devices, trade(): return lax.ppermute(value, axis, [(i, i ^ bits) for i in range(4)])  11.7 us
    concatenate x1, other arithmetic, per_device(): jnp.concatenate([jnp.concatenate([own, near], 0), jnp.concatenate([opposi...  8.5 us
  transfers between devices with their start and end apart: 13, of which 9 were waited for; matrix products, arithmetic and copies ran while one was open for 10% of the time, Pallas kernels for 0%

profile of v1, /device:TPU:0, one launch (start us, length us, event | category | flops | bytes accessed | tf_op | source)
XLA Modules:
  0.0 285.4 jit_solution(7037355570228211340)
XLA Ops:
  0.0 1.5 copy.8
  1.5 0.1 constant_dynamic-slice_fusion.9
  1.6 1.7 collective-permute-start
  3.3 11.9 %collective-permute-done = bf16[512,512]{0,1:T(8,128)(2,1)S(1)} collective-permute-done((bf16[512,512]{0,1:T(8,128)(2,1)S(1)}, bf16[512,512]{0,1:T(8,128)(2,1)S(1)}, u32[]{:S(2)}, u32[]{:S(2)}) %collective-permute-start) | collective-permute-done | bytes 524320 | tf_op jit(solution)/shard_map/ppermute | solution.py:13
  15.2 0.1 pad_maximum_fusion.3
  15.4 3.0 %collective-permute-start.2 = (bf16[1024,512]{0,1:T(8,128)(2,1)S(1)}, bf16[1024,512]{0,1:T(8,128)(2,1)S(1)}, u32[]{:S(2)}, u32[]{:S(2)}) collective-permute-start(bf16[1024,512]{0,1:T(8,128)(2,1)S(1)} %pad_maximum_fusion.3), channel_id=1, source_target_pairs={{0,48},{16,32},{32,16},{48,0},{1,49},{17,33},{33,17},{49,1},{2,50}... | collective-permute-start | bytes 3145736 | tf_op jit(solution)/shard_map/ppermute | solution.py:17
  18.4 0.2 collective-permute-start.1
  18.6 22.1 %collective-permute-done.2 = bf16[1024,512]{0,1:T(8,128)(2,1)S(1)} collective-permute-done((bf16[1024,512]{0,1:T(8,128)(2,1)S(1)}, bf16[1024,512]{0,1:T(8,128)(2,1)S(1)}, u32[]{:S(2)}, u32[]{:S(2)}) %collective-permute-start.2) | collective-permute-done | bytes 1048608 | tf_op jit(solution)/shard_map/ppermute | solution.py:17
  40.7 0.6 collective-permute-start.3
  41.3 1.5 collective-permute-done.1
  42.8 1.1 collective-permute-start.4
  43.9 3.0 %collective-permute-start.7 = (bf16[512,1024]{0,1:T(8,128)(2,1)S(1)}, bf16[512,1024]{0,1:T(8,128)(2,1)S(1)}, u32[]{:S(2)}, u32[]{:S(2)}) collective-permute-start(bf16[512,1024]{0,1:T(8,128)(2,1)S(1)} %copy.8), channel_id=1, source_target_pairs={{0,66},{2,64},{64,2},{66,0},{1,67},{3,65},{65,3},{67,1},{4,70},{6,... | collective-permute-start | bytes 3145736 | tf_op jit(solution)/shard_map/ppermute | solution.py:17
  46.9 0.1 collective-permute-start.6
  47.0 6.3 %collective-permute-done.3 = bf16[512,512]{0,1:T(8,128)(2,1)S(1)} collective-permute-done((bf16[512,512]{0,1:T(8,128)(2,1)S(1)}, bf16[512,512]{0,1:T(8,128)(2,1)S(1)}, u32[]{:S(2)}, u32[]{:S(2)}) %collective-permute-start.3) | collective-permute-done | bytes 524320 | tf_op jit(solution)/shard_map/ppermute | solution.py:17
  53.4 1.7 collective-permute-done.4
  55.0 14.6 %pad_maximum_fusion = bf16[1024,2048]{0,1:T(8,128)(2,1)} fusion(bf16[1024,512]{0,1:T(8,128)(2,1)S(1)} %collective-permute-done.2, bf16[512,512]{0,1:T(8,128)(2,1)S(1)} %collective-permute-done.4, bf16[512,512]{0,1:T(8,128)(2,1)S(1)} %collective-permute-done.3, bf16[1024,512]{0,1:T(8,128)(2,1)S(1)} %collective-permute-done.1, ...), kind=kLoop, calls=%fused_computation.16 | loop fusion | flops 25165824 | bytes 8388608 | tf_op jit(solution)/shard_map/concatenate | solution.py:55
  69.7 0.0 collective-permute-start.5
  69.7 0.0 copy-start.2
  69.7 0.9 slice.18
  70.6 1.6 collective-permute-start.8
  72.2 0.9 slice.19
  73.1 0.4 copy-done.3
  73.4 2.2 collective-permute-start.9
  75.6 9.6 %collective-permute-done.8 = bf16[256,1024]{0,1:T(8,128)(2,1)} collective-permute-done((bf16[256,1024]{0,1:T(8,128)(2,1)}, bf16[256,1024]{0,1:T(8,128)(2,1)}, u32[]{:S(2)}, u32[]{:S(2)}) %collective-permute-start.8) | collective-permute-done | bytes 524320 | tf_op jit(solution)/shard_map/ppermute | solution.py:17
  85.3 3.7 %collective-permute-done.9 = bf16[256,1024]{0,1:T(8,128)(2,1)} collective-permute-done((bf16[256,1024]{0,1:T(8,128)(2,1)}, bf16[256,1024]{0,1:T(8,128)(2,1)}, u32[]{:S(2)}, u32[]{:S(2)}) %collective-permute-start.9) | collective-permute-done | bytes 524320 | tf_op jit(solution)/shard_map/ppermute | solution.py:17
  89.0 8.5 %maximum_maximum_fusion = bf16[1024,2048]{0,1:T(8,128)(2,1)S(1)} fusion(bf16[512,1024]{0,1:T(8,128)(2,1)} %copy-done.2, bf16[256,1024]{0,1:T(8,128)(2,1)} %collective-permute-done.9, bf16[256,1024]{0,1:T(8,128)(2,1)} %collective-permute-done.8, bf16[512,1024]{0,1:T(8,128)(2,1)} %copy-done.3, bf16[512,1024]{0,1:T(8,128)(2,1)S(1)} %copy.8), kind=kLoop, calls=%fused_computation.17 | loop fusion | flops 20971520 | bytes 8388608 | tf_op jit(solution)/shard_map/concatenate | solution.py:59
  97.5 0.0 copy-start
  97.5 2.5 constant_dynamic-slice_fusion.7
  100.0 0.8 abs_reduce_fusion
  100.8 66.9 %pmax.7 = f32[]{:T(128)} all-reduce(bf16[]{:T(256)} %abs_reduce_fusion), channel_id=1, replica_groups=mesh['yh'=2,'x'=4,'z'=4,'yl'=2,'core'=2] {'yh','x','z','yl','core'}, use_global_device_ids=true, to_apply=%region_1.0 | all-reduce | flops 1 | bytes 6 | tf_op jit(solution)/shard_map/pmax | solution.py:47
  168.4 24.3 %multiply_convert_fusion = f16[2048,1024]{1,0:T(8,128)(2,1)S(1)} fusion(f32[]{:T(128)S(6)} %div.3, bf16[1024,1024]{0,1:T(8,128)(2,1)} %collective-permute-done.10, bf16[1024,1024]{0,1:T(8,128)(2,1)} %bitcast.36, bf16[1024,2048]{0,1:T(8,128)(2,1)} %collective-permute-done.5, bf16[1024,512]{0,1:T(8,128)(2,1)S(1)} %collective-permute-done.2, ...), kind=kOutput, calls=%fused_computation.15 | convolution fusion | flops 8663334912 | bytes 16777220 | tf_op jit(solution)/shard_map/dot_general | solution.py:65
  192.7 1.3 constant_dynamic-slice_fusion.5
  194.1 3.0 %pad_maximum_fusion.1 = f16[4,4,128,1024]{3,2,1,0:T(8,128)(2,1)} fusion(f16[1,4,128,1024]{3,2,1,0:T(8,128)(2,1)S(1)} %get-tuple-element.6, f16[1,4,128,1024]{3,2,1,0:T(8,128)(2,1)S(1)} %get-tuple-element.7, f16[1,4,128,1024]{3,2,1,0:T(8,128)(2,1)S(1)} %get-tuple-element.8, f16[1,4,128,1024]{3,2,1,0:T(8,128)(2,1)S(1)} %get-tuple-element.5), kind=kLoop, calls=%fused_computation.21 | loop fusion | flops 6291456 | bytes 8388608 | tf_op jit(solution)/shard_map/stack | solution.py:67
  197.1 4.5 %all-to-all-start = ((f16[16,128,1024]{2,1,0:T(8,128)(2,1)}), f16[16,128,1024]{2,1,0:T(8,128)(2,1)}, u32[]{:S(2)}, u32[]{:S(2)}) async-start(f16[16,128,1024]{2,1,0:T(8,128)(2,1)} %bitcast.29), calls=%async_computation | async-start | bytes 8388608 | tf_op jit(solution)/shard_map/all_to_all | solution.py:68
  201.6 63.4 %all-to-all-done = f16[16,128,1024]{2,1,0:T(8,128)(2,1)} async-done(((f16[16,128,1024]{2,1,0:T(8,128)(2,1)}), f16[16,128,1024]{2,1,0:T(8,128)(2,1)}, u32[]{:S(2)}, u32[]{:S(2)}) %all-to-all-start) | async-done | bytes 4194336 | tf_op jit(solution)/shard_map/all_to_all | solution.py:68
  265.0 3.6 %convert_reduce_fusion = f32[4,128,1024]{2,1,0:T(8,128)S(1)} fusion(f16[16,128,1024]{2,1,0:T(8,128)(2,1)} %all-to-all-done), kind=kLoop, calls=%fused_computation.14 | loop fusion | flops 3670016 | bytes 6291456 | tf_op jit(solution)/shard_map/reduce_sum | solution.py:69
  268.6 1.7 multiply_multiply_fusion
  270.3 3.0 %mul.51 = f32[4,2,64,2,512]{4,3,2,1,0:T(2,128)S(1)} reshape(f32[4,128,1024]{2,1,0:T(8,128)} %multiply_multiply_fusion) | data formatting | bytes 4194304 | tf_op jit(solution)/shard_map/mul | solution.py:69
  273.3 0.7 constant_dynamic-slice_fusion.1
  274.0 0.2 copy.19
  274.2 0.1 collective-permute-start.11
  274.4 2.6 collective-permute-done.11
  277.0 0.3 fusion.22
  277.3 0.2 pad_maximum_fusion.2
  277.5 0.2 fusion.21
  277.8 2.9 %copy.15 = f32[64,2,4,2,512]{4,3,2,1,0:T(2,128)} copy(f32[64,2,4,2,512]{4,0,1,2,3:T(8,128)S(1)} %fusion.21) | data formatting | bytes 4194304 | tf_op jit(solution)/shard_map/transpose | solution.py:77
  280.7 3.1 %reshape.48 = f32[64,8192]{1,0:T(8,128)S(1)} reshape(f32[64,2,4,2,512]{4,3,2,1,0:T(2,128)} %copy.15) | data formatting | bytes 4194304 | tf_op jit(solution)/shard_map/reshape | solution.py:77
  283.8 1.6 select_add_fusion
  (17 shorter events, 0.1 us)
Async XLA Ops:
  1.6 13.7 %collective-permute-start = (bf16[512,512]{0,1:T(8,128)(2,1)S(1)}, bf16[512,512]{0,1:T(8,128)(2,1)S(1)}, u32[]{:S(2)}, u32[]{:S(2)}) collective-permute-start(bf16[512,512]{0,1:T(8,128)(2,1)S(1)} %bitcast.38), channel_id=1, source_target_pairs={{0,2},{2,0},{1,3},{3,1},{4,6},{6,4},{5,7},{7,5},{8,10},{10,8},{9,1... | collective-permute-start | bytes 1572872 | tf_op jit(solution)/shard_map/ppermute | solution.py:13
  15.4 25.3 %collective-permute-start.2 = (bf16[1024,512]{0,1:T(8,128)(2,1)S(1)}, bf16[1024,512]{0,1:T(8,128)(2,1)S(1)}, u32[]{:S(2)}, u32[]{:S(2)}) collective-permute-start(bf16[1024,512]{0,1:T(8,128)(2,1)S(1)} %pad_maximum_fusion.3), channel_id=1, source_target_pairs={{0,48},{16,32},{32,16},{48,0},{1,49},{17,33},{33,17},{49,1},{2,50}... | collective-permute-start | bytes 3145736 | tf_op jit(solution)/shard_map/ppermute | solution.py:17
  18.4 24.4 %collective-permute-start.1 = (bf16[1024,512]{0,1:T(8,128)(2,1)S(1)}, bf16[1024,512]{0,1:T(8,128)(2,1)S(1)}, u32[]{:S(2)}, u32[]{:S(2)}) collective-permute-start(bf16[1024,512]{0,1:T(8,128)(2,1)S(1)} %pad_maximum_fusion.3), channel_id=1, source_target_pairs={{0,16},{16,0},{32,48},{48,32},{1,17},{17,1},{33,49},{49,33},{2,18}... | collective-permute-start | bytes 3145736 | tf_op jit(solution)/shard_map/ppermute | solution.py:17
  40.7 12.7 %collective-permute-start.3 = (bf16[512,512]{0,1:T(8,128)(2,1)S(1)}, bf16[512,512]{0,1:T(8,128)(2,1)S(1)}, u32[]{:S(2)}, u32[]{:S(2)}) collective-permute-start(bf16[512,512]{0,1:T(8,128)(2,1)S(1)} %slice.16), channel_id=1, source_target_pairs={{0,16},{16,0},{32,48},{48,32},{1,17},{17,1},{33,49},{49,33},{2,18}... | collective-permute-start | bytes 1572872 | tf_op jit(solution)/shard_map/ppermute | solution.py:17
  42.8 29.4 %copy-start.1 = (bf16[1024,512]{0,1:T(8,128)(2,1)}, bf16[1024,512]{0,1:T(8,128)(2,1)S(1)}, u32[]{:S(2)}) copy-start(bf16[1024,512]{0,1:T(8,128)(2,1)S(1)} %collective-permute-done.1) | copy-start | bytes 3145732
  42.8 12.2 %collective-permute-start.4 = (bf16[512,512]{0,1:T(8,128)(2,1)S(1)}, bf16[512,512]{0,1:T(8,128)(2,1)S(1)}, u32[]{:S(2)}, u32[]{:S(2)}) collective-permute-start(bf16[512,512]{0,1:T(8,128)(2,1)S(1)} %slice.17), channel_id=1, source_target_pairs={{0,48},{16,32},{32,16},{48,0},{1,49},{17,33},{33,17},{49,1},{2,50}... | collective-permute-start | bytes 1572872 | tf_op jit(solution)/shard_map/ppermute | solution.py:17
  43.9 25.8 %collective-permute-start.7 = (bf16[512,1024]{0,1:T(8,128)(2,1)S(1)}, bf16[512,1024]{0,1:T(8,128)(2,1)S(1)}, u32[]{:S(2)}, u32[]{:S(2)}) collective-permute-start(bf16[512,1024]{0,1:T(8,128)(2,1)S(1)} %copy.8), channel_id=1, source_target_pairs={{0,66},{2,64},{64,2},{66,0},{1,67},{3,65},{65,3},{67,1},{4,70},{6,... | collective-permute-start | bytes 3145736 | tf_op jit(solution)/shard_map/ppermute | solution.py:17
  46.9 25.3 %collective-permute-start.6 = (bf16[512,1024]{0,1:T(8,128)(2,1)S(1)}, bf16[512,1024]{0,1:T(8,128)(2,1)S(1)}, u32[]{:S(2)}, u32[]{:S(2)}) collective-permute-start(bf16[512,1024]{0,1:T(8,128)(2,1)S(1)} %copy.8), channel_id=1, source_target_pairs={{0,2},{2,0},{64,66},{66,64},{1,3},{3,1},{65,67},{67,65},{4,6},{6,4... | collective-permute-start | bytes 3145736 | tf_op jit(solution)/shard_map/ppermute | solution.py:17
  53.4 16.3 %copy-start.4 = (bf16[512,512]{0,1:T(8,128)(2,1)}, bf16[512,512]{0,1:T(8,128)(2,1)S(1)}, u32[]{:S(2)}) copy-start(bf16[512,512]{0,1:T(8,128)(2,1)S(1)} %collective-permute-done.3) | copy-start | bytes 1572868
  55.0 14.6 %copy-start.5 = (bf16[512,512]{0,1:T(8,128)(2,1)}, bf16[512,512]{0,1:T(8,128)(2,1)S(1)}, u32[]{:S(2)}) copy-start(bf16[512,512]{0,1:T(8,128)(2,1)S(1)} %collective-permute-done.4) | copy-start | bytes 1572868
  69.7 98.8 %collective-permute-start.5 = (bf16[1024,2048]{0,1:T(8,128)(2,1)}, bf16[1024,2048]{0,1:T(8,128)(2,1)}, u32[]{:S(2)}, u32[]{:S(2)}) collective-permute-start(bf16[1024,2048]{0,1:T(8,128)(2,1)} %pad_maximum_fusion), channel_id=1, source_target_pairs={{0,1},{1,0},{2,3},{3,2},{4,5},{5,4},{6,7},{7,6},{8,9},{9,8},{10,11... | collective-permute-start | bytes 12582920 | tf_op jit(solution)/shard_map/ppermute | solution.py:13
  69.7 3.4 %copy-start.2 = (bf16[512,1024]{0,1:T(8,128)(2,1)}, bf16[512,1024]{0,1:T(8,128)(2,1)S(1)}, u32[]{:S(2)}) copy-start(bf16[512,1024]{0,1:T(8,128)(2,1)S(1)} %collective-permute-done.7) | copy-start | bytes 3145732
  70.6 14.6 %collective-permute-start.8 = (bf16[256,1024]{0,1:T(8,128)(2,1)}, bf16[256,1024]{0,1:T(8,128)(2,1)}, u32[]{:S(2)}, u32[]{:S(2)}) collective-permute-start(bf16[256,1024]{0,1:T(8,128)(2,1)} %slice.18), channel_id=1, source_target_pairs={{0,2},{2,0},{64,66},{66,64},{1,3},{3,1},{65,67},{67,65},{4,6},{6,4... | collective-permute-start | bytes 1572872 | tf_op jit(solution)/shard_map/ppermute | solution.py:17
  72.2 1.2 copy-start.3
  73.4 15.6 %collective-permute-start.9 = (bf16[256,1024]{0,1:T(8,128)(2,1)}, bf16[256,1024]{0,1:T(8,128)(2,1)}, u32[]{:S(2)}, u32[]{:S(2)}) collective-permute-start(bf16[256,1024]{0,1:T(8,128)(2,1)} %slice.19), channel_id=1, source_target_pairs={{0,66},{2,64},{64,2},{66,0},{1,67},{3,65},{65,3},{67,1},{4,70},{6,... | collective-permute-start | bytes 1572872 | tf_op jit(solution)/shard_map/ppermute | solution.py:17
  97.5 2.5 copy-start
  100.0 68.4 %collective-permute-start.10 = (bf16[1024,1024]{0,1:T(8,128)(2,1)}, bf16[1024,1024]{0,1:T(8,128)(2,1)}, u32[]{:S(2)}, u32[]{:S(2)}) collective-permute-start(bf16[1024,1024]{0,1:T(8,128)(2,1)} %bitcast.5), channel_id=1, source_target_pairs={{0,1},{1,0},{2,3},{3,2},{4,5},{5,4},{6,7},{7,6},{8,9},{9,8},{10,11... | collective-permute-start | bytes 6291464 | tf_op jit(solution)/shard_map/ppermute | solution.py:13
  197.1 67.9 %all-to-all-start = ((f16[16,128,1024]{2,1,0:T(8,128)(2,1)}), f16[16,128,1024]{2,1,0:T(8,128)(2,1)}, u32[]{:S(2)}, u32[]{:S(2)}) async-start(f16[16,128,1024]{2,1,0:T(8,128)(2,1)} %bitcast.29), calls=%async_computation | async-start | bytes 8388608 | tf_op jit(solution)/shard_map/all_to_all | solution.py:68
  274.2 2.7 collective-permute-start.11

commit v2 on v0

v2 whole, which is shorter than its diff:
```python
import jax
import jax.numpy as jnp
from jax import lax
from jax.experimental import pallas as pl
from jax.experimental.pallas import tpu as pltpu
from jax.sharding import Mesh, PartitionSpec as P

damping = 0.5
parts = ("yh", "x", "z", "yl", "core")
sizes = (2, 4, 4, 2, 2)
ring = ("yh", "yl")
mib = 1024 * 1024
lane = 128
top_power = 14.0


def swap(value):
    return lax.ppermute(value, "core", [(0, 1), (1, 0)])


def trade(value, axis, bits):
    return lax.ppermute(value, axis, [(i, i ^ bits) for i in range(4)])


def after(value, *others):
    return lax.optimization_barrier((value, *others))[0]


vmem = pl.BlockSpec(memory_space=pltpu.VMEM)
smem = pl.BlockSpec(memory_space=pltpu.SMEM)


def split_kernel(place, block, theirs, both):
    yl = place[0]
    for slab in range(4):
        here = slice(slab * lane, (slab + 1) * lane)
        for other in range(2):
            start = pl.multiple_of((slab * 2 + (yl ^ other)) * lane, lane)
            some = block[:, pl.ds(start, lane)]
            both[other, :, here] = some
            if other:
                theirs[:, here] = some


def split(features, yl):
    rows, cols = features.shape
    return pl.pallas_call(
        split_kernel,
        in_specs=[smem, vmem],
        out_specs=[vmem] * 2,
        out_shape=[
            jax.ShapeDtypeStruct((rows, cols // 2), features.dtype),
            jax.ShapeDtypeStruct((2, rows, cols // 2), features.dtype),
        ],
        compiler_params=pltpu.CompilerParams(vmem_limit_bytes=16 * mib),
    )(jnp.stack([yl]), features)


def turn_kernel(place, *refs):
    core = place[0]
    *blocks, out = refs
    part = lane // 2
    for which, block in enumerate(blocks):
        for slab in range(4):
            here = slice(slab * lane, (slab + 1) * lane)
            turned = (block[0, :, here] if len(block.shape) == 3 else block[:, here]).T
            out[which, slab * part : (slab + 1) * part, :] = jnp.where(core == 0, turned[:part], turned[part:])


def turn(block, away, core):
    rows, cols = block.shape[-2:]
    return pl.pallas_call(
        turn_kernel,
        in_specs=[smem, vmem, vmem],
        out_specs=vmem,
        out_shape=jax.ShapeDtypeStruct((2, cols // 2, rows), block.dtype),
        compiler_params=pltpu.CompilerParams(vmem_limit_bytes=16 * mib),
    )(jnp.stack([core]), block, away)


def weights(cols):
    return 1.0 + lax.broadcasted_iota(jnp.int32, (1, cols), 1).astype(jnp.float32) / cols


def product(ns, x, lefts, rights, result=None):
    flat = [part for n in ns for part in lefts[n]]
    arrays, picks = zip(*rights)
    rows, depth, cols, block = flat[0].shape[1], flat[0].shape[2], arrays[0].shape[-1], 256
    part, one = rows // 4, result is not None

    def kernel(where, *refs):
        out = refs[-1]
        col = pl.program_id(0) * block + lax.broadcasted_iota(jnp.int32, (1, block), 1)
        weight = 1.0 + col.astype(jnp.float32) / cols
        for i, n in enumerate(ns):
            at = 0 if one else where[0] ^ n
            kept, got = refs[2 * i], refs[2 * i + 1]
            terms = (kept[0], kept[1], got[0], got[1])
            for c in range(2):
                total = None
                for t, left in enumerate(terms):
                    right = refs[len(flat) + 4 * c + t]
                    right = right[0] if len(right.shape) == 3 else right[...]
                    term = jnp.dot(left, right, preferred_element_type=jnp.float32)
                    total = term if total is None else total + term
                most = jnp.max(jnp.max(jnp.abs(total), axis=0, keepdims=True), axis=1, keepdims=True)
                power = jnp.ceil(jnp.log2(jnp.maximum(most, jnp.float32(1e-30)))) - top_power
                total = total * (jnp.exp2(-power) * weight)
                power = jnp.broadcast_to(power, (4, block))
                for slab in range(4):
                    out[at, slab, c * part : (c + 1) * part, :] = total[slab * part : (slab + 1) * part]
                    out[at, slab, 2 * part + 4 * c : 2 * part + 4 * c + 4, :] = power

    specs = [pl.BlockSpec(v.shape, lambda i, where: (0, 0, 0)) for v in flat]
    for pick in picks:
        if pick is None:
            specs.append(pl.BlockSpec((depth, block), lambda i, where: (0, i)))
        else:
            specs.append(pl.BlockSpec((1, depth, block), lambda i, where, pick=pick: (pick, 0, i)))
    height = 2 * part + 8
    if one:
        specs.append(pl.BlockSpec(memory_space=pl.ANY))
        out_spec = pl.BlockSpec((1, 4, height, block), lambda i, where: (where[0] ^ ns[0], 0, 0, i))
    else:
        out_spec = pl.BlockSpec((4, 4, height, block), lambda i, where: (0, 0, 0, i))
    return pl.pallas_call(
        kernel,
        grid_spec=pltpu.PrefetchScalarGridSpec(
            num_scalar_prefetch=1, grid=(cols // block,), in_specs=specs, out_specs=out_spec
        ),
        out_shape=jax.ShapeDtypeStruct((4, 4, height, cols), jnp.float32),
        input_output_aliases={len(specs): 0} if one else {},
        compiler_params=pltpu.CompilerParams(vmem_limit_bytes=32 * mib),
        cost_estimate=pl.CostEstimate(
            flops=2 * rows * cols * depth * len(arrays) * len(ns), bytes_accessed=8 * mib, transcendentals=0
        ),
    )(jnp.stack([x]), *flat, *arrays, *([result] if one else []))


def place_kernel(where, sums, *refs):
    out = refs[-1]
    first_row, yl = where[1], where[2]
    rows, width = sums.shape[2], 2 * sums.shape[3]
    for i in range(4):
        row_ids = first_row + lax.broadcasted_iota(jnp.int32, (rows, width), 0)
        col_ids = (where[0] * 4 + i) * width + lax.broadcasted_iota(jnp.int32, (rows, width), 1)
        damp = jnp.where(row_ids == col_ids, jnp.float32(damping), jnp.float32(0.0))
        for slab in range(4):
            here = slice(slab * lane, (slab + 1) * lane)
            mine, theirs = sums[i, 0, :, here], sums[i, 1, :, here]
            for other in range(2):
                at = (2 * slab + other) * lane
                there = slice(i * width + at, i * width + at + lane)
                out[:, there] = jnp.where(yl == other, mine, theirs) + damp[:, at : at + lane]


def place(sums, where, result):
    rows, width = sums.shape[2], 8 * sums.shape[3]
    given = [] if result is None else [result]
    return pl.pallas_call(
        place_kernel,
        grid_spec=pltpu.PrefetchScalarGridSpec(
            num_scalar_prefetch=1,
            grid=(1,),
            in_specs=[pl.BlockSpec(sums.shape, lambda i, where: (0, 0, 0, 0))]
            + [pl.BlockSpec(memory_space=pl.ANY)] * len(given),
            out_specs=pl.BlockSpec((rows, width), lambda i, where: (0, where[0])),
        ),
        out_shape=jax.ShapeDtypeStruct((rows, 2 * width), jnp.float32),
        input_output_aliases={2: 0} if given else {},
        compiler_params=pltpu.CompilerParams(vmem_limit_bytes=16 * mib),
    )(where, sums, *given)


def per_device(features):
    yh, x, z, yl, core = (lax.axis_index(name) for name in parts)
    rows, cols = features.shape
    half, part = cols // 2, cols // 16

    theirs, both = split(features, yl)
    near_mine = trade(theirs, ring, 1)
    both_away = swap(both)
    kept = turn(both[:1], both_away[:1], core)
    kept_near, kept_far = trade(kept, "x", 1), trade(kept, "x", 3)
    near_mine_away = swap(after(near_mine, kept_near, kept_far))
    near_theirs = trade(after(both[0], near_mine), ring, 1)
    far = trade(both, ring, 3)
    got = turn(near_mine[None], near_mine_away[None], core)
    got_near, got_far = trade(got, "x", 1), trade(got, "x", 3)
    kept_opposite = trade(after(kept_far, got_near), "x", 1)
    got_opposite = trade(got_near, "x", 3)
    lefts = [(kept, got), (kept_near, got_near), (kept_opposite, got_opposite), (kept_far, got_far)]
    near_theirs_away = swap(after(near_theirs, got_near, got_far))

    first = [(both, 0), (both_away, 0), (near_mine, None), (near_mine_away, None)]
    first += [(both, 1), (both_away, 1), (near_theirs, None), (near_theirs_away, None)]
    tile = product([0, 1, 3], x, lefts, first)
    tile = product([2], x, lefts, first, tile)

    opposite_mine = trade(after(far[0], got_near, got_far), ring, 1)
    opposite_theirs = trade(after(near_mine, got_near, got_far), ring, 3)
    far_away = swap(after(far, got_near, got_far))
    second = [(opposite_mine, None), (swap(opposite_mine), None), (far, 1), (far_away, 1)]
    second += [(opposite_theirs, None), (swap(opposite_theirs), None), (far, 0), (far_away, 0)]

    first_row = ((((yh * 4 + x) * 4 + z) * 2 + yl) * 2 + core) * part
    result = None
    for side in range(2):
        if side:
            tile = product([0, 1, 2, 3], x, lefts, second)
        packed = tile.astype(jnp.float16).reshape(16, 2 * part + 8, half)
        came = lax.all_to_all(packed, ("x", "z"), 0, 0, tiled=True)
        if side:
            came = after(came, result)
        came = came.reshape(4, 4, 2 * part + 8, half)
        power = came[:, :, 2 * part :: 4].astype(jnp.float32)
        grow = jnp.exp2(power) / weights(half)
        sums = came[:, :, : 2 * part].astype(jnp.float32).reshape(4, 4, 2, part, half) * grow[:, :, :, None]
        sums = sums.sum(1)
        result = place(sums, jnp.stack([yh ^ side, first_row, yl]), result)
    return result


def solution(mesh):
    fine = Mesh(mesh.devices.reshape(sizes), parts)
    return jax.shard_map(
        per_device,
        mesh=fine,
        in_specs=(P(("z", "yl", "core"), ("yh", "x")),),
        out_specs=P(parts, None),
        check_vma=False,
    )
```

time: 572 us -> 143 us (0.25)
  waiting for transfers between devices: 525 us -> 72.8 us
  matrix products: 27.7 us -> 0 us
  starting transfers between devices: 1.59 us -> 28.9 us
  Pallas kernels: 0 us -> 20.5 us
  between operations: 13.4 us -> 0.21 us
  local copies, waits for them, and re-layouts: 0.24 us -> 12.6 us
    reduce_scatter x1 -> x0, waiting for transfers between devices: 350 us -> none  [per_device(): reduced = lax.psum_scatter(stacked, 'ex', scatter_dimension=0, tiled=True)]
    ppermute x7 -> x17, waiting for transfers between devices: 176 us -> 44.4 us  [the longest x11 41.3 us: trade(): return lax.ppermute(value, axis, [(i, i ^ bits) for i in range(4)])]
    all_to_all x0 -> x2, waiting for transfers between devices: none -> 28.4 us  [per_device(): came = lax.all_to_all(packed, ('x', 'z'), 0, 0, tiled=True)]
    dot_general x8 -> x0, matrix products: 27.7 us -> none  [local_tile(): lax.dot_general(left, right, (((0,), (0,)), ((), ())), preferred_element_...]
    pallas_call x0 -> x8, Pallas kernels: none -> 20.5 us  [the longest x3 16.3 us: product(): pl.pallas_call(kernel, grid_spec=pltpu.PrefetchScalarGridSpec(num_scalar_...]
    ppermute x7 -> x17, starting transfers between devices: 1.59 us -> 16.3 us  [the longest x11 16.2 us: trade(): return lax.ppermute(value, axis, [(i, i ^ bits) for i in range(4)])]
    all_to_all x0 -> x2, starting transfers between devices: none -> 12.6 us  [per_device(): came = lax.all_to_all(packed, ('x', 'z'), 0, 0, tiled=True)]
    unnamed x2 -> x26, local copies, waits for them, and re-layouts: 0.01 us -> 9.67 us
  transfers between devices with their start and end apart: 8 -> 19, of which waited for: 8 -> 15; matrix products, arithmetic and copies ran while one was open for 1% -> 6% of each run, Pallas kernels for 0% -> 13%
where the time goes in v2:
time: 143 us; the launch traced here: 142 us
  waiting for transfers between devices  72.8 us (51%)
  starting transfers between devices  28.9 us (20%)
  Pallas kernels  20.5 us (14%)
  local copies, waits for them, and re-layouts  12.6 us (9%)
  other arithmetic  6.76 us (5%)
    ppermute x11, waiting for transfers between devices, trade(): return lax.ppermute(value, axis, [(i, i ^ bits) for i in range(4)])  41.3 us
    all_to_all x2, waiting for transfers between devices, per_device(): came = lax.all_to_all(packed, ('x', 'z'), 0, 0, tiled=True)  28.4 us
    pallas_call x3, Pallas kernels, product(): pl.pallas_call(kernel, grid_spec=pltpu.PrefetchScalarGridSpec(num_scalar_...  16.3 us
    ppermute x11, starting transfers between devices, trade(): return lax.ppermute(value, axis, [(i, i ^ bits) for i in range(4)])  16.2 us
    all_to_all x2, starting transfers between devices, per_device(): came = lax.all_to_all(packed, ('x', 'z'), 0, 0, tiled=True)  12.6 us
    unnamed x26, local copies, waits for them, and re-layouts  9.67 us
    convert_element_type x2, other arithmetic, per_device(): packed = tile.astype(jnp.float16).reshape(16, 2 * part + 8, half)  3.83 us
    pallas_call x2, Pallas kernels, place(): pl.pallas_call(place_kernel, grid_spec=pltpu.PrefetchScalarGridSpec(num_s...  3.33 us
  transfers between devices with their start and end apart: 19, of which 15 were waited for; matrix products, arithmetic and copies ran while one was open for 6% of the time, Pallas kernels for 13%

profile of v2, /device:TPU:0, one launch (start us, length us, event | category | flops | bytes accessed | tf_op | source)
XLA Modules:
  0.0 141.8 jit_solution(14099648937324472255)
XLA Ops:
  0.0 1.2 copy-done.6
  1.6 1.7 %collective-permute-start.1 = (bf16[512,512]{1,0:T(8,128)(2,1)S(1)}, bf16[512,512]{1,0:T(8,128)(2,1)S(1)}, u32[]{:S(2)}, u32[]{:S(2)}) collective-permute-start(bf16[512,512]{1,0:T(8,128)(2,1)S(1)} %get-tuple-element.16), channel_id=1, source_target_pairs={{0,2},{2,0},{64,66},{66,64},{1,3},{3,1},{65,67},{67,65},{4,6},{6,4... | collective-permute-start | bytes 1572872 | tf_op jit(solution)/shard_map/ppermute | solution.py:22
  3.4 0.8 collective-permute-done.refs_7_.refs_11_.refs_3_
  4.3 0.3 shard_map.18.refs_0_
  4.6 1.7 %collective-permute-start.2 = (bf16[2,256,512]{2,1,0:T(8,128)(2,1)S(1)}, bf16[2,256,512]{2,1,0:T(8,128)(2,1)S(1)}, u32[]{:S(2)}, u32[]{:S(2)}) collective-permute-start(bf16[2,256,512]{2,1,0:T(8,128)(2,1)S(1)} %shard_map.18.refs_0_), channel_id=1, source_target_pairs={{0,16},{16,0},{32,48},{48,32},{1,17},{17,1},{33,49},{49,33},{2,18}... | collective-permute-start | bytes 1572872 | tf_op jit(solution)/shard_map/ppermute | solution.py:22
  6.3 2.1 %collective-permute-start.3 = (bf16[2,256,512]{2,1,0:T(8,128)(2,1)S(1)}, bf16[2,256,512]{2,1,0:T(8,128)(2,1)}, u32[]{:S(2)}, u32[]{:S(2)}) collective-permute-start(bf16[2,256,512]{2,1,0:T(8,128)(2,1)S(1)} %shard_map.18.refs_0_), channel_id=1, source_target_pairs={{0,48},{16,32},{32,16},{48,0},{1,49},{17,33},{33,17},{49,1},{2,50}... | collective-permute-start | bytes 1572872 | tf_op jit(solution)/shard_map/ppermute | solution.py:22
  8.4 0.8 copy-done
  9.2 6.8 %collective-permute-done.1.refs_8_.refs_4_ = bf16[512,512]{1,0:T(8,128)(2,1)S(1)} collective-permute-done((bf16[512,512]{1,0:T(8,128)(2,1)S(1)}, bf16[512,512]{1,0:T(8,128)(2,1)S(1)}, u32[]{:S(2)}, u32[]{:S(2)}) %collective-permute-start.1) | collective-permute-done | bytes 524320 | tf_op jit(solution)/shard_map/ppermute | solution.py:22
  15.9 2.7 %collective-permute-done.2.refs_2_ = bf16[2,256,512]{2,1,0:T(8,128)(2,1)S(1)} collective-permute-done((bf16[2,256,512]{2,1,0:T(8,128)(2,1)S(1)}, bf16[2,256,512]{2,1,0:T(8,128)(2,1)S(1)}, u32[]{:S(2)}, u32[]{:S(2)}) %collective-permute-start.2) | collective-permute-done | bytes 524320 | tf_op jit(solution)/shard_map/ppermute | solution.py:22
  18.7 0.8 copy-done.7
  19.5 1.8 %collective-permute-done.3.refs_6_.refs_4_ = bf16[2,256,512]{2,1,0:T(8,128)(2,1)} collective-permute-done((bf16[2,256,512]{2,1,0:T(8,128)(2,1)S(1)}, bf16[2,256,512]{2,1,0:T(8,128)(2,1)}, u32[]{:S(2)}, u32[]{:S(2)}) %collective-permute-start.3) | collective-permute-done | bytes 524320 | tf_op jit(solution)/shard_map/ppermute | solution.py:22
  21.3 1.6 %collective-permute-start.15 = (bf16[512,512]{1,0:T(8,128)(2,1)S(1)}, bf16[512,512]{1,0:T(8,128)(2,1)}, u32[]{:S(2)}, u32[]{:S(2)}) collective-permute-start(bf16[512,512]{1,0:T(8,128)(2,1)S(1)} %get-tuple-element.22), channel_id=1, source_target_pairs={{0,2},{2,0},{64,66},{66,64},{1,3},{3,1},{65,67},{67,65},{4,6},{6,4... | collective-permute-start | bytes 1572872 | tf_op jit(solution)/shard_map/ppermute | solution.py:22
  22.9 0.3 collective-permute-done.4.refs_9_.refs_5_
  23.6 2.2 %collective-permute-start.8 = (bf16[2,256,512]{2,1,0:T(8,128)(2,1)S(1)}, bf16[2,256,512]{2,1,0:T(8,128)(2,1)S(1)}, u32[]{:S(2)}, u32[]{:S(2)}) collective-permute-start(bf16[2,256,512]{2,1,0:T(8,128)(2,1)S(1)} %shard_map.19.refs_1_), channel_id=1, source_target_pairs={{0,48},{16,32},{32,16},{48,0},{1,49},{17,33},{33,17},{49,1},{2,50}... | collective-permute-start | bytes 1572872 | tf_op jit(solution)/shard_map/ppermute | solution.py:22
  25.8 0.8 copy-done.3
  26.6 9.1 %collective-permute-done.15.refs_12_.refs_8_ = bf16[512,512]{1,0:T(8,128)(2,1)} collective-permute-done((bf16[512,512]{1,0:T(8,128)(2,1)S(1)}, bf16[512,512]{1,0:T(8,128)(2,1)}, u32[]{:S(2)}, u32[]{:S(2)}) %collective-permute-start.15) | collective-permute-done | bytes 524320 | tf_op jit(solution)/shard_map/ppermute | solution.py:22
  35.7 1.9 %collective-permute-done.5.refs_3_ = bf16[2,256,512]{2,1,0:T(8,128)(2,1)} collective-permute-done((bf16[2,256,512]{2,1,0:T(8,128)(2,1)S(1)}, bf16[2,256,512]{2,1,0:T(8,128)(2,1)}, u32[]{:S(2)}, u32[]{:S(2)}) %collective-permute-start.5) | collective-permute-done | bytes 524320 | tf_op jit(solution)/shard_map/ppermute | solution.py:22
  37.7 1.2 collective-permute-done.8.refs_7_.refs_5_
  38.9 0.8 copy-done.10
  39.7 3.0 %collective-permute-start.9 = (bf16[2,512,512]{2,1,0:T(8,128)(2,1)S(1)}, bf16[2,512,512]{2,1,0:T(8,128)(2,1)}, u32[]{:S(2)}, u32[]{:S(2)}) collective-permute-start(bf16[2,512,512]{2,1,0:T(8,128)(2,1)S(1)} %get-tuple-element.15.refs_6_.refs_10_.refs_2_), channel_id=1, source_target_pairs={{0,66},{2,64},{64,2},{66,0},{1,67},{3,65},{65,3},{67,1},{4,70},{6,... | collective-permute-start | bytes 3145736 | tf_op jit(solution)/shard_map/ppermute | solution.py:22
  42.7 0.4 collective-permute-start.6
  43.1 2.1 %collective-permute-start.7 = (bf16[2,256,512]{2,1,0:T(8,128)(2,1)}, bf16[2,256,512]{2,1,0:T(8,128)(2,1)}, u32[]{:S(2)}, u32[]{:S(2)}) collective-permute-start(bf16[2,256,512]{2,1,0:T(8,128)(2,1)} %collective-permute-done.5.refs_3_), channel_id=1, source_target_pairs={{0,48},{16,32},{32,16},{48,0},{1,49},{17,33},{33,17},{49,1},{2,50}... | collective-permute-start | bytes 1572872 | tf_op jit(solution)/shard_map/ppermute | solution.py:22
  45.2 1.0 copy-done.1
  46.3 1.0 copy-done.4
  47.3 1.0 copy-done.8
  48.4 1.0 copy-done.11
  49.4 5.8 %shard_map.21.refs_10_ = f32[4,4,136,512]{3,2,1,0:T(8,128)S(1)} custom-call(s32[1]{0:T(128)} %bitcast.3.where, bf16[2,256,512]{2,1,0:T(8,128)(2,1)S(1)} %copy-done.1, bf16[2,256,512]{2,1,0:T(8,128)(2,1)S(1)} %copy-done.4, bf16[2,256,512]{2,1,0:T(8,128)(2,1)S(1)} %copy-done.8, bf16[2,256,512]{2,1,0:T(8,128)(2,1)} %collective-permute-done.5.refs_3_, ...), custom_call_target="tpu_custom_call" | custom-call | flops 3221225472 | bytes 8388608 | tf_op jit(solution)/shard_map/pallas_call | solution.py:126
  55.2 1.9 %collective-permute-done.6.refs_4_.refs_0_ = bf16[2,256,512]{2,1,0:T(8,128)(2,1)} collective-permute-done((bf16[2,256,512]{2,1,0:T(8,128)(2,1)}, bf16[2,256,512]{2,1,0:T(8,128)(2,1)}, u32[]{:S(2)}, u32[]{:S(2)}) %collective-permute-start.6) | collective-permute-done | bytes 524320 | tf_op jit(solution)/shard_map/ppermute | solution.py:22
  57.1 1.4 collective-permute-done.7.refs_5_.refs_1_
  58.4 3.3 %shard_map.22 = f32[4,4,136,512]{3,2,1,0:T(8,128)S(1)} custom-call(s32[1]{0:T(128)} %bitcast.3.where, bf16[2,256,512]{2,1,0:T(8,128)(2,1)} %collective-permute-done.6.refs_4_.refs_0_, bf16[2,256,512]{2,1,0:T(8,128)(2,1)} %collective-permute-done.7.refs_5_.refs_1_, ...), custom_call_target="tpu_custom_call", output_to_operand_aliasing={{}: (11, {})} | custom-call | flops 1073741824 | bytes 8388608 | tf_op jit(solution)/shard_map/pallas_call | solution.py:126
  61.8 1.9 %convert_element_type.31 = f16[4,4,136,512]{3,2,1,0:T(8,128)(2,1)} convert(f32[4,4,136,512]{3,2,1,0:T(8,128)S(1)} %shard_map.22) | non-fusion elementwise | flops 1114112 | bytes 6684672 | tf_op jit(solution)/shard_map/convert_element_type | solution.py:211
  63.7 7.1 %all-to-all-start.1 = ((f16[16,136,512]{2,1,0:T(8,128)(2,1)}), f16[16,136,512]{2,1,0:T(8,128)(2,1)}, u32[]{:S(2)}, u32[]{:S(2)}) async-start(f16[16,136,512]{2,1,0:T(8,128)(2,1)} %bitcast.30), calls=%async_computation.1 | async-start | bytes 4456448 | tf_op jit(solution)/shard_map/all_to_all | solution.py:212
  70.8 1.1 slice_bitcast_fusion
  72.1 1.1 collective-permute-start.13
  73.2 11.4 %collective-permute-done.10.refs_8_ = bf16[512,512]{1,0:T(8,128)(2,1)S(1)} collective-permute-done((bf16[512,512]{1,0:T(8,128)(2,1)S(1)}, bf16[512,512]{1,0:T(8,128)(2,1)S(1)}, u32[]{:S(2)}, u32[]{:S(2)}) %collective-permute-start.10) | collective-permute-done | bytes 524320 | tf_op jit(solution)/shard_map/ppermute | solution.py:22
  84.6 3.0 %collective-permute-done.13.refs_12_ = bf16[512,512]{1,0:T(8,128)(2,1)S(1)} collective-permute-done((bf16[512,512]{1,0:T(8,128)(2,1)S(1)}, bf16[512,512]{1,0:T(8,128)(2,1)S(1)}, u32[]{:S(2)}, u32[]{:S(2)}) %collective-permute-start.13) | collective-permute-done | bytes 524320 | tf_op jit(solution)/shard_map/ppermute | solution.py:22
  87.7 1.9 %collective-permute-done.14.refs_13_ = bf16[512,512]{1,0:T(8,128)(2,1)S(1)} collective-permute-done((bf16[512,512]{1,0:T(8,128)(2,1)S(1)}, bf16[512,512]{1,0:T(8,128)(2,1)S(1)}, u32[]{:S(2)}, u32[]{:S(2)}) %collective-permute-start.14) | collective-permute-done | bytes 524320 | tf_op jit(solution)/shard_map/ppermute | solution.py:18
  89.6 1.0 copy-done.12
  90.6 7.2 %shard_map.20 = f32[4,4,136,512]{3,2,1,0:T(8,128)S(1)} custom-call(s32[1]{0:T(128)} %bitcast.3.where, bf16[2,256,512]{2,1,0:T(8,128)(2,1)S(1)} %copy-done.2, bf16[2,256,512]{2,1,0:T(8,128)(2,1)S(1)} %copy-done.5, bf16[2,256,512]{2,1,0:T(8,128)(2,1)S(1)} %copy-done.9, bf16[2,256,512]{2,1,0:T(8,128)(2,1)} %collective-permute-done.5.refs_3_, ...), custom_call_target="tpu_custom_call" | custom-call | flops 4294967296 | bytes 8388608 | tf_op jit(solution)/shard_map/pallas_call | solution.py:126
  97.8 1.9 %convert_element_type.30 = f16[4,4,136,512]{3,2,1,0:T(8,128)(2,1)} convert(f32[4,4,136,512]{3,2,1,0:T(8,128)S(1)} %shard_map.20) | non-fusion elementwise | flops 1114112 | bytes 6684672 | tf_op jit(solution)/shard_map/convert_element_type | solution.py:211
  99.8 1.7 %all-to-all-done.1 = f16[16,136,512]{2,1,0:T(8,128)(2,1)} async-done(((f16[16,136,512]{2,1,0:T(8,128)(2,1)}), f16[16,136,512]{2,1,0:T(8,128)(2,1)}, u32[]{:S(2)}, u32[]{:S(2)}) %all-to-all-start.1) | async-done | bytes 2228256 | tf_op jit(solution)/shard_map/all_to_all | solution.py:212
  101.4 5.5 %all-to-all-start = ((f16[16,136,512]{2,1,0:T(8,128)(2,1)}), f16[16,136,512]{2,1,0:T(8,128)(2,1)S(1)}, u32[]{:S(2)}, u32[]{:S(2)}) async-start(f16[16,136,512]{2,1,0:T(8,128)(2,1)} %bitcast.8), calls=%async_computation | async-start | bytes 4456448 | tf_op jit(solution)/shard_map/all_to_all | solution.py:212
  107.1 1.6 %slice.26 = f16[4,4,2,512]{3,2,1,0:T(2,128)(2,1)S(1)} slice(f16[4,4,136,512]{3,2,1,0:T(8,128)(2,1)} %bitcast.12), slice={[0:4:1], [0:4:1], [128:136:4], [0:512:1]} | slice | bytes 65536 | tf_op jit(solution)/shard_map/slice | solution.py:216
  108.8 2.2 %fusion.1 = f32[4,128,512]{2,1,0:T(8,128)S(1)} fusion(f16[4,4,136,512]{3,2,1,0:T(8,128)(2,1)} %bitcast.12, f32[4,4,2,512]{3,2,1,0:T(2,128)S(1)} %exponential_divide_fusion.1), kind=kLoop, calls=%fused_computation.3 | loop fusion | flops 2883584 | bytes 3211264 | tf_op jit(solution)/shard_map/reduce_sum | solution.py:219
  111.1 1.7 %shard_map.23.refs_0_ = f32[64,8192]{1,0:T(8,128)} custom-call(s32[3]{0:T(128)S(1)} %add_add_fusion.1.where, f32[4,2,64,512]{3,2,1,0:T(8,128)S(1)} %bitcast.28), custom_call_target="tpu_custom_call" | custom-call | tf_op jit(solution)/shard_map/pallas_call | solution.py:160
  112.7 26.8 %all-to-all-done = f16[16,136,512]{2,1,0:T(8,128)(2,1)S(1)} async-done(((f16[16,136,512]{2,1,0:T(8,128)(2,1)}), f16[16,136,512]{2,1,0:T(8,128)(2,1)S(1)}, u32[]{:S(2)}, u32[]{:S(2)}) %all-to-all-start) | async-done | bytes 2228256 | tf_op jit(solution)/shard_map/all_to_all | solution.py:212
  139.7 0.4 fusion
  140.2 1.7 %shard_map.24 = f32[64,8192]{1,0:T(8,128)} custom-call(s32[3]{0:T(128)S(1)} %add_add_fusion.where, f32[4,2,64,512]{3,2,1,0:T(8,128)S(1)} %bitcast.29, f32[64,8192]{1,0:T(8,128)} %shard_map.23.refs_0_), custom_call_target="tpu_custom_call", output_to_operand_aliasing={{}: (2, {})} | custom-call | tf_op jit(solution)/shard_map/pallas_call | solution.py:160
  (38 shorter events, 1.6 us)
Async XLA Ops:
  0.0 1.2 copy-start.6
  1.5 2.7 %collective-permute-start = (bf16[2,512,512]{2,1,0:T(8,128)(2,1)S(1)}, bf16[2,512,512]{2,1,0:T(8,128)(2,1)S(1)}, u32[]{:S(2)}, u32[]{:S(2)}) collective-permute-start(bf16[2,512,512]{2,1,0:T(8,128)(2,1)S(1)} %get-tuple-element.15.refs_6_.refs_10_.refs_2_), channel_id=1, source_target_pairs={{0,1},{1,0},{2,3},{3,2},{4,5},{5,4},{6,7},{7,6},{8,9},{9,8},{10,11... | collective-permute-start | bytes 3145736 | tf_op jit(solution)/shard_map/ppermute | solution.py:18
  1.6 14.3 %collective-permute-start.1 = (bf16[512,512]{1,0:T(8,128)(2,1)S(1)}, bf16[512,512]{1,0:T(8,128)(2,1)S(1)}, u32[]{:S(2)}, u32[]{:S(2)}) collective-permute-start(bf16[512,512]{1,0:T(8,128)(2,1)S(1)} %get-tuple-element.16), channel_id=1, source_target_pairs={{0,2},{2,0},{64,66},{66,64},{1,3},{3,1},{65,67},{67,65},{4,6},{6,4... | collective-permute-start | bytes 1572872 | tf_op jit(solution)/shard_map/ppermute | solution.py:22
  4.6 14.0 %collective-permute-start.2 = (bf16[2,256,512]{2,1,0:T(8,128)(2,1)S(1)}, bf16[2,256,512]{2,1,0:T(8,128)(2,1)S(1)}, u32[]{:S(2)}, u32[]{:S(2)}) collective-permute-start(bf16[2,256,512]{2,1,0:T(8,128)(2,1)S(1)} %shard_map.18.refs_0_), channel_id=1, source_target_pairs={{0,16},{16,0},{32,48},{48,32},{1,17},{17,1},{33,49},{49,33},{2,18}... | collective-permute-start | bytes 1572872 | tf_op jit(solution)/shard_map/ppermute | solution.py:22
  6.3 15.0 %collective-permute-start.3 = (bf16[2,256,512]{2,1,0:T(8,128)(2,1)S(1)}, bf16[2,256,512]{2,1,0:T(8,128)(2,1)}, u32[]{:S(2)}, u32[]{:S(2)}) collective-permute-start(bf16[2,256,512]{2,1,0:T(8,128)(2,1)S(1)} %shard_map.18.refs_0_), channel_id=1, source_target_pairs={{0,48},{16,32},{32,16},{48,0},{1,49},{17,33},{33,17},{49,1},{2,50}... | collective-permute-start | bytes 1572872 | tf_op jit(solution)/shard_map/ppermute | solution.py:22
  8.4 0.8 copy-start
  18.7 0.8 copy-start.7
  21.3 1.9 %collective-permute-start.4 = (bf16[512,512]{1,0:T(8,128)(2,1)S(1)}, bf16[512,512]{1,0:T(8,128)(2,1)S(1)}, u32[]{:S(2)}, u32[]{:S(2)}) collective-permute-start(bf16[512,512]{1,0:T(8,128)(2,1)S(1)} %collective-permute-done.1.refs_8_.refs_4_), channel_id=1, source_target_pairs={{0,1},{1,0},{2,3},{3,2},{4,5},{5,4},{6,7},{7,6},{8,9},{9,8},{10,11... | collective-permute-start | bytes 1572872 | tf_op jit(solution)/shard_map/ppermute | solution.py:18
  21.3 14.4 %collective-permute-start.15 = (bf16[512,512]{1,0:T(8,128)(2,1)S(1)}, bf16[512,512]{1,0:T(8,128)(2,1)}, u32[]{:S(2)}, u32[]{:S(2)}) collective-permute-start(bf16[512,512]{1,0:T(8,128)(2,1)S(1)} %get-tuple-element.22), channel_id=1, source_target_pairs={{0,2},{2,0},{64,66},{66,64},{1,3},{3,1},{65,67},{67,65},{4,6},{6,4... | collective-permute-start | bytes 1572872 | tf_op jit(solution)/shard_map/ppermute | solution.py:22
  23.5 14.2 %collective-permute-start.5 = (bf16[2,256,512]{2,1,0:T(8,128)(2,1)S(1)}, bf16[2,256,512]{2,1,0:T(8,128)(2,1)}, u32[]{:S(2)}, u32[]{:S(2)}) collective-permute-start(bf16[2,256,512]{2,1,0:T(8,128)(2,1)S(1)} %shard_map.19.refs_1_), channel_id=1, source_target_pairs={{0,16},{16,0},{32,48},{48,32},{1,17},{17,1},{33,49},{49,33},{2,18}... | collective-permute-start | bytes 1572872 | tf_op jit(solution)/shard_map/ppermute | solution.py:22
  23.6 15.3 %collective-permute-start.8 = (bf16[2,256,512]{2,1,0:T(8,128)(2,1)S(1)}, bf16[2,256,512]{2,1,0:T(8,128)(2,1)S(1)}, u32[]{:S(2)}, u32[]{:S(2)}) collective-permute-start(bf16[2,256,512]{2,1,0:T(8,128)(2,1)S(1)} %shard_map.19.refs_1_), channel_id=1, source_target_pairs={{0,48},{16,32},{32,16},{48,0},{1,49},{17,33},{33,17},{49,1},{2,50}... | collective-permute-start | bytes 1572872 | tf_op jit(solution)/shard_map/ppermute | solution.py:22
  25.8 0.8 copy-start.3
  38.9 0.8 copy-start.10
  39.7 5.6 %collective-permute-start.16 = (bf16[512,512]{1,0:T(8,128)(2,1)}, bf16[512,512]{1,0:T(8,128)(2,1)}, u32[]{:S(2)}, u32[]{:S(2)}) collective-permute-start(bf16[512,512]{1,0:T(8,128)(2,1)} %collective-permute-done.15.refs_12_.refs_8_), channel_id=1, source_target_pairs={{0,1},{1,0},{2,3},{3,2},{4,5},{5,4},{6,7},{7,6},{8,9},{9,8},{10,11... | collective-permute-start | bytes 1572872 | tf_op jit(solution)/shard_map/ppermute | solution.py:18
  39.7 31.1 %collective-permute-start.9 = (bf16[2,512,512]{2,1,0:T(8,128)(2,1)S(1)}, bf16[2,512,512]{2,1,0:T(8,128)(2,1)}, u32[]{:S(2)}, u32[]{:S(2)}) collective-permute-start(bf16[2,512,512]{2,1,0:T(8,128)(2,1)S(1)} %get-tuple-element.15.refs_6_.refs_10_.refs_2_), channel_id=1, source_target_pairs={{0,66},{2,64},{64,2},{66,0},{1,67},{3,65},{65,3},{67,1},{4,70},{6,... | collective-permute-start | bytes 3145736 | tf_op jit(solution)/shard_map/ppermute | solution.py:22
  42.7 14.4 %collective-permute-start.6 = (bf16[2,256,512]{2,1,0:T(8,128)(2,1)}, bf16[2,256,512]{2,1,0:T(8,128)(2,1)}, u32[]{:S(2)}, u32[]{:S(2)}) collective-permute-start(bf16[2,256,512]{2,1,0:T(8,128)(2,1)} %collective-permute-done.3.refs_6_.refs_4_), channel_id=1, source_target_pairs={{0,16},{16,0},{32,48},{48,32},{1,17},{17,1},{33,49},{49,33},{2,18}... | collective-permute-start | bytes 1572872 | tf_op jit(solution)/shard_map/ppermute | solution.py:22
  43.1 15.3 %collective-permute-start.7 = (bf16[2,256,512]{2,1,0:T(8,128)(2,1)}, bf16[2,256,512]{2,1,0:T(8,128)(2,1)}, u32[]{:S(2)}, u32[]{:S(2)}) collective-permute-start(bf16[2,256,512]{2,1,0:T(8,128)(2,1)} %collective-permute-done.5.refs_3_), channel_id=1, source_target_pairs={{0,48},{16,32},{32,16},{48,0},{1,49},{17,33},{33,17},{49,1},{2,50}... | collective-permute-start | bytes 1572872 | tf_op jit(solution)/shard_map/ppermute | solution.py:22
  45.2 1.0 copy-start.1
  46.3 1.0 copy-start.4
  47.3 1.0 copy-start.8
  48.4 1.0 copy-start.11
  63.7 25.9 %copy-start.2 = (bf16[2,256,512]{2,1,0:T(8,128)(2,1)S(1)}, bf16[2,256,512]{2,1,0:T(8,128)(2,1)}, u32[]{:S(2)}) copy-start(bf16[2,256,512]{2,1,0:T(8,128)(2,1)} %copy-done) | copy-start | bytes 1572868
  63.7 25.9 %copy-start.5 = (bf16[2,256,512]{2,1,0:T(8,128)(2,1)S(1)}, bf16[2,256,512]{2,1,0:T(8,128)(2,1)}, u32[]{:S(2)}) copy-start(bf16[2,256,512]{2,1,0:T(8,128)(2,1)} %copy-done.3) | copy-start | bytes 1572868
  63.7 25.9 %copy-start.9 = (bf16[2,256,512]{2,1,0:T(8,128)(2,1)S(1)}, bf16[2,256,512]{2,1,0:T(8,128)(2,1)}, u32[]{:S(2)}) copy-start(bf16[2,256,512]{2,1,0:T(8,128)(2,1)} %copy-done.7) | copy-start | bytes 1572868
  63.7 37.7 %all-to-all-start.1 = ((f16[16,136,512]{2,1,0:T(8,128)(2,1)}), f16[16,136,512]{2,1,0:T(8,128)(2,1)}, u32[]{:S(2)}, u32[]{:S(2)}) async-start(f16[16,136,512]{2,1,0:T(8,128)(2,1)} %bitcast.30), calls=%async_computation.1 | async-start | bytes 4456448 | tf_op jit(solution)/shard_map/all_to_all | solution.py:212
  71.9 12.7 %collective-permute-start.10 = (bf16[512,512]{1,0:T(8,128)(2,1)S(1)}, bf16[512,512]{1,0:T(8,128)(2,1)S(1)}, u32[]{:S(2)}, u32[]{:S(2)}) collective-permute-start(bf16[512,512]{1,0:T(8,128)(2,1)S(1)} %slice_bitcast_fusion), channel_id=1, source_target_pairs={{0,2},{2,0},{64,66},{66,64},{1,3},{3,1},{65,67},{67,65},{4,6},{6,4... | collective-permute-start | bytes 1572872 | tf_op jit(solution)/shard_map/ppermute | solution.py:22
  72.1 15.6 %collective-permute-start.12 = (bf16[2,512,512]{2,1,0:T(8,128)(2,1)}, bf16[2,512,512]{2,1,0:T(8,128)(2,1)S(1)}, u32[]{:S(2)}, u32[]{:S(2)}) collective-permute-start(bf16[2,512,512]{2,1,0:T(8,128)(2,1)} %collective-permute-done.9.refs_10_.refs_14_), channel_id=1, source_target_pairs={{0,1},{1,0},{2,3},{3,2},{4,5},{5,4},{6,7},{7,6},{8,9},{9,8},{10,11... | collective-permute-start | bytes 3145736 | tf_op jit(solution)/shard_map/ppermute | solution.py:18
  72.1 15.5 %collective-permute-start.13 = (bf16[512,512]{1,0:T(8,128)(2,1)S(1)}, bf16[512,512]{1,0:T(8,128)(2,1)S(1)}, u32[]{:S(2)}, u32[]{:S(2)}) collective-permute-start(bf16[512,512]{1,0:T(8,128)(2,1)S(1)} %collective-permute-done.1.refs_8_.refs_4_), channel_id=1, source_target_pairs={{0,66},{2,64},{64,2},{66,0},{1,67},{3,65},{65,3},{67,1},{4,70},{6,... | collective-permute-start | bytes 1572872 | tf_op jit(solution)/shard_map/ppermute | solution.py:22
  84.6 3.1 %collective-permute-start.11 = (bf16[512,512]{1,0:T(8,128)(2,1)S(1)}, bf16[512,512]{1,0:T(8,128)(2,1)S(1)}, u32[]{:S(2)}, u32[]{:S(2)}) collective-permute-start(bf16[512,512]{1,0:T(8,128)(2,1)S(1)} %collective-permute-done.10.refs_8_), channel_id=1, source_target_pairs={{0,1},{1,0},{2,3},{3,2},{4,5},{5,4},{6,7},{7,6},{8,9},{9,8},{10,11... | collective-permute-start | bytes 1572872 | tf_op jit(solution)/shard_map/ppermute | solution.py:18
  87.7 1.9 %collective-permute-start.14 = (bf16[512,512]{1,0:T(8,128)(2,1)S(1)}, bf16[512,512]{1,0:T(8,128)(2,1)S(1)}, u32[]{:S(2)}, u32[]{:S(2)}) collective-permute-start(bf16[512,512]{1,0:T(8,128)(2,1)S(1)} %collective-permute-done.13.refs_12_), channel_id=1, source_target_pairs={{0,1},{1,0},{2,3},{3,2},{4,5},{5,4},{6,7},{7,6},{8,9},{9,8},{10,11... | collective-permute-start | bytes 1572872 | tf_op jit(solution)/shard_map/ppermute | solution.py:18
  89.6 1.0 copy-start.12
  101.4 38.1 %all-to-all-start = ((f16[16,136,512]{2,1,0:T(8,128)(2,1)}), f16[16,136,512]{2,1,0:T(8,128)(2,1)S(1)}, u32[]{:S(2)}, u32[]{:S(2)}) async-start(f16[16,136,512]{2,1,0:T(8,128)(2,1)} %bitcast.8), calls=%async_computation | async-start | bytes 4456448 | tf_op jit(solution)/shard_map/all_to_all | solution.py:212

commit v3 on v2

v3 whole, which is shorter than its diff:
```python
import jax
import jax.numpy as jnp
from jax import lax
from jax.experimental import pallas as pl
from jax.experimental.pallas import tpu as pltpu
from jax.sharding import Mesh, PartitionSpec as P

damping = 0.5
parts = ("yh", "x", "z", "yl", "core")
sizes = (2, 4, 4, 2, 2)
ring = ("yh", "yl")
mib = 1024 * 1024
lane = 128
top_power = 14.0


def swap(value):
    return lax.ppermute(value, "core", [(0, 1), (1, 0)])


def trade(value, axis, bits):
    return lax.ppermute(value, axis, [(i, i ^ bits) for i in range(4)])


def together(*values):
    return lax.optimization_barrier(values)


def after(value, *others):
    return lax.optimization_barrier((value, *others))[0]


vmem = pl.BlockSpec(memory_space=pltpu.VMEM)
smem = pl.BlockSpec(memory_space=pltpu.SMEM)


def split_kernel(place, block, theirs, both):
    yl = place[0]
    for slab in range(4):
        here = slice(slab * lane, (slab + 1) * lane)
        for other in range(2):
            start = pl.multiple_of((slab * 2 + (yl ^ other)) * lane, lane)
            some = block[:, pl.ds(start, lane)]
            both[other, :, here] = some
            if other:
                theirs[:, here] = some


def split(features, yl):
    rows, cols = features.shape
    return pl.pallas_call(
        split_kernel,
        in_specs=[smem, vmem],
        out_specs=[vmem] * 2,
        out_shape=[
            jax.ShapeDtypeStruct((rows, cols // 2), features.dtype),
            jax.ShapeDtypeStruct((2, rows, cols // 2), features.dtype),
        ],
        compiler_params=pltpu.CompilerParams(vmem_limit_bytes=16 * mib),
    )(jnp.stack([yl]), features)


def turn_kernel(place, *refs):
    core = place[0]
    *blocks, out = refs
    part = lane // 2
    for which, block in enumerate(blocks):
        for slab in range(4):
            here = slice(slab * lane, (slab + 1) * lane)
            turned = (block[0, :, here] if len(block.shape) == 3 else block[:, here]).T
            out[which, slab * part : (slab + 1) * part, :] = jnp.where(core == 0, turned[:part], turned[part:])


def turn(block, away, core):
    rows, cols = block.shape[-2:]
    first = pl.BlockSpec((1, rows, cols), lambda i: (0, 0, 0)) if block.ndim == 3 else pl.BlockSpec((rows, cols), lambda i: (0, 0))
    return pl.pallas_call(
        turn_kernel,
        grid=(1,),
        in_specs=[smem, first, first],
        out_specs=pl.BlockSpec((2, cols // 2, rows), lambda i: (0, 0, 0)),
        out_shape=jax.ShapeDtypeStruct((2, cols // 2, rows), block.dtype),
        compiler_params=pltpu.CompilerParams(vmem_limit_bytes=16 * mib),
    )(jnp.stack([core]), block, away)


def weights(cols):
    return 1.0 + lax.broadcasted_iota(jnp.int32, (1, cols), 1).astype(jnp.float32) / cols


def product(ns, turn_by, lefts, rights, by_z=False, result=None):
    flat = [part for n in ns for part in lefts[n]]
    starts = [sum(len(lefts[m]) for m in ns[:i]) for i in range(len(ns))]
    arrays, picks = zip(*rights)
    rows, depth, cols, block = flat[0].shape[-2], flat[0].shape[-1], arrays[0].shape[-1], 256
    eights, one = rows // 4 // 8, result is not None

    def kernel(where, *refs):
        out = refs[-1]
        col = pl.program_id(0) * block + lax.broadcasted_iota(jnp.int32, (1, block), 1)
        weight = 1.0 + col.astype(jnp.float32) / cols
        for i, n in enumerate(ns):
            terms = []
            for ref in refs[starts[i] : starts[i] + len(lefts[n])]:
                terms += [ref[0], ref[1]] if len(ref.shape) == 3 else [ref[...]]
            totals, most = [], jnp.full((1, 1), 1e-30, jnp.float32)
            for c in range(2):
                total = None
                for t, left in enumerate(terms):
                    right = refs[len(flat) + 4 * c + t]
                    right = right[0] if len(right.shape) == 3 else right[...]
                    term = jnp.dot(left, right, preferred_element_type=jnp.float32)
                    total = term if total is None else total + term
                totals.append(total)
                most = jnp.maximum(most, jnp.max(jnp.max(jnp.abs(total), axis=0, keepdims=True), axis=1, keepdims=True))
            power = jnp.ceil(jnp.log2(most)) - top_power
            shrink = jnp.exp2(-power) * weight
            for slab in range(4):
                if by_z:
                    at = (slab ^ where[0], i)
                else:
                    at = (0 if one else where[0] ^ n, slab)
                for c in range(2):
                    some = totals[c][slab * 8 * eights : (slab + 1) * 8 * eights] * shrink
                    out[(*at, slice(c * eights, (c + 1) * eights))] = some.reshape(eights, 8, block)
                out[(*at, 2 * eights)] = jnp.broadcast_to(power, (8, block))

    specs = [pl.BlockSpec(v.shape, lambda i, where, dims=v.ndim: (0,) * dims) for v in flat]
    for pick in picks:
        if pick is None:
            specs.append(pl.BlockSpec((depth, block), lambda i, where: (0, i)))
        else:
            specs.append(pl.BlockSpec((1, depth, block), lambda i, where, pick=pick: (pick, 0, i)))
    height = 2 * eights + 1
    if one:
        specs.append(pl.BlockSpec(memory_space=pl.ANY))
    count = len(ns) if by_z else 4
    if one:
        out_spec = pl.BlockSpec((1, 4, height, 8, block), lambda i, where: (where[0] ^ ns[0], 0, 0, 0, i))
    else:
        out_spec = pl.BlockSpec((4, count, height, 8, block), lambda i, where: (0, 0, 0, 0, i))
    return pl.pallas_call(
        kernel,
        grid_spec=pltpu.PrefetchScalarGridSpec(
            num_scalar_prefetch=1, grid=(cols // block,), in_specs=specs, out_specs=out_spec
        ),
        out_shape=jax.ShapeDtypeStruct((4, count, height, 8, cols), jnp.float32),
        input_output_aliases={len(specs): 0} if one else {},
        compiler_params=pltpu.CompilerParams(vmem_limit_bytes=32 * mib),
        cost_estimate=pl.CostEstimate(
            flops=2 * rows * cols * depth * len(arrays) * len(ns), bytes_accessed=8 * mib, transcendentals=0
        ),
    )(jnp.stack([turn_by]), *flat, *arrays, *([result] if one else []))


def unscale(value):
    grow = jnp.exp2(value[..., -1:, :, :].astype(jnp.float32)) / weights(value.shape[-1])
    return value[..., :-1, :, :].astype(jnp.float32) * grow


def place(sums, where, result=None):
    _, rows, half = sums[0].shape
    width = 2 * half
    given = [] if result is None else [result]

    def kernel(where, *refs):
        out = refs[-1]
        for i in range(4):
            block = where[3 + i]
            row_ids = where[1] + lax.broadcasted_iota(jnp.int32, (rows, width), 0)
            col_ids = (where[0] * 4 + block) * width + lax.broadcasted_iota(jnp.int32, (rows, width), 1)
            damp = jnp.where(row_ids == col_ids, jnp.float32(damping), jnp.float32(0.0))
            for slab in range(4):
                here = slice(slab * lane, (slab + 1) * lane)
                mine, theirs = refs[i][0, :, here], refs[i][1, :, here]
                for other in range(2):
                    at = (2 * slab + other) * lane
                    there = pl.ds(pl.multiple_of(block * width + at, lane), lane)
                    out[:, there] = jnp.where(where[2] == other, mine, theirs) + damp[:, at : at + lane]

    return pl.pallas_call(
        kernel,
        grid_spec=pltpu.PrefetchScalarGridSpec(
            num_scalar_prefetch=1,
            grid=(1,),
            in_specs=[pl.BlockSpec(v.shape, lambda i, where: (0, 0, 0)) for v in sums]
            + [pl.BlockSpec(memory_space=pl.ANY)] * len(given),
            out_specs=pl.BlockSpec((rows, 4 * width), lambda i, where: (0, where[0])),
        ),
        out_shape=jax.ShapeDtypeStruct((rows, 8 * width), jnp.float32),
        input_output_aliases={5: 0} if given else {},
        compiler_params=pltpu.CompilerParams(vmem_limit_bytes=16 * mib),
    )(jnp.stack(where), *sums, *given)


def per_device(features):
    yh, x, z, yl, core = (lax.axis_index(name) for name in parts)
    rows, cols = features.shape
    half, part = cols // 2, cols // 16

    theirs, both = split(features, yl)
    near_mine = trade(theirs, ring, 1)
    both_away = swap(both)
    kept = turn(both, both_away, core)
    kept_near, kept_far = trade(kept, "x", 1), trade(kept, "x", 3)
    near_mine_away = swap(after(near_mine, kept_near, kept_far))
    got = turn(near_mine, near_mine_away, core)
    got_near, got_far = trade(got, "x", 1), trade(got, "x", 3)
    near_theirs = trade(after(both[0], near_mine), ring, 1)
    tick = swap(after(got[0, :8, :lane]))
    near_theirs_away = swap(near_theirs)
    got_near, got_far, near_theirs = together(got_near, got_far, near_theirs)
    kept_opposite, got_opposite = trade(after(kept_far, got_near), "x", 1), trade(got_near, "x", 3)
    lefts = [(kept, got), (kept_near, got_near), (kept_opposite, got_opposite), (kept_far, got_far)]
    far = trade(after(both, tick), ring, 3)

    first = [(both, 0), (both_away, 0), (near_mine, None), (near_mine_away, None)]
    first += [(both, 1), (both_away, 1), (near_theirs, None), (near_theirs_away, None)]
    tile = product([0, 1, 3], x, lefts, first)
    tile = product([2], x, lefts, first, result=tile)
    far, near_mine, tile = together(far, near_mine, tile)
    opposite_mine, opposite_theirs = trade(far[0], ring, 1), trade(near_mine, ring, 3)
    far_away = swap(far)
    second = [(opposite_mine, None), (swap(opposite_mine), None), (far, 1), (far_away, 1)]
    second += [(opposite_theirs, None), (swap(opposite_theirs), None), (far, 0), (far_away, 0)]

    first_row = ((((yh * 4 + x) * 4 + z) * 2 + yl) * 2 + core) * part
    zero = jnp.int32(0)
    result = None
    for side in range(2):
        if side:
            tile = product([0, 1, 2, 3], x, lefts, second)
        packed = tile.astype(jnp.float16).reshape(16, -1, 8, half)
        across = lax.all_to_all(packed, ("x", "z"), 0, 0, tiled=True)
        if side:
            across, result = together(across, result)
        sums = unscale(across.reshape(4, 4, -1, 8, half)).sum(1).reshape(4, 2, part, half)
        result = place([sums[i] for i in range(4)], [yh ^ side, first_row, yl] + [zero + i for i in range(4)], result)
    return result


def solution(mesh):
    fine = Mesh(mesh.devices.reshape(sizes), parts)
    return jax.shard_map(
        per_device,
        mesh=fine,
        in_specs=(P(("z", "yl", "core"), ("yh", "x")),),
        out_specs=P(parts, None),
        check_vma=False,
    )
```

time: 143 us -> 135 us (0.944)
  waiting for transfers between devices: 72.8 us -> 68.9 us
  local copies, waits for them, and re-layouts: 12.6 us -> 9.28 us
    ppermute x11, waiting for transfers between devices: 41.3 us -> 36.1 us  [trade(): return lax.ppermute(value, axis, [(i, i ^ bits) for i in range(4)])]
    unnamed x26, local copies, waits for them, and re-layouts: 9.67 us -> 7.85 us
    all_to_all x2, starting transfers between devices: 12.6 us -> 10.9 us  [per_device(): across = lax.all_to_all(packed, ('x', 'z'), 0, 0, tiled=True)]
    slice x3 -> x2, local copies, waits for them, and re-layouts: 1.83 us -> 0.14 us  [per_device(): sums[i]]
  transfers between devices with their start and end apart: 19 -> 19, of which waited for: 15 -> 15; matrix products, arithmetic and copies ran while one was open for 6% -> 5% of each run, Pallas kernels for 13% -> 14%
where the time goes in v3:
time: 135 us
  waiting for transfers between devices  68.9 us (51%)
  starting transfers between devices  28.1 us (21%)
  Pallas kernels  20.7 us (15%)
  local copies, waits for them, and re-layouts  9.28 us (7%)
  other arithmetic  7.58 us (6%)
    ppermute x11, waiting for transfers between devices, trade(): return lax.ppermute(value, axis, [(i, i ^ bits) for i in range(4)])  36.1 us
    all_to_all x2, waiting for transfers between devices, per_device(): across = lax.all_to_all(packed, ('x', 'z'), 0, 0, tiled=True)  29.7 us
    ppermute x11, starting transfers between devices, trade(): return lax.ppermute(value, axis, [(i, i ^ bits) for i in range(4)])  17.1 us
    pallas_call x3, Pallas kernels, product(): pl.pallas_call(kernel, grid_spec=pltpu.PrefetchScalarGridSpec(num_scalar_...  16.3 us
    all_to_all x2, starting transfers between devices, per_device(): across = lax.all_to_all(packed, ('x', 'z'), 0, 0, tiled=True)  10.9 us
    unnamed x26, local copies, waits for them, and re-layouts  7.85 us
    convert_element_type x2, other arithmetic, per_device(): packed = tile.astype(jnp.float16).reshape(16, -1, 8, half)  3.86 us
    pallas_call x2, Pallas kernels, place(): pl.pallas_call(kernel, grid_spec=pltpu.PrefetchScalarGridSpec(num_scalar_...  3.47 us
  transfers between devices with their start and end apart: 19, of which 15 were waited for; matrix products, arithmetic and copies ran while one was open for 5% of the time, Pallas kernels for 14%

profile of v3, /device:TPU:0, one launch (start us, length us, event | category | flops | bytes accessed | tf_op | source)
XLA Modules:
  0.0 134.7 jit_solution(579999146457702867)
XLA Ops:
  0.0 1.2 copy-done.6
  1.2 0.3 shard_map.17
  1.6 1.7 %collective-permute-start.1 = (bf16[512,512]{1,0:T(8,128)(2,1)S(1)}, bf16[512,512]{1,0:T(8,128)(2,1)S(1)}, u32[]{:S(2)}, u32[]{:S(2)}) collective-permute-start(bf16[512,512]{1,0:T(8,128)(2,1)S(1)} %get-tuple-element.19), channel_id=1, source_target_pairs={{0,2},{2,0},{64,66},{66,64},{1,3},{3,1},{65,67},{67,65},{4,6},{6,4... | collective-permute-start | bytes 1572872 | tf_op jit(solution)/shard_map/ppermute | solution.py:22
  3.3 0.9 collective-permute-done.refs_1_.refs_7_.refs_11_.refs_3_
  4.2 0.3 shard_map.18.refs_0_
  4.6 2.9 %collective-permute-start.3 = (bf16[2,256,512]{2,1,0:T(8,128)(2,1)S(1)}, bf16[2,256,512]{2,1,0:T(8,128)(2,1)}, u32[]{:S(2)}, u32[]{:S(2)}) collective-permute-start(bf16[2,256,512]{2,1,0:T(8,128)(2,1)S(1)} %shard_map.18.refs_0_), channel_id=1, source_target_pairs={{0,48},{16,32},{32,16},{48,0},{1,49},{17,33},{33,17},{49,1},{2,50}... | collective-permute-start | bytes 1572872 | tf_op jit(solution)/shard_map/ppermute | solution.py:22
  7.7 8.2 %collective-permute-done.1.refs_0_.refs_8_.refs_4_ = bf16[512,512]{1,0:T(8,128)(2,1)S(1)} collective-permute-done((bf16[512,512]{1,0:T(8,128)(2,1)S(1)}, bf16[512,512]{1,0:T(8,128)(2,1)S(1)}, u32[]{:S(2)}, u32[]{:S(2)}) %collective-permute-start.1) | collective-permute-done | bytes 524320 | tf_op jit(solution)/shard_map/ppermute | solution.py:22
  15.9 4.0 %collective-permute-done.3.refs_4_.refs_6_ = bf16[2,256,512]{2,1,0:T(8,128)(2,1)} collective-permute-done((bf16[2,256,512]{2,1,0:T(8,128)(2,1)S(1)}, bf16[2,256,512]{2,1,0:T(8,128)(2,1)}, u32[]{:S(2)}, u32[]{:S(2)}) %collective-permute-start.3) | collective-permute-done | bytes 524320 | tf_op jit(solution)/shard_map/ppermute | solution.py:22
  19.9 1.2 collective-permute-done.2.refs_2_
  21.2 0.8 copy-done.7
  22.0 1.7 %collective-permute-start.7 = (bf16[512,512]{1,0:T(8,128)(2,1)S(1)}, bf16[512,512]{1,0:T(8,128)(2,1)}, u32[]{:S(2)}, u32[]{:S(2)}) collective-permute-start(bf16[512,512]{1,0:T(8,128)(2,1)S(1)} %slice_bitcast_fusion.1), channel_id=1, source_target_pairs={{0,2},{2,0},{64,66},{66,64},{1,3},{3,1},{65,67},{67,65},{4,6},{6,4... | collective-permute-start | bytes 1572872 | tf_op jit(solution)/shard_map/ppermute | solution.py:22
  23.9 0.3 shard_map.19.refs_1_
  24.2 0.4 collective-permute-start.5
  24.6 1.4 %collective-permute-start.6 = (bf16[2,256,512]{2,1,0:T(8,128)(2,1)S(1)}, bf16[2,256,512]{2,1,0:T(8,128)(2,1)S(1)}, u32[]{:S(2)}, u32[]{:S(2)}) collective-permute-start(bf16[2,256,512]{2,1,0:T(8,128)(2,1)S(1)} %shard_map.19.refs_1_), channel_id=1, source_target_pairs={{0,48},{16,32},{32,16},{48,0},{1,49},{17,33},{33,17},{49,1},{2,50}... | collective-permute-start | bytes 1572872 | tf_op jit(solution)/shard_map/ppermute | solution.py:22
  26.0 0.8 copy-done
  26.8 3.0 %collective-permute-start.10 = (bf16[2,512,512]{2,1,0:T(8,128)(2,1)S(1)}, bf16[2,512,512]{2,1,0:T(8,128)(2,1)}, u32[]{:S(2)}, u32[]{:S(2)}) collective-permute-start(bf16[2,512,512]{2,1,0:T(8,128)(2,1)S(1)} %get-tuple-element.18.refs_0_.refs_6_.refs_10_.refs_2_), channel_id=1, source_target_pairs={{0,66},{2,64},{64,2},{66,0},{1,67},{3,65},{65,3},{67,1},{4,70},{6,... | collective-permute-start | bytes 3145736 | tf_op jit(solution)/shard_map/ppermute | solution.py:22
  29.9 6.7 %collective-permute-done.7.refs_12_.refs_8_ = bf16[512,512]{1,0:T(8,128)(2,1)} collective-permute-done((bf16[512,512]{1,0:T(8,128)(2,1)S(1)}, bf16[512,512]{1,0:T(8,128)(2,1)}, u32[]{:S(2)}, u32[]{:S(2)}) %collective-permute-start.7) | collective-permute-done | bytes 524320 | tf_op jit(solution)/shard_map/ppermute | solution.py:22
  36.6 1.8 %collective-permute-done.5.refs_3_ = bf16[2,256,512]{2,1,0:T(8,128)(2,1)} collective-permute-done((bf16[2,256,512]{2,1,0:T(8,128)(2,1)S(1)}, bf16[2,256,512]{2,1,0:T(8,128)(2,1)}, u32[]{:S(2)}, u32[]{:S(2)}) %collective-permute-start.5) | collective-permute-done | bytes 524320 | tf_op jit(solution)/shard_map/ppermute | solution.py:22
  38.4 1.2 collective-permute-done.6.refs_5_.refs_7_
  39.6 0.8 copy-done.10
  40.4 0.4 collective-permute-start.8
  40.8 1.6 %collective-permute-start.9 = (bf16[2,256,512]{2,1,0:T(8,128)(2,1)}, bf16[2,256,512]{2,1,0:T(8,128)(2,1)}, u32[]{:S(2)}, u32[]{:S(2)}) collective-permute-start(bf16[2,256,512]{2,1,0:T(8,128)(2,1)} %collective-permute-done.5.refs_3_), channel_id=1, source_target_pairs={{0,48},{16,32},{32,16},{48,0},{1,49},{17,33},{33,17},{49,1},{2,50}... | collective-permute-start | bytes 1572872 | tf_op jit(solution)/shard_map/ppermute | solution.py:22
  42.4 1.0 copy-done.1
  43.5 1.0 copy-done.4
  44.5 1.0 copy-done.8
  45.6 1.0 copy-done.11
  46.6 5.8 %shard_map.20.refs_10_ = f32[4,4,17,8,512]{4,3,2,1,0:T(8,128)S(1)} custom-call(s32[1]{0:T(128)} %bitcast.3.where, bf16[2,256,512]{2,1,0:T(8,128)(2,1)S(1)} %copy-done.4, bf16[2,256,512]{2,1,0:T(8,128)(2,1)S(1)} %copy-done.1, bf16[2,256,512]{2,1,0:T(8,128)(2,1)S(1)} %copy-done.8, bf16[2,256,512]{2,1,0:T(8,128)(2,1)} %collective-permute-done.5.refs_3_, ...), custom_call_target="tpu_custom_call" | custom-call | flops 3221225472 | bytes 8388608 | tf_op jit(solution)/shard_map/pallas_call | solution.py:142
  52.4 1.3 collective-permute-done.8.refs_0_.refs_4_
  53.7 1.3 collective-permute-done.9.refs_1_.refs_5_
  55.0 3.3 %shard_map.21 = f32[4,4,17,8,512]{4,3,2,1,0:T(8,128)S(1)} custom-call(s32[1]{0:T(128)} %bitcast.3.where, bf16[2,256,512]{2,1,0:T(8,128)(2,1)} %collective-permute-done.8.refs_0_.refs_4_, bf16[2,256,512]{2,1,0:T(8,128)(2,1)} %collective-permute-done.9.refs_1_.refs_5_, ...), custom_call_target="tpu_custom_call", output_to_operand_aliasing={{}: (11, {})} | custom-call | flops 1073741824 | bytes 8388608 | tf_op jit(solution)/shard_map/pallas_call | solution.py:142
  58.3 1.9 %convert_element_type.31 = f16[4,4,17,8,512]{4,3,2,1,0:T(8,128)(2,1)} convert(f32[4,4,17,8,512]{4,3,2,1,0:T(8,128)S(1)} %shard_map.21) | non-fusion elementwise | flops 1114112 | bytes 6684672 | tf_op jit(solution)/shard_map/convert_element_type | solution.py:233
  60.3 6.8 %all-to-all-start.1 = ((f16[16,17,8,512]{3,2,1,0:T(8,128)(2,1)}), f16[16,17,8,512]{3,2,1,0:T(8,128)(2,1)}, u32[]{:S(2)}, u32[]{:S(2)}) async-start(f16[16,17,8,512]{3,2,1,0:T(8,128)(2,1)} %bitcast.34), calls=%async_computation.1 | async-start | bytes 4456448 | tf_op jit(solution)/shard_map/all_to_all | solution.py:234
  67.1 1.1 slice_bitcast_fusion
  68.2 1.6 %collective-permute-start.12 = (bf16[512,512]{1,0:T(8,128)(2,1)S(1)}, bf16[512,512]{1,0:T(8,128)(2,1)S(1)}, u32[]{:S(2)}, u32[]{:S(2)}) collective-permute-start(bf16[512,512]{1,0:T(8,128)(2,1)S(1)} %slice_bitcast_fusion), channel_id=1, source_target_pairs={{0,2},{2,0},{64,66},{66,64},{1,3},{3,1},{65,67},{67,65},{4,6},{6,4... | collective-permute-start | bytes 1572872 | tf_op jit(solution)/shard_map/ppermute | solution.py:22
  69.7 2.2 %collective-permute-start.15 = (bf16[512,512]{1,0:T(8,128)(2,1)S(1)}, bf16[512,512]{1,0:T(8,128)(2,1)S(1)}, u32[]{:S(2)}, u32[]{:S(2)}) collective-permute-start(bf16[512,512]{1,0:T(8,128)(2,1)S(1)} %collective-permute-done.1.refs_0_.refs_8_.refs_4_), channel_id=1, source_target_pairs={{0,66},{2,64},{64,2},{66,0},{1,67},{3,65},{65,3},{67,1},{4,70},{6,... | collective-permute-start | bytes 1572872 | tf_op jit(solution)/shard_map/ppermute | solution.py:22
  71.9 8.1 %collective-permute-done.12.refs_8_ = bf16[512,512]{1,0:T(8,128)(2,1)S(1)} collective-permute-done((bf16[512,512]{1,0:T(8,128)(2,1)S(1)}, bf16[512,512]{1,0:T(8,128)(2,1)S(1)}, u32[]{:S(2)}, u32[]{:S(2)}) %collective-permute-start.12) | collective-permute-done | bytes 524320 | tf_op jit(solution)/shard_map/ppermute | solution.py:22
  80.0 2.3 %collective-permute-done.15.refs_12_ = bf16[512,512]{1,0:T(8,128)(2,1)S(1)} collective-permute-done((bf16[512,512]{1,0:T(8,128)(2,1)S(1)}, bf16[512,512]{1,0:T(8,128)(2,1)S(1)}, u32[]{:S(2)}, u32[]{:S(2)}) %collective-permute-start.15) | collective-permute-done | bytes 524320 | tf_op jit(solution)/shard_map/ppermute | solution.py:22
  82.3 1.9 %collective-permute-done.16.refs_13_ = bf16[512,512]{1,0:T(8,128)(2,1)S(1)} collective-permute-done((bf16[512,512]{1,0:T(8,128)(2,1)S(1)}, bf16[512,512]{1,0:T(8,128)(2,1)S(1)}, u32[]{:S(2)}, u32[]{:S(2)}) %collective-permute-start.16) | collective-permute-done | bytes 524320 | tf_op jit(solution)/shard_map/ppermute | solution.py:18
  84.2 7.2 %shard_map.22 = f32[4,4,17,8,512]{4,3,2,1,0:T(8,128)S(1)} custom-call(s32[1]{0:T(128)} %bitcast.3.where, bf16[2,256,512]{2,1,0:T(8,128)(2,1)S(1)} %copy-done.5, bf16[2,256,512]{2,1,0:T(8,128)(2,1)S(1)} %copy-done.2, bf16[2,256,512]{2,1,0:T(8,128)(2,1)S(1)} %copy-done.9, bf16[2,256,512]{2,1,0:T(8,128)(2,1)} %collective-permute-done.5.refs_3_, ...), custom_call_target="tpu_custom_call" | custom-call | flops 4294967296 | bytes 8388608 | tf_op jit(solution)/shard_map/pallas_call | solution.py:142
  91.4 1.9 %convert_element_type.30 = f16[4,4,17,8,512]{4,3,2,1,0:T(8,128)(2,1)} convert(f32[4,4,17,8,512]{4,3,2,1,0:T(8,128)S(1)} %shard_map.22) | non-fusion elementwise | flops 1114112 | bytes 6684672 | tf_op jit(solution)/shard_map/convert_element_type | solution.py:233
  93.4 3.3 %all-to-all-done.1 = f16[16,17,8,512]{3,2,1,0:T(8,128)(2,1)} async-done(((f16[16,17,8,512]{3,2,1,0:T(8,128)(2,1)}), f16[16,17,8,512]{3,2,1,0:T(8,128)(2,1)}, u32[]{:S(2)}, u32[]{:S(2)}) %all-to-all-start.1) | async-done | bytes 2228256 | tf_op jit(solution)/shard_map/all_to_all | solution.py:234
  96.7 4.1 %all-to-all-start = ((f16[16,17,8,512]{3,2,1,0:T(8,128)(2,1)}), f16[16,17,8,512]{3,2,1,0:T(8,128)(2,1)S(1)}, u32[]{:S(2)}, u32[]{:S(2)}) async-start(f16[16,17,8,512]{3,2,1,0:T(8,128)(2,1)} %bitcast.7), calls=%async_computation | async-start | bytes 4456448 | tf_op jit(solution)/shard_map/all_to_all | solution.py:234
  101.0 1.0 divide_bitcast_fusion.1
  102.0 2.2 %multiply_reduce_fusion.1 = f32[4,16,8,512]{3,2,1,0:T(8,128)S(1)} fusion(f16[4,4,17,8,512]{4,3,2,1,0:T(8,128)(2,1)} %bitcast.10, f32[4,4,8,512]{3,2,1,0:T(8,128)S(1)} %divide_bitcast_fusion.1), kind=kLoop, calls=%fused_computation.1 | loop fusion | flops 2883584 | bytes 3407872 | tf_op jit(solution)/shard_map/reduce_sum | solution.py:237
  104.3 1.7 %shard_map.23.refs_4_ = f32[64,8192]{1,0:T(8,128)} custom-call(s32[7]{0:T(128)S(1)} %stack.37.where, f32[2,64,512]{2,1,0:T(8,128)S(1)} %bitcast.29, f32[2,64,512]{2,1,0:T(8,128)S(1)} %bitcast.28, f32[2,64,512]{2,1,0:T(8,128)S(1)} %bitcast.27, f32[2,64,512]{2,1,0:T(8,128)S(1)} %bitcast.26), custom_call_target="tpu_custom_call" | custom-call | tf_op jit(solution)/shard_map/pallas_call | solution.py:181
  106.0 26.4 %all-to-all-done = f16[16,17,8,512]{3,2,1,0:T(8,128)(2,1)S(1)} async-done(((f16[16,17,8,512]{3,2,1,0:T(8,128)(2,1)}), f16[16,17,8,512]{3,2,1,0:T(8,128)(2,1)S(1)}, u32[]{:S(2)}, u32[]{:S(2)}) %all-to-all-start) | async-done | bytes 2228256 | tf_op jit(solution)/shard_map/all_to_all | solution.py:234
  132.4 0.5 multiply_reduce_fusion
  133.0 1.7 %shard_map.24 = f32[64,8192]{1,0:T(8,128)} custom-call(s32[7]{0:T(128)S(1)} %stack.33.where, f32[2,64,512]{2,1,0:T(8,128)S(1)} %bitcast.33, f32[2,64,512]{2,1,0:T(8,128)S(1)} %bitcast.32, f32[2,64,512]{2,1,0:T(8,128)S(1)} %bitcast.31, f32[2,64,512]{2,1,0:T(8,128)S(1)} %bitcast.30, f32[64,8192]{1,0:T(8,128)} %shard_map.23.refs_4_), custom_call_target="tpu_custom_call", output_to_operand_aliasing={{}: (5, {})} | custom-call | tf_op jit(solution)/shard_map/pallas_call | solution.py:181
  (37 shorter events, 1.0 us)
Async XLA Ops:
  0.0 1.2 copy-start.6
  1.5 2.7 %collective-permute-start = (bf16[2,512,512]{2,1,0:T(8,128)(2,1)S(1)}, bf16[2,512,512]{2,1,0:T(8,128)(2,1)S(1)}, u32[]{:S(2)}, u32[]{:S(2)}) collective-permute-start(bf16[2,512,512]{2,1,0:T(8,128)(2,1)S(1)} %get-tuple-element.18.refs_0_.refs_6_.refs_10_.refs_2_), channel_id=1, source_target_pairs={{0,1},{1,0},{2,3},{3,2},{4,5},{5,4},{6,7},{7,6},{8,9},{9,8},{10,11... | collective-permute-start | bytes 3145736 | tf_op jit(solution)/shard_map/ppermute | solution.py:18
  1.6 14.3 %collective-permute-start.1 = (bf16[512,512]{1,0:T(8,128)(2,1)S(1)}, bf16[512,512]{1,0:T(8,128)(2,1)S(1)}, u32[]{:S(2)}, u32[]{:S(2)}) collective-permute-start(bf16[512,512]{1,0:T(8,128)(2,1)S(1)} %get-tuple-element.19), channel_id=1, source_target_pairs={{0,2},{2,0},{64,66},{66,64},{1,3},{3,1},{65,67},{67,65},{4,6},{6,4... | collective-permute-start | bytes 1572872 | tf_op jit(solution)/shard_map/ppermute | solution.py:22
  4.6 19.1 %copy-start.3 = (bf16[2,256,512]{2,1,0:T(8,128)(2,1)}, bf16[2,256,512]{2,1,0:T(8,128)(2,1)S(1)}, u32[]{:S(2)}) copy-start(bf16[2,256,512]{2,1,0:T(8,128)(2,1)S(1)} %shard_map.18.refs_0_) | copy-start | bytes 1572868
  4.6 15.4 %collective-permute-start.3 = (bf16[2,256,512]{2,1,0:T(8,128)(2,1)S(1)}, bf16[2,256,512]{2,1,0:T(8,128)(2,1)}, u32[]{:S(2)}, u32[]{:S(2)}) collective-permute-start(bf16[2,256,512]{2,1,0:T(8,128)(2,1)S(1)} %shard_map.18.refs_0_), channel_id=1, source_target_pairs={{0,48},{16,32},{32,16},{48,0},{1,49},{17,33},{33,17},{49,1},{2,50}... | collective-permute-start | bytes 1572872 | tf_op jit(solution)/shard_map/ppermute | solution.py:22
  7.5 13.7 %collective-permute-start.2 = (bf16[2,256,512]{2,1,0:T(8,128)(2,1)S(1)}, bf16[2,256,512]{2,1,0:T(8,128)(2,1)S(1)}, u32[]{:S(2)}, u32[]{:S(2)}) collective-permute-start(bf16[2,256,512]{2,1,0:T(8,128)(2,1)S(1)} %shard_map.18.refs_0_), channel_id=1, source_target_pairs={{0,16},{16,0},{32,48},{48,32},{1,17},{17,1},{33,49},{49,33},{2,18}... | collective-permute-start | bytes 1572872 | tf_op jit(solution)/shard_map/ppermute | solution.py:22
  21.2 0.8 copy-start.7
  22.0 1.9 %collective-permute-start.4 = (bf16[512,512]{1,0:T(8,128)(2,1)S(1)}, bf16[512,512]{1,0:T(8,128)(2,1)S(1)}, u32[]{:S(2)}, u32[]{:S(2)}) collective-permute-start(bf16[512,512]{1,0:T(8,128)(2,1)S(1)} %collective-permute-done.1.refs_0_.refs_8_.refs_4_), channel_id=1, source_target_pairs={{0,1},{1,0},{2,3},{3,2},{4,5},{5,4},{6,7},{7,6},{8,9},{9,8},{10,11... | collective-permute-start | bytes 1572872 | tf_op jit(solution)/shard_map/ppermute | solution.py:18
  22.0 14.5 %collective-permute-start.7 = (bf16[512,512]{1,0:T(8,128)(2,1)S(1)}, bf16[512,512]{1,0:T(8,128)(2,1)}, u32[]{:S(2)}, u32[]{:S(2)}) collective-permute-start(bf16[512,512]{1,0:T(8,128)(2,1)S(1)} %slice_bitcast_fusion.1), channel_id=1, source_target_pairs={{0,2},{2,0},{64,66},{66,64},{1,3},{3,1},{65,67},{67,65},{4,6},{6,4... | collective-permute-start | bytes 1572872 | tf_op jit(solution)/shard_map/ppermute | solution.py:22
  24.2 14.2 %collective-permute-start.5 = (bf16[2,256,512]{2,1,0:T(8,128)(2,1)S(1)}, bf16[2,256,512]{2,1,0:T(8,128)(2,1)}, u32[]{:S(2)}, u32[]{:S(2)}) collective-permute-start(bf16[2,256,512]{2,1,0:T(8,128)(2,1)S(1)} %shard_map.19.refs_1_), channel_id=1, source_target_pairs={{0,16},{16,0},{32,48},{48,32},{1,17},{17,1},{33,49},{49,33},{2,18}... | collective-permute-start | bytes 1572872 | tf_op jit(solution)/shard_map/ppermute | solution.py:22
  24.6 15.0 %collective-permute-start.6 = (bf16[2,256,512]{2,1,0:T(8,128)(2,1)S(1)}, bf16[2,256,512]{2,1,0:T(8,128)(2,1)S(1)}, u32[]{:S(2)}, u32[]{:S(2)}) collective-permute-start(bf16[2,256,512]{2,1,0:T(8,128)(2,1)S(1)} %shard_map.19.refs_1_), channel_id=1, source_target_pairs={{0,48},{16,32},{32,16},{48,0},{1,49},{17,33},{33,17},{49,1},{2,50}... | collective-permute-start | bytes 1572872 | tf_op jit(solution)/shard_map/ppermute | solution.py:22
  26.0 0.8 copy-start
  26.8 31.5 %collective-permute-start.10 = (bf16[2,512,512]{2,1,0:T(8,128)(2,1)S(1)}, bf16[2,512,512]{2,1,0:T(8,128)(2,1)}, u32[]{:S(2)}, u32[]{:S(2)}) collective-permute-start(bf16[2,512,512]{2,1,0:T(8,128)(2,1)S(1)} %get-tuple-element.18.refs_0_.refs_6_.refs_10_.refs_2_), channel_id=1, source_target_pairs={{0,66},{2,64},{64,2},{66,0},{1,67},{3,65},{65,3},{67,1},{4,70},{6,... | collective-permute-start | bytes 3145736 | tf_op jit(solution)/shard_map/ppermute | solution.py:22
  36.5 5.9 %collective-permute-start.11 = (bf16[512,512]{1,0:T(8,128)(2,1)}, bf16[512,512]{1,0:T(8,128)(2,1)}, u32[]{:S(2)}, u32[]{:S(2)}) collective-permute-start(bf16[512,512]{1,0:T(8,128)(2,1)} %collective-permute-done.7.refs_12_.refs_8_), channel_id=1, source_target_pairs={{0,1},{1,0},{2,3},{3,2},{4,5},{5,4},{6,7},{7,6},{8,9},{9,8},{10,11... | collective-permute-start | bytes 1572872 | tf_op jit(solution)/shard_map/ppermute | solution.py:18
  39.6 0.8 copy-start.10
  40.4 13.3 %collective-permute-start.8 = (bf16[2,256,512]{2,1,0:T(8,128)(2,1)}, bf16[2,256,512]{2,1,0:T(8,128)(2,1)}, u32[]{:S(2)}, u32[]{:S(2)}) collective-permute-start(bf16[2,256,512]{2,1,0:T(8,128)(2,1)} %collective-permute-done.3.refs_4_.refs_6_), channel_id=1, source_target_pairs={{0,16},{16,0},{32,48},{48,32},{1,17},{17,1},{33,49},{49,33},{2,18}... | collective-permute-start | bytes 1572872 | tf_op jit(solution)/shard_map/ppermute | solution.py:22
  40.8 14.2 %collective-permute-start.9 = (bf16[2,256,512]{2,1,0:T(8,128)(2,1)}, bf16[2,256,512]{2,1,0:T(8,128)(2,1)}, u32[]{:S(2)}, u32[]{:S(2)}) collective-permute-start(bf16[2,256,512]{2,1,0:T(8,128)(2,1)} %collective-permute-done.5.refs_3_), channel_id=1, source_target_pairs={{0,48},{16,32},{32,16},{48,0},{1,49},{17,33},{33,17},{49,1},{2,50}... | collective-permute-start | bytes 1572872 | tf_op jit(solution)/shard_map/ppermute | solution.py:22
  42.4 1.0 copy-start.1
  43.5 1.0 copy-start.4
  44.5 1.0 copy-start.8
  45.6 1.0 copy-start.11
  60.2 23.9 %copy-start.2 = (bf16[2,256,512]{2,1,0:T(8,128)(2,1)S(1)}, bf16[2,256,512]{2,1,0:T(8,128)(2,1)}, u32[]{:S(2)}) copy-start(bf16[2,256,512]{2,1,0:T(8,128)(2,1)} %copy-done) | copy-start | bytes 1572868
  60.2 23.9 %copy-start.5 = (bf16[2,256,512]{2,1,0:T(8,128)(2,1)S(1)}, bf16[2,256,512]{2,1,0:T(8,128)(2,1)}, u32[]{:S(2)}) copy-start(bf16[2,256,512]{2,1,0:T(8,128)(2,1)} %copy-done.3) | copy-start | bytes 1572868
  60.2 23.9 %copy-start.9 = (bf16[2,256,512]{2,1,0:T(8,128)(2,1)S(1)}, bf16[2,256,512]{2,1,0:T(8,128)(2,1)}, u32[]{:S(2)}) copy-start(bf16[2,256,512]{2,1,0:T(8,128)(2,1)} %copy-done.7) | copy-start | bytes 1572868
  60.3 23.9 %copy-start.12 = (bf16[2,256,512]{2,1,0:T(8,128)(2,1)S(1)}, bf16[2,256,512]{2,1,0:T(8,128)(2,1)}, u32[]{:S(2)}) copy-start(bf16[2,256,512]{2,1,0:T(8,128)(2,1)} %copy-done.10) | copy-start | bytes 1572868
  60.3 36.5 %all-to-all-start.1 = ((f16[16,17,8,512]{3,2,1,0:T(8,128)(2,1)}), f16[16,17,8,512]{3,2,1,0:T(8,128)(2,1)}, u32[]{:S(2)}, u32[]{:S(2)}) async-start(f16[16,17,8,512]{3,2,1,0:T(8,128)(2,1)} %bitcast.34), calls=%async_computation.1 | async-start | bytes 4456448 | tf_op jit(solution)/shard_map/all_to_all | solution.py:234
  68.2 11.8 %collective-permute-start.12 = (bf16[512,512]{1,0:T(8,128)(2,1)S(1)}, bf16[512,512]{1,0:T(8,128)(2,1)S(1)}, u32[]{:S(2)}, u32[]{:S(2)}) collective-permute-start(bf16[512,512]{1,0:T(8,128)(2,1)S(1)} %slice_bitcast_fusion), channel_id=1, source_target_pairs={{0,2},{2,0},{64,66},{66,64},{1,3},{3,1},{65,67},{67,65},{4,6},{6,4... | collective-permute-start | bytes 1572872 | tf_op jit(solution)/shard_map/ppermute | solution.py:22
  69.7 12.6 %collective-permute-start.15 = (bf16[512,512]{1,0:T(8,128)(2,1)S(1)}, bf16[512,512]{1,0:T(8,128)(2,1)S(1)}, u32[]{:S(2)}, u32[]{:S(2)}) collective-permute-start(bf16[512,512]{1,0:T(8,128)(2,1)S(1)} %collective-permute-done.1.refs_0_.refs_8_.refs_4_), channel_id=1, source_target_pairs={{0,66},{2,64},{64,2},{66,0},{1,67},{3,65},{65,3},{67,1},{4,70},{6,... | collective-permute-start | bytes 1572872 | tf_op jit(solution)/shard_map/ppermute | solution.py:22
  71.9 12.3 %collective-permute-start.14 = (bf16[2,512,512]{2,1,0:T(8,128)(2,1)}, bf16[2,512,512]{2,1,0:T(8,128)(2,1)S(1)}, u32[]{:S(2)}, u32[]{:S(2)}) collective-permute-start(bf16[2,512,512]{2,1,0:T(8,128)(2,1)} %collective-permute-done.10.refs_10_.refs_14_), channel_id=1, source_target_pairs={{0,1},{1,0},{2,3},{3,2},{4,5},{5,4},{6,7},{7,6},{8,9},{9,8},{10,11... | collective-permute-start | bytes 3145736 | tf_op jit(solution)/shard_map/ppermute | solution.py:18
  80.0 2.3 %collective-permute-start.13 = (bf16[512,512]{1,0:T(8,128)(2,1)S(1)}, bf16[512,512]{1,0:T(8,128)(2,1)S(1)}, u32[]{:S(2)}, u32[]{:S(2)}) collective-permute-start(bf16[512,512]{1,0:T(8,128)(2,1)S(1)} %collective-permute-done.12.refs_8_), channel_id=1, source_target_pairs={{0,1},{1,0},{2,3},{3,2},{4,5},{5,4},{6,7},{7,6},{8,9},{9,8},{10,11... | collective-permute-start | bytes 1572872 | tf_op jit(solution)/shard_map/ppermute | solution.py:18
  82.3 1.9 %collective-permute-start.16 = (bf16[512,512]{1,0:T(8,128)(2,1)S(1)}, bf16[512,512]{1,0:T(8,128)(2,1)S(1)}, u32[]{:S(2)}, u32[]{:S(2)}) collective-permute-start(bf16[512,512]{1,0:T(8,128)(2,1)S(1)} %collective-permute-done.15.refs_12_), channel_id=1, source_target_pairs={{0,1},{1,0},{2,3},{3,2},{4,5},{5,4},{6,7},{7,6},{8,9},{9,8},{10,11... | collective-permute-start | bytes 1572872 | tf_op jit(solution)/shard_map/ppermute | solution.py:18
  96.7 35.7 %all-to-all-start = ((f16[16,17,8,512]{3,2,1,0:T(8,128)(2,1)}), f16[16,17,8,512]{3,2,1,0:T(8,128)(2,1)S(1)}, u32[]{:S(2)}, u32[]{:S(2)}) async-start(f16[16,17,8,512]{3,2,1,0:T(8,128)(2,1)} %bitcast.7), calls=%async_computation | async-start | bytes 4456448 | tf_op jit(solution)/shard_map/all_to_all | solution.py:234

commit v4 on v3

--- a/solution.py
+++ b/solution.py
@@ -24,6 +24,10 @@
 
 def together(*values):
     return lax.optimization_barrier(values)
+
+
+def in_hbm(value):
+    return pltpu.with_memory_space_constraint(value, pltpu.HBM)
 
 
 def after(value, *others):
@@ -88,11 +92,11 @@
     return 1.0 + lax.broadcasted_iota(jnp.int32, (1, cols), 1).astype(jnp.float32) / cols
 
 
-def product(ns, turn_by, lefts, rights, by_z=False, result=None):
+def product(ns, turn_by, lefts, rights, by_z=False, result=None, alone=False):
     flat = [part for n in ns for part in lefts[n]]
     starts = [sum(len(lefts[m]) for m in ns[:i]) for i in range(len(ns))]
     arrays, picks = zip(*rights)
-    rows, depth, cols, block = flat[0].shape[-2], flat[0].shape[-1], arrays[0].shape[-1], 256
+    rows, depth, cols, block = flat[0].shape[-2], flat[0].shape[-1], arrays[0].shape[-1], 512
     eights, one = rows // 4 // 8, result is not None
 
     def kernel(where, *refs):
@@ -119,7 +123,7 @@
                 if by_z:
                     at = (slab ^ where[0], i)
                 else:
-                    at = (0 if one else where[0] ^ n, slab)
+                    at = (0 if one or alone else where[0] ^ n, slab)
                 for c in range(2):
                     some = totals[c][slab * 8 * eights : (slab + 1) * 8 * eights] * shrink
                     out[(*at, slice(c * eights, (c + 1) * eights))] = some.reshape(eights, 8, block)
@@ -134,23 +138,23 @@
     height = 2 * eights + 1
     if one:
         specs.append(pl.BlockSpec(memory_space=pl.ANY))
-    count = len(ns) if by_z else 4
+    count, slots = (len(ns) if by_z else 4), (1 if alone else 4)
     if one:
         out_spec = pl.BlockSpec((1, 4, height, 8, block), lambda i, where: (where[0] ^ ns[0], 0, 0, 0, i))
     else:
-        out_spec = pl.BlockSpec((4, count, height, 8, block), lambda i, where: (0, 0, 0, 0, i))
+        out_spec = pl.BlockSpec((slots, count, height, 8, block), lambda i, where: (0, 0, 0, 0, i))
     return pl.pallas_call(
         kernel,
         grid_spec=pltpu.PrefetchScalarGridSpec(
             num_scalar_prefetch=1, grid=(cols // block,), in_specs=specs, out_specs=out_spec
         ),
-        out_shape=jax.ShapeDtypeStruct((4, count, height, 8, cols), jnp.float32),
+        out_shape=jax.ShapeDtypeStruct((slots, count, height, 8, cols), jnp.float32),
         input_output_aliases={len(specs): 0} if one else {},
         compiler_params=pltpu.CompilerParams(vmem_limit_bytes=32 * mib),
         cost_estimate=pl.CostEstimate(
             flops=2 * rows * cols * depth * len(arrays) * len(ns), bytes_accessed=8 * mib, transcendentals=0
         ),
-    )(jnp.stack([turn_by]), *flat, *arrays, *([result] if one else []))
+    )(jnp.stack([turn_by]), *[in_hbm(v) if n in (1, 3) else v for n in ns for v in lefts[n]], *arrays, *([result] if one else []))
 
 
 def unscale(value):
@@ -217,8 +221,10 @@
     first = [(both, 0), (both_away, 0), (near_mine, None), (near_mine_away, None)]
     first += [(both, 1), (both_away, 1), (near_theirs, None), (near_theirs_away, None)]
     tile = product([0, 1, 3], x, lefts, first)
-    tile = product([2], x, lefts, first, result=tile)
-    far, near_mine, tile = together(far, near_mine, tile)
+    tile = tile.astype(jnp.float16)
+    last = product([2], x, lefts, first, alone=True).astype(jnp.float16)
+    tile = lax.dynamic_update_slice_in_dim(tile, last, x ^ 2, 0)
+    far, near_mine, _ = together(far, near_mine, tile)
     opposite_mine, opposite_theirs = trade(far[0], ring, 1), trade(near_mine, ring, 3)
     far_away = swap(far)
     second = [(opposite_mine, None), (swap(opposite_mine), None), (far, 1), (far_away, 1)]

time: 135 us -> 134 us (level)
  waiting for transfers between devices: 68.9 us -> 72 us
    ppermute x11, waiting for transfers between devices: 36.1 us -> 39.5 us  [trade(): return lax.ppermute(value, axis, [(i, i ^ bits) for i in range(4)])]
    convert_element_type x2 -> x1, other arithmetic: 3.86 us -> 1.94 us  [per_device(): packed = tile.astype(jnp.float16).reshape(16, -1, 8, half)]
    unnamed x26 -> x20, local copies, waits for them, and re-layouts: 7.85 us -> 6.68 us
  transfers between devices with their start and end apart: 19 -> 19, of which waited for: 15 -> 16; matrix products, arithmetic and copies ran while one was open for 5% -> 5% of each run, Pallas kernels for 14% -> 13%
where the time goes in v4:
time: 134 us
  waiting for transfers between devices  72 us (54%)
  starting transfers between devices  27.5 us (21%)
  Pallas kernels  19.7 us (15%)
  local copies, waits for them, and re-layouts  8.1 us (6%)
  other arithmetic  6.31 us (5%)
    ppermute x11, waiting for transfers between devices, trade(): return lax.ppermute(value, axis, [(i, i ^ bits) for i in range(4)])  39.5 us
    all_to_all x2, waiting for transfers between devices, per_device(): across = lax.all_to_all(packed, ('x', 'z'), 0, 0, tiled=True)  29.4 us
    ppermute x11, starting transfers between devices, trade(): return lax.ppermute(value, axis, [(i, i ^ bits) for i in range(4)])  16.5 us
    pallas_call x3, Pallas kernels, product(): pl.pallas_call(kernel, grid_spec=pltpu.PrefetchScalarGridSpec(num_scalar_...  15.3 us
    all_to_all x2, starting transfers between devices, per_device(): across = lax.all_to_all(packed, ('x', 'z'), 0, 0, tiled=True)  10.9 us
    unnamed x20, local copies, waits for them, and re-layouts  6.68 us
    pallas_call x2, Pallas kernels, place(): pl.pallas_call(kernel, grid_spec=pltpu.PrefetchScalarGridSpec(num_scalar_...  3.47 us
    ppermute x6, waiting for transfers between devices, swap(): return lax.ppermute(value, 'core', [(0, 1), (1, 0)])  3.02 us
  transfers between devices with their start and end apart: 19, of which 16 were waited for; matrix products, arithmetic and copies ran while one was open for 5% of the time, Pallas kernels for 13%

profile of v4, /device:TPU:0, one launch (start us, length us, event | category | flops | bytes accessed | tf_op | source)
XLA Modules:
  0.0 133.8 jit_solution(7990471718368657997)
XLA Ops:
  0.0 1.2 copy-done.6
  1.2 0.3 shard_map.17
  1.6 1.7 %collective-permute-start.1 = (bf16[512,512]{1,0:T(8,128)(2,1)S(1)}, bf16[512,512]{1,0:T(8,128)(2,1)S(1)}, u32[]{:S(2)}, u32[]{:S(2)}) collective-permute-start(bf16[512,512]{1,0:T(8,128)(2,1)S(1)} %get-tuple-element.18), channel_id=1, source_target_pairs={{0,2},{2,0},{64,66},{66,64},{1,3},{3,1},{65,67},{67,65},{4,6},{6,4... | collective-permute-start | bytes 1572872 | tf_op jit(solution)/shard_map/ppermute | solution.py:22
  3.3 0.9 collective-permute-done.refs_1_.refs_7_.refs_11_.refs_3_
  4.2 0.3 shard_map.18.refs_0_
  4.6 2.9 %collective-permute-start.3 = (bf16[2,256,512]{2,1,0:T(8,128)(2,1)S(1)}, bf16[2,256,512]{2,1,0:T(8,128)(2,1)}, u32[]{:S(2)}, u32[]{:S(2)}) collective-permute-start(bf16[2,256,512]{2,1,0:T(8,128)(2,1)S(1)} %shard_map.18.refs_0_), channel_id=1, source_target_pairs={{0,48},{16,32},{32,16},{48,0},{1,49},{17,33},{33,17},{49,1},{2,50}... | collective-permute-start | bytes 1572872 | tf_op jit(solution)/shard_map/ppermute | solution.py:22
  7.7 8.2 %collective-permute-done.1.refs_0_.refs_8_.refs_4_ = bf16[512,512]{1,0:T(8,128)(2,1)S(1)} collective-permute-done((bf16[512,512]{1,0:T(8,128)(2,1)S(1)}, bf16[512,512]{1,0:T(8,128)(2,1)S(1)}, u32[]{:S(2)}, u32[]{:S(2)}) %collective-permute-start.1) | collective-permute-done | bytes 524320 | tf_op jit(solution)/shard_map/ppermute | solution.py:22
  15.9 4.0 %collective-permute-done.3.refs_4_.refs_6_ = bf16[2,256,512]{2,1,0:T(8,128)(2,1)} collective-permute-done((bf16[2,256,512]{2,1,0:T(8,128)(2,1)S(1)}, bf16[2,256,512]{2,1,0:T(8,128)(2,1)}, u32[]{:S(2)}, u32[]{:S(2)}) %collective-permute-start.3) | collective-permute-done | bytes 524320 | tf_op jit(solution)/shard_map/ppermute | solution.py:22
  19.9 1.2 collective-permute-done.2.refs_2_
  21.2 0.8 copy-done.8
  22.0 1.7 %collective-permute-start.7 = (bf16[512,512]{1,0:T(8,128)(2,1)S(1)}, bf16[512,512]{1,0:T(8,128)(2,1)}, u32[]{:S(2)}, u32[]{:S(2)}) collective-permute-start(bf16[512,512]{1,0:T(8,128)(2,1)S(1)} %slice_bitcast_fusion.1), channel_id=1, source_target_pairs={{0,2},{2,0},{64,66},{66,64},{1,3},{3,1},{65,67},{67,65},{4,6},{6,4... | collective-permute-start | bytes 1572872 | tf_op jit(solution)/shard_map/ppermute | solution.py:22
  23.9 0.3 shard_map.19.refs_1_
  24.2 0.4 collective-permute-start.5
  24.6 1.4 %collective-permute-start.6 = (bf16[2,256,512]{2,1,0:T(8,128)(2,1)S(1)}, bf16[2,256,512]{2,1,0:T(8,128)(2,1)S(1)}, u32[]{:S(2)}, u32[]{:S(2)}) collective-permute-start(bf16[2,256,512]{2,1,0:T(8,128)(2,1)S(1)} %shard_map.19.refs_1_), channel_id=1, source_target_pairs={{0,48},{16,32},{32,16},{48,0},{1,49},{17,33},{33,17},{49,1},{2,50}... | collective-permute-start | bytes 1572872 | tf_op jit(solution)/shard_map/ppermute | solution.py:22
  26.0 0.8 copy-done
  26.8 9.7 %collective-permute-done.7.refs_12_.refs_8_ = bf16[512,512]{1,0:T(8,128)(2,1)} collective-permute-done((bf16[512,512]{1,0:T(8,128)(2,1)S(1)}, bf16[512,512]{1,0:T(8,128)(2,1)}, u32[]{:S(2)}, u32[]{:S(2)}) %collective-permute-start.7) | collective-permute-done | bytes 524320 | tf_op jit(solution)/shard_map/ppermute | solution.py:22
  36.6 1.8 %collective-permute-done.5.refs_3_ = bf16[2,256,512]{2,1,0:T(8,128)(2,1)} collective-permute-done((bf16[2,256,512]{2,1,0:T(8,128)(2,1)S(1)}, bf16[2,256,512]{2,1,0:T(8,128)(2,1)}, u32[]{:S(2)}, u32[]{:S(2)}) %collective-permute-start.5) | collective-permute-done | bytes 524320 | tf_op jit(solution)/shard_map/ppermute | solution.py:22
  38.4 1.2 collective-permute-done.6.refs_5_.refs_7_
  39.6 0.4 collective-permute-start.8
  40.0 0.4 copy-done.9
  40.4 1.6 %collective-permute-start.9 = (bf16[2,256,512]{2,1,0:T(8,128)(2,1)}, bf16[2,256,512]{2,1,0:T(8,128)(2,1)}, u32[]{:S(2)}, u32[]{:S(2)}) collective-permute-start(bf16[2,256,512]{2,1,0:T(8,128)(2,1)} %collective-permute-done.5.refs_3_), channel_id=1, source_target_pairs={{0,48},{16,32},{32,16},{48,0},{1,49},{17,33},{33,17},{49,1},{2,50}... | collective-permute-start | bytes 1572872 | tf_op jit(solution)/shard_map/ppermute | solution.py:22
  42.0 3.0 %collective-permute-start.10 = (bf16[2,512,512]{2,1,0:T(8,128)(2,1)S(1)}, bf16[2,512,512]{2,1,0:T(8,128)(2,1)}, u32[]{:S(2)}, u32[]{:S(2)}) collective-permute-start(bf16[2,512,512]{2,1,0:T(8,128)(2,1)S(1)} %get-tuple-element.17.refs_0_.refs_6_.refs_10_.refs_2_), channel_id=1, source_target_pairs={{0,66},{2,64},{64,2},{66,0},{1,67},{3,65},{65,3},{67,1},{4,70},{6,... | collective-permute-start | bytes 3145736 | tf_op jit(solution)/shard_map/ppermute | solution.py:22
  45.0 1.0 copy-done.1
  46.1 1.0 copy-done.4
  47.1 5.5 %shard_map.20 = f32[4,4,17,8,512]{4,3,2,1,0:T(8,128)S(1)} custom-call(s32[1]{0:T(128)} %bitcast.3.where, bf16[2,256,512]{2,1,0:T(8,128)(2,1)S(1)} %copy-done.4, bf16[2,256,512]{2,1,0:T(8,128)(2,1)S(1)} %copy-done.1, bf16[2,256,512]{2,1,0:T(8,128)(2,1)} %copy-done.8, bf16[2,256,512]{2,1,0:T(8,128)(2,1)} %collective-permute-done.5.refs_3_, ...), custom_call_target="tpu_custom_call" | custom-call | flops 3221225472 | bytes 8388608 | tf_op jit(solution)/shard_map/pallas_call | solution.py:146
  52.6 0.5 convert_element_type.33
  53.2 1.7 %collective-permute-done.9.refs_1_.refs_5_ = bf16[2,256,512]{2,1,0:T(8,128)(2,1)} collective-permute-done((bf16[2,256,512]{2,1,0:T(8,128)(2,1)}, bf16[2,256,512]{2,1,0:T(8,128)(2,1)}, u32[]{:S(2)}, u32[]{:S(2)}) %collective-permute-start.9) | collective-permute-done | bytes 524320 | tf_op jit(solution)/shard_map/ppermute | solution.py:22
  54.8 2.9 %shard_map.21 = f32[1,4,17,8,512]{4,3,2,1,0:T(8,128)S(1)} custom-call(s32[1]{0:T(128)} %bitcast.3.where, bf16[2,256,512]{2,1,0:T(8,128)(2,1)} %collective-permute-done.8.refs_0_.refs_4_, bf16[2,256,512]{2,1,0:T(8,128)(2,1)} %collective-permute-done.9.refs_1_.refs_5_, bf16[2,512,512]{2,1,0:T(8,128)(2,1)S(1)} %get-tuple-element.17.refs_0_.refs_6_.refs_10_.refs_2_, ...), custom_call_target="tpu_custom_call" | custom-call | flops 1073741824 | bytes 8388608 | tf_op jit(solution)/shard_map/pallas_call | solution.py:146
  57.9 1.4 %copy-done.7 = f16[4,4,17,8,512]{4,3,2,1,0:T(8,128)(2,1)} copy-done((f16[4,4,17,8,512]{4,3,2,1,0:T(8,128)(2,1)}, f16[4,4,17,8,512]{4,3,2,1,0:T(8,128)(2,1)S(1)}, u32[]{:S(2)}) %copy-start.7) | copy-done | bytes 2228248
  59.3 6.8 %all-to-all-start.1 = ((f16[16,17,8,512]{3,2,1,0:T(8,128)(2,1)}), f16[16,17,8,512]{3,2,1,0:T(8,128)(2,1)}, u32[]{:S(2)}, u32[]{:S(2)}) async-start(f16[16,17,8,512]{3,2,1,0:T(8,128)(2,1)} %bitcast.34), calls=%async_computation.1 | async-start | bytes 4456448 | tf_op jit(solution)/shard_map/all_to_all | solution.py:240
  66.1 1.4 %collective-permute-done.10.refs_10_.refs_14_ = bf16[2,512,512]{2,1,0:T(8,128)(2,1)} collective-permute-done((bf16[2,512,512]{2,1,0:T(8,128)(2,1)S(1)}, bf16[2,512,512]{2,1,0:T(8,128)(2,1)}, u32[]{:S(2)}, u32[]{:S(2)}) %collective-permute-start.10) | collective-permute-done | bytes 1048608 | tf_op jit(solution)/shard_map/ppermute | solution.py:22
  67.5 1.1 slice_bitcast_fusion
  68.5 0.4 collective-permute-start.12
  68.9 2.7 %collective-permute-start.15 = (bf16[512,512]{1,0:T(8,128)(2,1)S(1)}, bf16[512,512]{1,0:T(8,128)(2,1)S(1)}, u32[]{:S(2)}, u32[]{:S(2)}) collective-permute-start(bf16[512,512]{1,0:T(8,128)(2,1)S(1)} %collective-permute-done.1.refs_0_.refs_8_.refs_4_), channel_id=1, source_target_pairs={{0,66},{2,64},{64,2},{66,0},{1,67},{3,65},{65,3},{67,1},{4,70},{6,... | collective-permute-start | bytes 1572872 | tf_op jit(solution)/shard_map/ppermute | solution.py:22
  71.7 8.9 %collective-permute-done.12.refs_8_ = bf16[512,512]{1,0:T(8,128)(2,1)S(1)} collective-permute-done((bf16[512,512]{1,0:T(8,128)(2,1)S(1)}, bf16[512,512]{1,0:T(8,128)(2,1)S(1)}, u32[]{:S(2)}, u32[]{:S(2)}) %collective-permute-start.12) | collective-permute-done | bytes 524320 | tf_op jit(solution)/shard_map/ppermute | solution.py:22
  80.6 1.3 collective-permute-done.15.refs_12_
  81.9 0.6 collective-permute-done.13.refs_9_
  82.5 1.3 collective-permute-done.16.refs_13_
  83.9 6.9 %shard_map.22 = f32[4,4,17,8,512]{4,3,2,1,0:T(8,128)S(1)} custom-call(s32[1]{0:T(128)} %bitcast.3.where, bf16[2,256,512]{2,1,0:T(8,128)(2,1)S(1)} %copy-done.5, bf16[2,256,512]{2,1,0:T(8,128)(2,1)S(1)} %copy-done.2, bf16[2,256,512]{2,1,0:T(8,128)(2,1)} %copy-done.8, bf16[2,256,512]{2,1,0:T(8,128)(2,1)} %collective-permute-done.5.refs_3_, ...), custom_call_target="tpu_custom_call" | custom-call | flops 4294967296 | bytes 8388608 | tf_op jit(solution)/shard_map/pallas_call | solution.py:146
  90.8 1.9 %convert_element_type.35 = f16[4,4,17,8,512]{4,3,2,1,0:T(8,128)(2,1)} convert(f32[4,4,17,8,512]{4,3,2,1,0:T(8,128)S(1)} %shard_map.22) | non-fusion elementwise | flops 1114112 | bytes 6684672 | tf_op jit(solution)/shard_map/convert_element_type | solution.py:239
  92.7 3.2 %all-to-all-done.1 = f16[16,17,8,512]{3,2,1,0:T(8,128)(2,1)} async-done(((f16[16,17,8,512]{3,2,1,0:T(8,128)(2,1)}), f16[16,17,8,512]{3,2,1,0:T(8,128)(2,1)}, u32[]{:S(2)}, u32[]{:S(2)}) %all-to-all-start.1) | async-done | bytes 2228256 | tf_op jit(solution)/shard_map/all_to_all | solution.py:240
  96.0 4.1 %all-to-all-start = ((f16[16,17,8,512]{3,2,1,0:T(8,128)(2,1)}), f16[16,17,8,512]{3,2,1,0:T(8,128)(2,1)S(1)}, u32[]{:S(2)}, u32[]{:S(2)}) async-start(f16[16,17,8,512]{3,2,1,0:T(8,128)(2,1)} %bitcast.7), calls=%async_computation | async-start | bytes 4456448 | tf_op jit(solution)/shard_map/all_to_all | solution.py:240
  100.2 1.0 divide_bitcast_fusion.1
  101.2 2.2 %multiply_reduce_fusion.1 = f32[4,16,8,512]{3,2,1,0:T(8,128)S(1)} fusion(f16[4,4,17,8,512]{4,3,2,1,0:T(8,128)(2,1)} %bitcast.10, f32[4,4,8,512]{3,2,1,0:T(8,128)S(1)} %divide_bitcast_fusion.1), kind=kLoop, calls=%fused_computation.1 | loop fusion | flops 2883584 | bytes 3407872 | tf_op jit(solution)/shard_map/reduce_sum | solution.py:243
  103.5 1.7 %shard_map.23.refs_4_ = f32[64,8192]{1,0:T(8,128)} custom-call(s32[7]{0:T(128)S(1)} %stack.37.where, f32[2,64,512]{2,1,0:T(8,128)S(1)} %bitcast.29, f32[2,64,512]{2,1,0:T(8,128)S(1)} %bitcast.28, f32[2,64,512]{2,1,0:T(8,128)S(1)} %bitcast.27, f32[2,64,512]{2,1,0:T(8,128)S(1)} %bitcast.26), custom_call_target="tpu_custom_call" | custom-call | tf_op jit(solution)/shard_map/pallas_call | solution.py:185
  105.3 26.2 %all-to-all-done = f16[16,17,8,512]{3,2,1,0:T(8,128)(2,1)S(1)} async-done(((f16[16,17,8,512]{3,2,1,0:T(8,128)(2,1)}), f16[16,17,8,512]{3,2,1,0:T(8,128)(2,1)S(1)}, u32[]{:S(2)}, u32[]{:S(2)}) %all-to-all-start) | async-done | bytes 2228256 | tf_op jit(solution)/shard_map/all_to_all | solution.py:240
  131.5 0.5 multiply_reduce_fusion
  132.0 1.7 %shard_map.24 = f32[64,8192]{1,0:T(8,128)} custom-call(s32[7]{0:T(128)S(1)} %stack.33.where, f32[2,64,512]{2,1,0:T(8,128)S(1)} %bitcast.33, f32[2,64,512]{2,1,0:T(8,128)S(1)} %bitcast.32, f32[2,64,512]{2,1,0:T(8,128)S(1)} %bitcast.31, f32[2,64,512]{2,1,0:T(8,128)S(1)} %bitcast.30, f32[64,8192]{1,0:T(8,128)} %shard_map.23.refs_4_), custom_call_target="tpu_custom_call", output_to_operand_aliasing={{}: (5, {})} | custom-call | tf_op jit(solution)/shard_map/pallas_call | solution.py:185
  (32 shorter events, 1.1 us)
Async XLA Ops:
  0.0 1.2 copy-start.6
  1.5 2.7 %collective-permute-start = (bf16[2,512,512]{2,1,0:T(8,128)(2,1)S(1)}, bf16[2,512,512]{2,1,0:T(8,128)(2,1)S(1)}, u32[]{:S(2)}, u32[]{:S(2)}) collective-permute-start(bf16[2,512,512]{2,1,0:T(8,128)(2,1)S(1)} %get-tuple-element.17.refs_0_.refs_6_.refs_10_.refs_2_), channel_id=1, source_target_pairs={{0,1},{1,0},{2,3},{3,2},{4,5},{5,4},{6,7},{7,6},{8,9},{9,8},{10,11... | collective-permute-start | bytes 3145736 | tf_op jit(solution)/shard_map/ppermute | solution.py:18
  1.6 14.3 %collective-permute-start.1 = (bf16[512,512]{1,0:T(8,128)(2,1)S(1)}, bf16[512,512]{1,0:T(8,128)(2,1)S(1)}, u32[]{:S(2)}, u32[]{:S(2)}) collective-permute-start(bf16[512,512]{1,0:T(8,128)(2,1)S(1)} %get-tuple-element.18), channel_id=1, source_target_pairs={{0,2},{2,0},{64,66},{66,64},{1,3},{3,1},{65,67},{67,65},{4,6},{6,4... | collective-permute-start | bytes 1572872 | tf_op jit(solution)/shard_map/ppermute | solution.py:22
  4.6 19.1 %copy-start.3 = (bf16[2,256,512]{2,1,0:T(8,128)(2,1)}, bf16[2,256,512]{2,1,0:T(8,128)(2,1)S(1)}, u32[]{:S(2)}) copy-start(bf16[2,256,512]{2,1,0:T(8,128)(2,1)S(1)} %shard_map.18.refs_0_) | copy-start | bytes 1572868
  4.6 15.4 %collective-permute-start.3 = (bf16[2,256,512]{2,1,0:T(8,128)(2,1)S(1)}, bf16[2,256,512]{2,1,0:T(8,128)(2,1)}, u32[]{:S(2)}, u32[]{:S(2)}) collective-permute-start(bf16[2,256,512]{2,1,0:T(8,128)(2,1)S(1)} %shard_map.18.refs_0_), channel_id=1, source_target_pairs={{0,48},{16,32},{32,16},{48,0},{1,49},{17,33},{33,17},{49,1},{2,50}... | collective-permute-start | bytes 1572872 | tf_op jit(solution)/shard_map/ppermute | solution.py:22
  7.5 13.7 %collective-permute-start.2 = (bf16[2,256,512]{2,1,0:T(8,128)(2,1)S(1)}, bf16[2,256,512]{2,1,0:T(8,128)(2,1)S(1)}, u32[]{:S(2)}, u32[]{:S(2)}) collective-permute-start(bf16[2,256,512]{2,1,0:T(8,128)(2,1)S(1)} %shard_map.18.refs_0_), channel_id=1, source_target_pairs={{0,16},{16,0},{32,48},{48,32},{1,17},{17,1},{33,49},{49,33},{2,18}... | collective-permute-start | bytes 1572872 | tf_op jit(solution)/shard_map/ppermute | solution.py:22
  21.2 0.8 copy-start.8
  22.0 1.9 %collective-permute-start.4 = (bf16[512,512]{1,0:T(8,128)(2,1)S(1)}, bf16[512,512]{1,0:T(8,128)(2,1)S(1)}, u32[]{:S(2)}, u32[]{:S(2)}) collective-permute-start(bf16[512,512]{1,0:T(8,128)(2,1)S(1)} %collective-permute-done.1.refs_0_.refs_8_.refs_4_), channel_id=1, source_target_pairs={{0,1},{1,0},{2,3},{3,2},{4,5},{5,4},{6,7},{7,6},{8,9},{9,8},{10,11... | collective-permute-start | bytes 1572872 | tf_op jit(solution)/shard_map/ppermute | solution.py:18
  22.0 14.5 %collective-permute-start.7 = (bf16[512,512]{1,0:T(8,128)(2,1)S(1)}, bf16[512,512]{1,0:T(8,128)(2,1)}, u32[]{:S(2)}, u32[]{:S(2)}) collective-permute-start(bf16[512,512]{1,0:T(8,128)(2,1)S(1)} %slice_bitcast_fusion.1), channel_id=1, source_target_pairs={{0,2},{2,0},{64,66},{66,64},{1,3},{3,1},{65,67},{67,65},{4,6},{6,4... | collective-permute-start | bytes 1572872 | tf_op jit(solution)/shard_map/ppermute | solution.py:22
  24.2 14.2 %collective-permute-start.5 = (bf16[2,256,512]{2,1,0:T(8,128)(2,1)S(1)}, bf16[2,256,512]{2,1,0:T(8,128)(2,1)}, u32[]{:S(2)}, u32[]{:S(2)}) collective-permute-start(bf16[2,256,512]{2,1,0:T(8,128)(2,1)S(1)} %shard_map.19.refs_1_), channel_id=1, source_target_pairs={{0,16},{16,0},{32,48},{48,32},{1,17},{17,1},{33,49},{49,33},{2,18}... | collective-permute-start | bytes 1572872 | tf_op jit(solution)/shard_map/ppermute | solution.py:22
  24.6 15.0 %collective-permute-start.6 = (bf16[2,256,512]{2,1,0:T(8,128)(2,1)S(1)}, bf16[2,256,512]{2,1,0:T(8,128)(2,1)S(1)}, u32[]{:S(2)}, u32[]{:S(2)}) collective-permute-start(bf16[2,256,512]{2,1,0:T(8,128)(2,1)S(1)} %shard_map.19.refs_1_), channel_id=1, source_target_pairs={{0,48},{16,32},{32,16},{48,0},{1,49},{17,33},{33,17},{49,1},{2,50}... | collective-permute-start | bytes 1572872 | tf_op jit(solution)/shard_map/ppermute | solution.py:22
  26.0 0.8 copy-start
  36.6 8.5 %collective-permute-start.11 = (bf16[512,512]{1,0:T(8,128)(2,1)}, bf16[512,512]{1,0:T(8,128)(2,1)}, u32[]{:S(2)}, u32[]{:S(2)}) collective-permute-start(bf16[512,512]{1,0:T(8,128)(2,1)} %collective-permute-done.7.refs_12_.refs_8_), channel_id=1, source_target_pairs={{0,1},{1,0},{2,3},{3,2},{4,5},{5,4},{6,7},{7,6},{8,9},{9,8},{10,11... | collective-permute-start | bytes 1572872 | tf_op jit(solution)/shard_map/ppermute | solution.py:18
  39.6 0.8 copy-start.9
  39.6 13.6 %collective-permute-start.8 = (bf16[2,256,512]{2,1,0:T(8,128)(2,1)}, bf16[2,256,512]{2,1,0:T(8,128)(2,1)}, u32[]{:S(2)}, u32[]{:S(2)}) collective-permute-start(bf16[2,256,512]{2,1,0:T(8,128)(2,1)} %collective-permute-done.3.refs_4_.refs_6_), channel_id=1, source_target_pairs={{0,16},{16,0},{32,48},{48,32},{1,17},{17,1},{33,49},{49,33},{2,18}... | collective-permute-start | bytes 1572872 | tf_op jit(solution)/shard_map/ppermute | solution.py:22
  40.4 14.4 %collective-permute-start.9 = (bf16[2,256,512]{2,1,0:T(8,128)(2,1)}, bf16[2,256,512]{2,1,0:T(8,128)(2,1)}, u32[]{:S(2)}, u32[]{:S(2)}) collective-permute-start(bf16[2,256,512]{2,1,0:T(8,128)(2,1)} %collective-permute-done.5.refs_3_), channel_id=1, source_target_pairs={{0,48},{16,32},{32,16},{48,0},{1,49},{17,33},{33,17},{49,1},{2,50}... | collective-permute-start | bytes 1572872 | tf_op jit(solution)/shard_map/ppermute | solution.py:22
  42.0 25.5 %collective-permute-start.10 = (bf16[2,512,512]{2,1,0:T(8,128)(2,1)S(1)}, bf16[2,512,512]{2,1,0:T(8,128)(2,1)}, u32[]{:S(2)}, u32[]{:S(2)}) collective-permute-start(bf16[2,512,512]{2,1,0:T(8,128)(2,1)S(1)} %get-tuple-element.17.refs_0_.refs_6_.refs_10_.refs_2_), channel_id=1, source_target_pairs={{0,66},{2,64},{64,2},{66,0},{1,67},{3,65},{65,3},{67,1},{4,70},{6,... | collective-permute-start | bytes 3145736 | tf_op jit(solution)/shard_map/ppermute | solution.py:22
  45.0 1.0 copy-start.1
  46.1 1.0 copy-start.4
  57.9 1.4 %copy-start.7 = (f16[4,4,17,8,512]{4,3,2,1,0:T(8,128)(2,1)}, f16[4,4,17,8,512]{4,3,2,1,0:T(8,128)(2,1)S(1)}, u32[]{:S(2)}) copy-start(f16[4,4,17,8,512]{4,3,2,1,0:T(8,128)(2,1)S(1)} %convert_dynamic-update-slice_fusion) | copy-start | bytes 6684676
  59.3 24.6 %copy-start.2 = (bf16[2,256,512]{2,1,0:T(8,128)(2,1)S(1)}, bf16[2,256,512]{2,1,0:T(8,128)(2,1)}, u32[]{:S(2)}) copy-start(bf16[2,256,512]{2,1,0:T(8,128)(2,1)} %copy-done) | copy-start | bytes 1572868
  59.3 24.6 %copy-start.5 = (bf16[2,256,512]{2,1,0:T(8,128)(2,1)S(1)}, bf16[2,256,512]{2,1,0:T(8,128)(2,1)}, u32[]{:S(2)}) copy-start(bf16[2,256,512]{2,1,0:T(8,128)(2,1)} %copy-done.3) | copy-start | bytes 1572868
  59.3 36.7 %all-to-all-start.1 = ((f16[16,17,8,512]{3,2,1,0:T(8,128)(2,1)}), f16[16,17,8,512]{3,2,1,0:T(8,128)(2,1)}, u32[]{:S(2)}, u32[]{:S(2)}) async-start(f16[16,17,8,512]{3,2,1,0:T(8,128)(2,1)} %bitcast.34), calls=%async_computation.1 | async-start | bytes 4456448 | tf_op jit(solution)/shard_map/all_to_all | solution.py:240
  68.5 12.1 %collective-permute-start.12 = (bf16[512,512]{1,0:T(8,128)(2,1)S(1)}, bf16[512,512]{1,0:T(8,128)(2,1)S(1)}, u32[]{:S(2)}, u32[]{:S(2)}) collective-permute-start(bf16[512,512]{1,0:T(8,128)(2,1)S(1)} %slice_bitcast_fusion), channel_id=1, source_target_pairs={{0,2},{2,0},{64,66},{66,64},{1,3},{3,1},{65,67},{67,65},{4,6},{6,4... | collective-permute-start | bytes 1572872 | tf_op jit(solution)/shard_map/ppermute | solution.py:22
  68.9 13.0 %collective-permute-start.15 = (bf16[512,512]{1,0:T(8,128)(2,1)S(1)}, bf16[512,512]{1,0:T(8,128)(2,1)S(1)}, u32[]{:S(2)}, u32[]{:S(2)}) collective-permute-start(bf16[512,512]{1,0:T(8,128)(2,1)S(1)} %collective-permute-done.1.refs_0_.refs_8_.refs_4_), channel_id=1, source_target_pairs={{0,66},{2,64},{64,2},{66,0},{1,67},{3,65},{65,3},{67,1},{4,70},{6,... | collective-permute-start | bytes 1572872 | tf_op jit(solution)/shard_map/ppermute | solution.py:22
  71.7 12.2 %collective-permute-start.14 = (bf16[2,512,512]{2,1,0:T(8,128)(2,1)}, bf16[2,512,512]{2,1,0:T(8,128)(2,1)S(1)}, u32[]{:S(2)}, u32[]{:S(2)}) collective-permute-start(bf16[2,512,512]{2,1,0:T(8,128)(2,1)} %collective-permute-done.10.refs_10_.refs_14_), channel_id=1, source_target_pairs={{0,1},{1,0},{2,3},{3,2},{4,5},{5,4},{6,7},{7,6},{8,9},{9,8},{10,11... | collective-permute-start | bytes 3145736 | tf_op jit(solution)/shard_map/ppermute | solution.py:18
  80.6 1.9 %collective-permute-start.13 = (bf16[512,512]{1,0:T(8,128)(2,1)S(1)}, bf16[512,512]{1,0:T(8,128)(2,1)S(1)}, u32[]{:S(2)}, u32[]{:S(2)}) collective-permute-start(bf16[512,512]{1,0:T(8,128)(2,1)S(1)} %collective-permute-done.12.refs_8_), channel_id=1, source_target_pairs={{0,1},{1,0},{2,3},{3,2},{4,5},{5,4},{6,7},{7,6},{8,9},{9,8},{10,11... | collective-permute-start | bytes 1572872 | tf_op jit(solution)/shard_map/ppermute | solution.py:18
  81.9 1.9 %collective-permute-start.16 = (bf16[512,512]{1,0:T(8,128)(2,1)S(1)}, bf16[512,512]{1,0:T(8,128)(2,1)S(1)}, u32[]{:S(2)}, u32[]{:S(2)}) collective-permute-start(bf16[512,512]{1,0:T(8,128)(2,1)S(1)} %collective-permute-done.15.refs_12_), channel_id=1, source_target_pairs={{0,1},{1,0},{2,3},{3,2},{4,5},{5,4},{6,7},{7,6},{8,9},{9,8},{10,11... | collective-permute-start | bytes 1572872 | tf_op jit(solution)/shard_map/ppermute | solution.py:18
  96.0 35.5 %all-to-all-start = ((f16[16,17,8,512]{3,2,1,0:T(8,128)(2,1)}), f16[16,17,8,512]{3,2,1,0:T(8,128)(2,1)S(1)}, u32[]{:S(2)}, u32[]{:S(2)}) async-start(f16[16,17,8,512]{3,2,1,0:T(8,128)(2,1)} %bitcast.7), calls=%async_computation | async-start | bytes 4456448 | tf_op jit(solution)/shard_map/all_to_all | solution.py:240

commit v5 on v4

--- a/solution.py
+++ b/solution.py
@@ -163,6 +163,7 @@
 
 
 def place(sums, where, result=None):
+    own = result is None
     _, rows, half = sums[0].shape
     width = 2 * half
     given = [] if result is None else [result]
@@ -171,23 +172,25 @@
         out = refs[-1]
         for i in range(4):
             block = where[3 + i]
-            row_ids = where[1] + lax.broadcasted_iota(jnp.int32, (rows, width), 0)
-            col_ids = (where[0] * 4 + block) * width + lax.broadcasted_iota(jnp.int32, (rows, width), 1)
-            damp = jnp.where(row_ids == col_ids, jnp.float32(damping), jnp.float32(0.0))
+            if own:
+                row_ids = where[1] + lax.broadcasted_iota(jnp.int32, (rows, width), 0)
+                col_ids = (where[0] * 4 + block) * width + lax.broadcasted_iota(jnp.int32, (rows, width), 1)
+                damp = jnp.where(row_ids == col_ids, jnp.float32(damping), jnp.float32(0.0))
             for slab in range(4):
                 here = slice(slab * lane, (slab + 1) * lane)
                 mine, theirs = refs[i][0, :, here], refs[i][1, :, here]
                 for other in range(2):
                     at = (2 * slab + other) * lane
                     there = pl.ds(pl.multiple_of(block * width + at, lane), lane)
-                    out[:, there] = jnp.where(where[2] == other, mine, theirs) + damp[:, at : at + lane]
+                    value = jnp.where(where[2] == other, mine, theirs)
+                    out[:, there] = value + damp[:, at : at + lane] if own else value
 
     return pl.pallas_call(
         kernel,
         grid_spec=pltpu.PrefetchScalarGridSpec(
             num_scalar_prefetch=1,
             grid=(1,),
-            in_specs=[pl.BlockSpec(v.shape, lambda i, where: (0, 0, 0)) for v in sums]
+            in_specs=[vmem] * len(sums)
             + [pl.BlockSpec(memory_space=pl.ANY)] * len(given),
             out_specs=pl.BlockSpec((rows, 4 * width), lambda i, where: (0, where[0])),
         ),

time: 134 us -> 134 us (level)
  no operation moved by 1% of the time
where the time goes in v5:
time: 134 us
  waiting for transfers between devices  72 us (54%)
  starting transfers between devices  27.5 us (21%)
  Pallas kernels  19.6 us (15%)
  local copies, waits for them, and re-layouts  8.1 us (6%)
  other arithmetic  6.31 us (5%)
    ppermute x11, waiting for transfers between devices, trade(): return lax.ppermute(value, axis, [(i, i ^ bits) for i in range(4)])  39.5 us
    all_to_all x2, waiting for transfers between devices, per_device(): across = lax.all_to_all(packed, ('x', 'z'), 0, 0, tiled=True)  29.4 us
    ppermute x11, starting transfers between devices, trade(): return lax.ppermute(value, axis, [(i, i ^ bits) for i in range(4)])  16.5 us
    pallas_call x3, Pallas kernels, product(): pl.pallas_call(kernel, grid_spec=pltpu.PrefetchScalarGridSpec(num_scalar_...  15.3 us
    all_to_all x2, starting transfers between devices, per_device(): across = lax.all_to_all(packed, ('x', 'z'), 0, 0, tiled=True)  10.9 us
    unnamed x20, local copies, waits for them, and re-layouts  6.68 us
    pallas_call x2, Pallas kernels, place(): pl.pallas_call(kernel, grid_spec=pltpu.PrefetchScalarGridSpec(num_scalar_...  3.33 us
    ppermute x6, waiting for transfers between devices, swap(): return lax.ppermute(value, 'core', [(0, 1), (1, 0)])  3.02 us
  transfers between devices with their start and end apart: 19, of which 16 were waited for; matrix products, arithmetic and copies ran while one was open for 5% of the time, Pallas kernels for 13%

profile of v5, /device:TPU:0, one launch (start us, length us, event | category | flops | bytes accessed | tf_op | source)
XLA Modules:
  0.0 133.6 jit_solution(1249981026152380732)
XLA Ops:
  0.0 1.2 copy-done.6
  1.2 0.3 shard_map.17
  1.6 1.7 %collective-permute-start.1 = (bf16[512,512]{1,0:T(8,128)(2,1)S(1)}, bf16[512,512]{1,0:T(8,128)(2,1)S(1)}, u32[]{:S(2)}, u32[]{:S(2)}) collective-permute-start(bf16[512,512]{1,0:T(8,128)(2,1)S(1)} %get-tuple-element.18), channel_id=1, source_target_pairs={{0,2},{2,0},{64,66},{66,64},{1,3},{3,1},{65,67},{67,65},{4,6},{6,4... | collective-permute-start | bytes 1572872 | tf_op jit(solution)/shard_map/ppermute | solution.py:22
  3.3 0.9 collective-permute-done.refs_1_.refs_7_.refs_11_.refs_3_
  4.2 0.3 shard_map.18.refs_0_
  4.6 2.9 %collective-permute-start.3 = (bf16[2,256,512]{2,1,0:T(8,128)(2,1)S(1)}, bf16[2,256,512]{2,1,0:T(8,128)(2,1)}, u32[]{:S(2)}, u32[]{:S(2)}) collective-permute-start(bf16[2,256,512]{2,1,0:T(8,128)(2,1)S(1)} %shard_map.18.refs_0_), channel_id=1, source_target_pairs={{0,48},{16,32},{32,16},{48,0},{1,49},{17,33},{33,17},{49,1},{2,50}... | collective-permute-start | bytes 1572872 | tf_op jit(solution)/shard_map/ppermute | solution.py:22
  7.7 8.2 %collective-permute-done.1.refs_0_.refs_8_.refs_4_ = bf16[512,512]{1,0:T(8,128)(2,1)S(1)} collective-permute-done((bf16[512,512]{1,0:T(8,128)(2,1)S(1)}, bf16[512,512]{1,0:T(8,128)(2,1)S(1)}, u32[]{:S(2)}, u32[]{:S(2)}) %collective-permute-start.1) | collective-permute-done | bytes 524320 | tf_op jit(solution)/shard_map/ppermute | solution.py:22
  15.9 4.0 %collective-permute-done.3.refs_4_.refs_6_ = bf16[2,256,512]{2,1,0:T(8,128)(2,1)} collective-permute-done((bf16[2,256,512]{2,1,0:T(8,128)(2,1)S(1)}, bf16[2,256,512]{2,1,0:T(8,128)(2,1)}, u32[]{:S(2)}, u32[]{:S(2)}) %collective-permute-start.3) | collective-permute-done | bytes 524320 | tf_op jit(solution)/shard_map/ppermute | solution.py:22
  19.9 1.2 collective-permute-done.2.refs_2_
  21.2 0.8 copy-done.8
  22.0 1.7 %collective-permute-start.7 = (bf16[512,512]{1,0:T(8,128)(2,1)S(1)}, bf16[512,512]{1,0:T(8,128)(2,1)}, u32[]{:S(2)}, u32[]{:S(2)}) collective-permute-start(bf16[512,512]{1,0:T(8,128)(2,1)S(1)} %slice_bitcast_fusion.1), channel_id=1, source_target_pairs={{0,2},{2,0},{64,66},{66,64},{1,3},{3,1},{65,67},{67,65},{4,6},{6,4... | collective-permute-start | bytes 1572872 | tf_op jit(solution)/shard_map/ppermute | solution.py:22
  23.9 0.3 shard_map.19.refs_1_
  24.2 0.4 collective-permute-start.5
  24.6 1.4 %collective-permute-start.6 = (bf16[2,256,512]{2,1,0:T(8,128)(2,1)S(1)}, bf16[2,256,512]{2,1,0:T(8,128)(2,1)S(1)}, u32[]{:S(2)}, u32[]{:S(2)}) collective-permute-start(bf16[2,256,512]{2,1,0:T(8,128)(2,1)S(1)} %shard_map.19.refs_1_), channel_id=1, source_target_pairs={{0,48},{16,32},{32,16},{48,0},{1,49},{17,33},{33,17},{49,1},{2,50}... | collective-permute-start | bytes 1572872 | tf_op jit(solution)/shard_map/ppermute | solution.py:22
  26.0 0.8 copy-done
  26.8 9.7 %collective-permute-done.7.refs_12_.refs_8_ = bf16[512,512]{1,0:T(8,128)(2,1)} collective-permute-done((bf16[512,512]{1,0:T(8,128)(2,1)S(1)}, bf16[512,512]{1,0:T(8,128)(2,1)}, u32[]{:S(2)}, u32[]{:S(2)}) %collective-permute-start.7) | collective-permute-done | bytes 524320 | tf_op jit(solution)/shard_map/ppermute | solution.py:22
  36.6 1.8 %collective-permute-done.5.refs_3_ = bf16[2,256,512]{2,1,0:T(8,128)(2,1)} collective-permute-done((bf16[2,256,512]{2,1,0:T(8,128)(2,1)S(1)}, bf16[2,256,512]{2,1,0:T(8,128)(2,1)}, u32[]{:S(2)}, u32[]{:S(2)}) %collective-permute-start.5) | collective-permute-done | bytes 524320 | tf_op jit(solution)/shard_map/ppermute | solution.py:22
  38.4 1.2 collective-permute-done.6.refs_5_.refs_7_
  39.6 0.4 collective-permute-start.8
  40.0 0.4 copy-done.9
  40.4 1.6 %collective-permute-start.9 = (bf16[2,256,512]{2,1,0:T(8,128)(2,1)}, bf16[2,256,512]{2,1,0:T(8,128)(2,1)}, u32[]{:S(2)}, u32[]{:S(2)}) collective-permute-start(bf16[2,256,512]{2,1,0:T(8,128)(2,1)} %collective-permute-done.5.refs_3_), channel_id=1, source_target_pairs={{0,48},{16,32},{32,16},{48,0},{1,49},{17,33},{33,17},{49,1},{2,50}... | collective-permute-start | bytes 1572872 | tf_op jit(solution)/shard_map/ppermute | solution.py:22
  42.0 3.0 %collective-permute-start.10 = (bf16[2,512,512]{2,1,0:T(8,128)(2,1)S(1)}, bf16[2,512,512]{2,1,0:T(8,128)(2,1)}, u32[]{:S(2)}, u32[]{:S(2)}) collective-permute-start(bf16[2,512,512]{2,1,0:T(8,128)(2,1)S(1)} %get-tuple-element.17.refs_0_.refs_6_.refs_10_.refs_2_), channel_id=1, source_target_pairs={{0,66},{2,64},{64,2},{66,0},{1,67},{3,65},{65,3},{67,1},{4,70},{6,... | collective-permute-start | bytes 3145736 | tf_op jit(solution)/shard_map/ppermute | solution.py:22
  45.0 1.0 copy-done.1
  46.1 1.0 copy-done.4
  47.1 5.5 %shard_map.20 = f32[4,4,17,8,512]{4,3,2,1,0:T(8,128)S(1)} custom-call(s32[1]{0:T(128)} %bitcast.3.where, bf16[2,256,512]{2,1,0:T(8,128)(2,1)S(1)} %copy-done.4, bf16[2,256,512]{2,1,0:T(8,128)(2,1)S(1)} %copy-done.1, bf16[2,256,512]{2,1,0:T(8,128)(2,1)} %copy-done.8, bf16[2,256,512]{2,1,0:T(8,128)(2,1)} %collective-permute-done.5.refs_3_, ...), custom_call_target="tpu_custom_call" | custom-call | flops 3221225472 | bytes 8388608 | tf_op jit(solution)/shard_map/pallas_call | solution.py:146
  52.6 0.5 convert_element_type.33
  53.2 1.7 %collective-permute-done.9.refs_1_.refs_5_ = bf16[2,256,512]{2,1,0:T(8,128)(2,1)} collective-permute-done((bf16[2,256,512]{2,1,0:T(8,128)(2,1)}, bf16[2,256,512]{2,1,0:T(8,128)(2,1)}, u32[]{:S(2)}, u32[]{:S(2)}) %collective-permute-start.9) | collective-permute-done | bytes 524320 | tf_op jit(solution)/shard_map/ppermute | solution.py:22
  54.8 2.9 %shard_map.21 = f32[1,4,17,8,512]{4,3,2,1,0:T(8,128)S(1)} custom-call(s32[1]{0:T(128)} %bitcast.3.where, bf16[2,256,512]{2,1,0:T(8,128)(2,1)} %collective-permute-done.8.refs_0_.refs_4_, bf16[2,256,512]{2,1,0:T(8,128)(2,1)} %collective-permute-done.9.refs_1_.refs_5_, bf16[2,512,512]{2,1,0:T(8,128)(2,1)S(1)} %get-tuple-element.17.refs_0_.refs_6_.refs_10_.refs_2_, ...), custom_call_target="tpu_custom_call" | custom-call | flops 1073741824 | bytes 8388608 | tf_op jit(solution)/shard_map/pallas_call | solution.py:146
  57.9 1.4 %copy-done.7 = f16[4,4,17,8,512]{4,3,2,1,0:T(8,128)(2,1)} copy-done((f16[4,4,17,8,512]{4,3,2,1,0:T(8,128)(2,1)}, f16[4,4,17,8,512]{4,3,2,1,0:T(8,128)(2,1)S(1)}, u32[]{:S(2)}) %copy-start.7) | copy-done | bytes 2228248
  59.3 6.8 %all-to-all-start.1 = ((f16[16,17,8,512]{3,2,1,0:T(8,128)(2,1)}), f16[16,17,8,512]{3,2,1,0:T(8,128)(2,1)}, u32[]{:S(2)}, u32[]{:S(2)}) async-start(f16[16,17,8,512]{3,2,1,0:T(8,128)(2,1)} %bitcast.34), calls=%async_computation.1 | async-start | bytes 4456448 | tf_op jit(solution)/shard_map/all_to_all | solution.py:243
  66.1 1.4 %collective-permute-done.10.refs_10_.refs_14_ = bf16[2,512,512]{2,1,0:T(8,128)(2,1)} collective-permute-done((bf16[2,512,512]{2,1,0:T(8,128)(2,1)S(1)}, bf16[2,512,512]{2,1,0:T(8,128)(2,1)}, u32[]{:S(2)}, u32[]{:S(2)}) %collective-permute-start.10) | collective-permute-done | bytes 1048608 | tf_op jit(solution)/shard_map/ppermute | solution.py:22
  67.5 1.1 slice_bitcast_fusion
  68.5 0.4 collective-permute-start.12
  68.9 2.7 %collective-permute-start.15 = (bf16[512,512]{1,0:T(8,128)(2,1)S(1)}, bf16[512,512]{1,0:T(8,128)(2,1)S(1)}, u32[]{:S(2)}, u32[]{:S(2)}) collective-permute-start(bf16[512,512]{1,0:T(8,128)(2,1)S(1)} %collective-permute-done.1.refs_0_.refs_8_.refs_4_), channel_id=1, source_target_pairs={{0,66},{2,64},{64,2},{66,0},{1,67},{3,65},{65,3},{67,1},{4,70},{6,... | collective-permute-start | bytes 1572872 | tf_op jit(solution)/shard_map/ppermute | solution.py:22
  71.7 8.9 %collective-permute-done.12.refs_8_ = bf16[512,512]{1,0:T(8,128)(2,1)S(1)} collective-permute-done((bf16[512,512]{1,0:T(8,128)(2,1)S(1)}, bf16[512,512]{1,0:T(8,128)(2,1)S(1)}, u32[]{:S(2)}, u32[]{:S(2)}) %collective-permute-start.12) | collective-permute-done | bytes 524320 | tf_op jit(solution)/shard_map/ppermute | solution.py:22
  80.6 1.3 collective-permute-done.15.refs_12_
  81.9 0.6 collective-permute-done.13.refs_9_
  82.5 1.3 collective-permute-done.16.refs_13_
  83.9 6.9 %shard_map.22 = f32[4,4,17,8,512]{4,3,2,1,0:T(8,128)S(1)} custom-call(s32[1]{0:T(128)} %bitcast.3.where, bf16[2,256,512]{2,1,0:T(8,128)(2,1)S(1)} %copy-done.5, bf16[2,256,512]{2,1,0:T(8,128)(2,1)S(1)} %copy-done.2, bf16[2,256,512]{2,1,0:T(8,128)(2,1)} %copy-done.8, bf16[2,256,512]{2,1,0:T(8,128)(2,1)} %collective-permute-done.5.refs_3_, ...), custom_call_target="tpu_custom_call" | custom-call | flops 4294967296 | bytes 8388608 | tf_op jit(solution)/shard_map/pallas_call | solution.py:146
  90.8 1.9 %convert_element_type.35 = f16[4,4,17,8,512]{4,3,2,1,0:T(8,128)(2,1)} convert(f32[4,4,17,8,512]{4,3,2,1,0:T(8,128)S(1)} %shard_map.22) | non-fusion elementwise | flops 1114112 | bytes 6684672 | tf_op jit(solution)/shard_map/convert_element_type | solution.py:242
  92.7 3.2 %all-to-all-done.1 = f16[16,17,8,512]{3,2,1,0:T(8,128)(2,1)} async-done(((f16[16,17,8,512]{3,2,1,0:T(8,128)(2,1)}), f16[16,17,8,512]{3,2,1,0:T(8,128)(2,1)}, u32[]{:S(2)}, u32[]{:S(2)}) %all-to-all-start.1) | async-done | bytes 2228256 | tf_op jit(solution)/shard_map/all_to_all | solution.py:243
  96.0 4.1 %all-to-all-start = ((f16[16,17,8,512]{3,2,1,0:T(8,128)(2,1)}), f16[16,17,8,512]{3,2,1,0:T(8,128)(2,1)S(1)}, u32[]{:S(2)}, u32[]{:S(2)}) async-start(f16[16,17,8,512]{3,2,1,0:T(8,128)(2,1)} %bitcast.7), calls=%async_computation | async-start | bytes 4456448 | tf_op jit(solution)/shard_map/all_to_all | solution.py:243
  100.2 1.0 divide_bitcast_fusion.1
  101.2 2.2 %multiply_reduce_fusion.1 = f32[4,16,8,512]{3,2,1,0:T(8,128)S(1)} fusion(f16[4,4,17,8,512]{4,3,2,1,0:T(8,128)(2,1)} %bitcast.10, f32[4,4,8,512]{3,2,1,0:T(8,128)S(1)} %divide_bitcast_fusion.1), kind=kLoop, calls=%fused_computation.1 | loop fusion | flops 2883584 | bytes 3407872 | tf_op jit(solution)/shard_map/reduce_sum | solution.py:246
  103.5 1.7 %shard_map.23.refs_4_ = f32[64,8192]{1,0:T(8,128)} custom-call(s32[7]{0:T(128)S(1)} %stack.37.where, f32[2,64,512]{2,1,0:T(8,128)S(1)} %bitcast.29, f32[2,64,512]{2,1,0:T(8,128)S(1)} %bitcast.28, f32[2,64,512]{2,1,0:T(8,128)S(1)} %bitcast.27, f32[2,64,512]{2,1,0:T(8,128)S(1)} %bitcast.26), custom_call_target="tpu_custom_call" | custom-call | tf_op jit(solution)/shard_map/pallas_call | solution.py:188
  105.3 26.2 %all-to-all-done = f16[16,17,8,512]{3,2,1,0:T(8,128)(2,1)S(1)} async-done(((f16[16,17,8,512]{3,2,1,0:T(8,128)(2,1)}), f16[16,17,8,512]{3,2,1,0:T(8,128)(2,1)S(1)}, u32[]{:S(2)}, u32[]{:S(2)}) %all-to-all-start) | async-done | bytes 2228256 | tf_op jit(solution)/shard_map/all_to_all | solution.py:243
  131.5 0.5 multiply_reduce_fusion
  132.0 1.6 %shard_map.24 = f32[64,8192]{1,0:T(8,128)} custom-call(s32[7]{0:T(128)S(1)} %stack.33.where, f32[2,64,512]{2,1,0:T(8,128)S(1)} %bitcast.33, f32[2,64,512]{2,1,0:T(8,128)S(1)} %bitcast.32, f32[2,64,512]{2,1,0:T(8,128)S(1)} %bitcast.31, f32[2,64,512]{2,1,0:T(8,128)S(1)} %bitcast.30, f32[64,8192]{1,0:T(8,128)} %shard_map.23.refs_4_), custom_call_target="tpu_custom_call", output_to_operand_aliasing={{}: (5, {})} | custom-call | tf_op jit(solution)/shard_map/pallas_call | solution.py:188
  (32 shorter events, 1.1 us)
Async XLA Ops:
  0.0 1.2 copy-start.6
  1.5 2.7 %collective-permute-start = (bf16[2,512,512]{2,1,0:T(8,128)(2,1)S(1)}, bf16[2,512,512]{2,1,0:T(8,128)(2,1)S(1)}, u32[]{:S(2)}, u32[]{:S(2)}) collective-permute-start(bf16[2,512,512]{2,1,0:T(8,128)(2,1)S(1)} %get-tuple-element.17.refs_0_.refs_6_.refs_10_.refs_2_), channel_id=1, source_target_pairs={{0,1},{1,0},{2,3},{3,2},{4,5},{5,4},{6,7},{7,6},{8,9},{9,8},{10,11... | collective-permute-start | bytes 3145736 | tf_op jit(solution)/shard_map/ppermute | solution.py:18
  1.6 14.3 %collective-permute-start.1 = (bf16[512,512]{1,0:T(8,128)(2,1)S(1)}, bf16[512,512]{1,0:T(8,128)(2,1)S(1)}, u32[]{:S(2)}, u32[]{:S(2)}) collective-permute-start(bf16[512,512]{1,0:T(8,128)(2,1)S(1)} %get-tuple-element.18), channel_id=1, source_target_pairs={{0,2},{2,0},{64,66},{66,64},{1,3},{3,1},{65,67},{67,65},{4,6},{6,4... | collective-permute-start | bytes 1572872 | tf_op jit(solution)/shard_map/ppermute | solution.py:22
  4.6 19.1 %copy-start.3 = (bf16[2,256,512]{2,1,0:T(8,128)(2,1)}, bf16[2,256,512]{2,1,0:T(8,128)(2,1)S(1)}, u32[]{:S(2)}) copy-start(bf16[2,256,512]{2,1,0:T(8,128)(2,1)S(1)} %shard_map.18.refs_0_) | copy-start | bytes 1572868
  4.6 15.4 %collective-permute-start.3 = (bf16[2,256,512]{2,1,0:T(8,128)(2,1)S(1)}, bf16[2,256,512]{2,1,0:T(8,128)(2,1)}, u32[]{:S(2)}, u32[]{:S(2)}) collective-permute-start(bf16[2,256,512]{2,1,0:T(8,128)(2,1)S(1)} %shard_map.18.refs_0_), channel_id=1, source_target_pairs={{0,48},{16,32},{32,16},{48,0},{1,49},{17,33},{33,17},{49,1},{2,50}... | collective-permute-start | bytes 1572872 | tf_op jit(solution)/shard_map/ppermute | solution.py:22
  7.5 13.7 %collective-permute-start.2 = (bf16[2,256,512]{2,1,0:T(8,128)(2,1)S(1)}, bf16[2,256,512]{2,1,0:T(8,128)(2,1)S(1)}, u32[]{:S(2)}, u32[]{:S(2)}) collective-permute-start(bf16[2,256,512]{2,1,0:T(8,128)(2,1)S(1)} %shard_map.18.refs_0_), channel_id=1, source_target_pairs={{0,16},{16,0},{32,48},{48,32},{1,17},{17,1},{33,49},{49,33},{2,18}... | collective-permute-start | bytes 1572872 | tf_op jit(solution)/shard_map/ppermute | solution.py:22
  21.2 0.8 copy-start.8
  22.0 1.9 %collective-permute-start.4 = (bf16[512,512]{1,0:T(8,128)(2,1)S(1)}, bf16[512,512]{1,0:T(8,128)(2,1)S(1)}, u32[]{:S(2)}, u32[]{:S(2)}) collective-permute-start(bf16[512,512]{1,0:T(8,128)(2,1)S(1)} %collective-permute-done.1.refs_0_.refs_8_.refs_4_), channel_id=1, source_target_pairs={{0,1},{1,0},{2,3},{3,2},{4,5},{5,4},{6,7},{7,6},{8,9},{9,8},{10,11... | collective-permute-start | bytes 1572872 | tf_op jit(solution)/shard_map/ppermute | solution.py:18
  22.0 14.5 %collective-permute-start.7 = (bf16[512,512]{1,0:T(8,128)(2,1)S(1)}, bf16[512,512]{1,0:T(8,128)(2,1)}, u32[]{:S(2)}, u32[]{:S(2)}) collective-permute-start(bf16[512,512]{1,0:T(8,128)(2,1)S(1)} %slice_bitcast_fusion.1), channel_id=1, source_target_pairs={{0,2},{2,0},{64,66},{66,64},{1,3},{3,1},{65,67},{67,65},{4,6},{6,4... | collective-permute-start | bytes 1572872 | tf_op jit(solution)/shard_map/ppermute | solution.py:22
  24.2 14.2 %collective-permute-start.5 = (bf16[2,256,512]{2,1,0:T(8,128)(2,1)S(1)}, bf16[2,256,512]{2,1,0:T(8,128)(2,1)}, u32[]{:S(2)}, u32[]{:S(2)}) collective-permute-start(bf16[2,256,512]{2,1,0:T(8,128)(2,1)S(1)} %shard_map.19.refs_1_), channel_id=1, source_target_pairs={{0,16},{16,0},{32,48},{48,32},{1,17},{17,1},{33,49},{49,33},{2,18}... | collective-permute-start | bytes 1572872 | tf_op jit(solution)/shard_map/ppermute | solution.py:22
  24.6 15.0 %collective-permute-start.6 = (bf16[2,256,512]{2,1,0:T(8,128)(2,1)S(1)}, bf16[2,256,512]{2,1,0:T(8,128)(2,1)S(1)}, u32[]{:S(2)}, u32[]{:S(2)}) collective-permute-start(bf16[2,256,512]{2,1,0:T(8,128)(2,1)S(1)} %shard_map.19.refs_1_), channel_id=1, source_target_pairs={{0,48},{16,32},{32,16},{48,0},{1,49},{17,33},{33,17},{49,1},{2,50}... | collective-permute-start | bytes 1572872 | tf_op jit(solution)/shard_map/ppermute | solution.py:22
  26.0 0.8 copy-start
  36.6 8.5 %collective-permute-start.11 = (bf16[512,512]{1,0:T(8,128)(2,1)}, bf16[512,512]{1,0:T(8,128)(2,1)}, u32[]{:S(2)}, u32[]{:S(2)}) collective-permute-start(bf16[512,512]{1,0:T(8,128)(2,1)} %collective-permute-done.7.refs_12_.refs_8_), channel_id=1, source_target_pairs={{0,1},{1,0},{2,3},{3,2},{4,5},{5,4},{6,7},{7,6},{8,9},{9,8},{10,11... | collective-permute-start | bytes 1572872 | tf_op jit(solution)/shard_map/ppermute | solution.py:18
  39.6 0.8 copy-start.9
  39.6 13.6 %collective-permute-start.8 = (bf16[2,256,512]{2,1,0:T(8,128)(2,1)}, bf16[2,256,512]{2,1,0:T(8,128)(2,1)}, u32[]{:S(2)}, u32[]{:S(2)}) collective-permute-start(bf16[2,256,512]{2,1,0:T(8,128)(2,1)} %collective-permute-done.3.refs_4_.refs_6_), channel_id=1, source_target_pairs={{0,16},{16,0},{32,48},{48,32},{1,17},{17,1},{33,49},{49,33},{2,18}... | collective-permute-start | bytes 1572872 | tf_op jit(solution)/shard_map/ppermute | solution.py:22
  40.4 14.4 %collective-permute-start.9 = (bf16[2,256,512]{2,1,0:T(8,128)(2,1)}, bf16[2,256,512]{2,1,0:T(8,128)(2,1)}, u32[]{:S(2)}, u32[]{:S(2)}) collective-permute-start(bf16[2,256,512]{2,1,0:T(8,128)(2,1)} %collective-permute-done.5.refs_3_), channel_id=1, source_target_pairs={{0,48},{16,32},{32,16},{48,0},{1,49},{17,33},{33,17},{49,1},{2,50}... | collective-permute-start | bytes 1572872 | tf_op jit(solution)/shard_map/ppermute | solution.py:22
  42.0 25.5 %collective-permute-start.10 = (bf16[2,512,512]{2,1,0:T(8,128)(2,1)S(1)}, bf16[2,512,512]{2,1,0:T(8,128)(2,1)}, u32[]{:S(2)}, u32[]{:S(2)}) collective-permute-start(bf16[2,512,512]{2,1,0:T(8,128)(2,1)S(1)} %get-tuple-element.17.refs_0_.refs_6_.refs_10_.refs_2_), channel_id=1, source_target_pairs={{0,66},{2,64},{64,2},{66,0},{1,67},{3,65},{65,3},{67,1},{4,70},{6,... | collective-permute-start | bytes 3145736 | tf_op jit(solution)/shard_map/ppermute | solution.py:22
  45.0 1.0 copy-start.1
  46.1 1.0 copy-start.4
  57.9 1.4 %copy-start.7 = (f16[4,4,17,8,512]{4,3,2,1,0:T(8,128)(2,1)}, f16[4,4,17,8,512]{4,3,2,1,0:T(8,128)(2,1)S(1)}, u32[]{:S(2)}) copy-start(f16[4,4,17,8,512]{4,3,2,1,0:T(8,128)(2,1)S(1)} %convert_dynamic-update-slice_fusion) | copy-start | bytes 6684676
  59.3 24.6 %copy-start.2 = (bf16[2,256,512]{2,1,0:T(8,128)(2,1)S(1)}, bf16[2,256,512]{2,1,0:T(8,128)(2,1)}, u32[]{:S(2)}) copy-start(bf16[2,256,512]{2,1,0:T(8,128)(2,1)} %copy-done) | copy-start | bytes 1572868
  59.3 24.6 %copy-start.5 = (bf16[2,256,512]{2,1,0:T(8,128)(2,1)S(1)}, bf16[2,256,512]{2,1,0:T(8,128)(2,1)}, u32[]{:S(2)}) copy-start(bf16[2,256,512]{2,1,0:T(8,128)(2,1)} %copy-done.3) | copy-start | bytes 1572868
  59.3 36.7 %all-to-all-start.1 = ((f16[16,17,8,512]{3,2,1,0:T(8,128)(2,1)}), f16[16,17,8,512]{3,2,1,0:T(8,128)(2,1)}, u32[]{:S(2)}, u32[]{:S(2)}) async-start(f16[16,17,8,512]{3,2,1,0:T(8,128)(2,1)} %bitcast.34), calls=%async_computation.1 | async-start | bytes 4456448 | tf_op jit(solution)/shard_map/all_to_all | solution.py:243
  68.5 12.1 %collective-permute-start.12 = (bf16[512,512]{1,0:T(8,128)(2,1)S(1)}, bf16[512,512]{1,0:T(8,128)(2,1)S(1)}, u32[]{:S(2)}, u32[]{:S(2)}) collective-permute-start(bf16[512,512]{1,0:T(8,128)(2,1)S(1)} %slice_bitcast_fusion), channel_id=1, source_target_pairs={{0,2},{2,0},{64,66},{66,64},{1,3},{3,1},{65,67},{67,65},{4,6},{6,4... | collective-permute-start | bytes 1572872 | tf_op jit(solution)/shard_map/ppermute | solution.py:22
  68.9 13.0 %collective-permute-start.15 = (bf16[512,512]{1,0:T(8,128)(2,1)S(1)}, bf16[512,512]{1,0:T(8,128)(2,1)S(1)}, u32[]{:S(2)}, u32[]{:S(2)}) collective-permute-start(bf16[512,512]{1,0:T(8,128)(2,1)S(1)} %collective-permute-done.1.refs_0_.refs_8_.refs_4_), channel_id=1, source_target_pairs={{0,66},{2,64},{64,2},{66,0},{1,67},{3,65},{65,3},{67,1},{4,70},{6,... | collective-permute-start | bytes 1572872 | tf_op jit(solution)/shard_map/ppermute | solution.py:22
  71.7 12.2 %collective-permute-start.14 = (bf16[2,512,512]{2,1,0:T(8,128)(2,1)}, bf16[2,512,512]{2,1,0:T(8,128)(2,1)S(1)}, u32[]{:S(2)}, u32[]{:S(2)}) collective-permute-start(bf16[2,512,512]{2,1,0:T(8,128)(2,1)} %collective-permute-done.10.refs_10_.refs_14_), channel_id=1, source_target_pairs={{0,1},{1,0},{2,3},{3,2},{4,5},{5,4},{6,7},{7,6},{8,9},{9,8},{10,11... | collective-permute-start | bytes 3145736 | tf_op jit(solution)/shard_map/ppermute | solution.py:18
  80.6 1.9 %collective-permute-start.13 = (bf16[512,512]{1,0:T(8,128)(2,1)S(1)}, bf16[512,512]{1,0:T(8,128)(2,1)S(1)}, u32[]{:S(2)}, u32[]{:S(2)}) collective-permute-start(bf16[512,512]{1,0:T(8,128)(2,1)S(1)} %collective-permute-done.12.refs_8_), channel_id=1, source_target_pairs={{0,1},{1,0},{2,3},{3,2},{4,5},{5,4},{6,7},{7,6},{8,9},{9,8},{10,11... | collective-permute-start | bytes 1572872 | tf_op jit(solution)/shard_map/ppermute | solution.py:18
  81.9 1.9 %collective-permute-start.16 = (bf16[512,512]{1,0:T(8,128)(2,1)S(1)}, bf16[512,512]{1,0:T(8,128)(2,1)S(1)}, u32[]{:S(2)}, u32[]{:S(2)}) collective-permute-start(bf16[512,512]{1,0:T(8,128)(2,1)S(1)} %collective-permute-done.15.refs_12_), channel_id=1, source_target_pairs={{0,1},{1,0},{2,3},{3,2},{4,5},{5,4},{6,7},{7,6},{8,9},{9,8},{10,11... | collective-permute-start | bytes 1572872 | tf_op jit(solution)/shard_map/ppermute | solution.py:18
  96.0 35.5 %all-to-all-start = ((f16[16,17,8,512]{3,2,1,0:T(8,128)(2,1)}), f16[16,17,8,512]{3,2,1,0:T(8,128)(2,1)S(1)}, u32[]{:S(2)}, u32[]{:S(2)}) async-start(f16[16,17,8,512]{3,2,1,0:T(8,128)(2,1)} %bitcast.7), calls=%async_computation | async-start | bytes 4456448 | tf_op jit(solution)/shard_map/all_to_all | solution.py:243

commit v6 on v5

--- a/solution.py
+++ b/solution.py
@@ -154,7 +154,7 @@
         cost_estimate=pl.CostEstimate(
             flops=2 * rows * cols * depth * len(arrays) * len(ns), bytes_accessed=8 * mib, transcendentals=0
         ),
-    )(jnp.stack([turn_by]), *[in_hbm(v) if n in (1, 3) else v for n in ns for v in lefts[n]], *arrays, *([result] if one else []))
+    )(jnp.stack([turn_by]), *flat, *arrays, *([result] if one else []))
 
 
 def unscale(value):
@@ -209,10 +209,10 @@
     near_mine = trade(theirs, ring, 1)
     both_away = swap(both)
     kept = turn(both, both_away, core)
-    kept_near, kept_far = trade(kept, "x", 1), trade(kept, "x", 3)
+    kept_near, kept_far = in_hbm(trade(kept, "x", 1)), in_hbm(trade(kept, "x", 3))
     near_mine_away = swap(after(near_mine, kept_near, kept_far))
     got = turn(near_mine, near_mine_away, core)
-    got_near, got_far = trade(got, "x", 1), trade(got, "x", 3)
+    got_near, got_far = in_hbm(trade(got, "x", 1)), in_hbm(trade(got, "x", 3))
     near_theirs = trade(after(both[0], near_mine), ring, 1)
     tick = swap(after(got[0, :8, :lane]))
     near_theirs_away = swap(near_theirs)

time: 134 us -> 134 us (level)
  no operation moved by 1% of the time
where the time goes in v6:
time: 134 us
  waiting for transfers between devices  72 us (54%)
  starting transfers between devices  27.5 us (21%)
  Pallas kernels  19.6 us (15%)
  local copies, waits for them, and re-layouts  8.1 us (6%)
  other arithmetic  6.31 us (5%)
    ppermute x11, waiting for transfers between devices, trade(): return lax.ppermute(value, axis, [(i, i ^ bits) for i in range(4)])  39.5 us
    all_to_all x2, waiting for transfers between devices, per_device(): across = lax.all_to_all(packed, ('x', 'z'), 0, 0, tiled=True)  29.4 us
    ppermute x11, starting transfers between devices, trade(): return lax.ppermute(value, axis, [(i, i ^ bits) for i in range(4)])  16.5 us
    pallas_call x3, Pallas kernels, product(): pl.pallas_call(kernel, grid_spec=pltpu.PrefetchScalarGridSpec(num_scalar_...  15.3 us
    all_to_all x2, starting transfers between devices, per_device(): across = lax.all_to_all(packed, ('x', 'z'), 0, 0, tiled=True)  10.9 us
    unnamed x20, local copies, waits for them, and re-layouts  6.68 us
    pallas_call x2, Pallas kernels, place(): pl.pallas_call(kernel, grid_spec=pltpu.PrefetchScalarGridSpec(num_scalar_...  3.33 us
    ppermute x6, waiting for transfers between devices, swap(): return lax.ppermute(value, 'core', [(0, 1), (1, 0)])  3.02 us
  transfers between devices with their start and end apart: 19, of which 16 were waited for; matrix products, arithmetic and copies ran while one was open for 5% of the time, Pallas kernels for 13%

profile of v6, /device:TPU:0, one launch (start us, length us, event | category | flops | bytes accessed | tf_op | source)
XLA Modules:
  0.0 133.6 jit_solution(1249981026152380732)
XLA Ops:
  0.0 1.2 copy-done.6
  1.2 0.3 shard_map.17
  1.6 1.7 %collective-permute-start.1 = (bf16[512,512]{1,0:T(8,128)(2,1)S(1)}, bf16[512,512]{1,0:T(8,128)(2,1)S(1)}, u32[]{:S(2)}, u32[]{:S(2)}) collective-permute-start(bf16[512,512]{1,0:T(8,128)(2,1)S(1)} %get-tuple-element.18), channel_id=1, source_target_pairs={{0,2},{2,0},{64,66},{66,64},{1,3},{3,1},{65,67},{67,65},{4,6},{6,4... | collective-permute-start | bytes 1572872 | tf_op jit(solution)/shard_map/ppermute | solution.py:22
  3.3 0.9 collective-permute-done.refs_1_.refs_7_.refs_11_.refs_3_
  4.2 0.3 shard_map.18.refs_0_
  4.6 2.9 %collective-permute-start.3 = (bf16[2,256,512]{2,1,0:T(8,128)(2,1)S(1)}, bf16[2,256,512]{2,1,0:T(8,128)(2,1)}, u32[]{:S(2)}, u32[]{:S(2)}) collective-permute-start(bf16[2,256,512]{2,1,0:T(8,128)(2,1)S(1)} %shard_map.18.refs_0_), channel_id=1, source_target_pairs={{0,48},{16,32},{32,16},{48,0},{1,49},{17,33},{33,17},{49,1},{2,50}... | collective-permute-start | bytes 1572872 | tf_op jit(solution)/shard_map/ppermute | solution.py:22
  7.7 8.2 %collective-permute-done.1.refs_0_.refs_8_.refs_4_ = bf16[512,512]{1,0:T(8,128)(2,1)S(1)} collective-permute-done((bf16[512,512]{1,0:T(8,128)(2,1)S(1)}, bf16[512,512]{1,0:T(8,128)(2,1)S(1)}, u32[]{:S(2)}, u32[]{:S(2)}) %collective-permute-start.1) | collective-permute-done | bytes 524320 | tf_op jit(solution)/shard_map/ppermute | solution.py:22
  15.9 4.0 %collective-permute-done.3.refs_4_.refs_6_ = bf16[2,256,512]{2,1,0:T(8,128)(2,1)} collective-permute-done((bf16[2,256,512]{2,1,0:T(8,128)(2,1)S(1)}, bf16[2,256,512]{2,1,0:T(8,128)(2,1)}, u32[]{:S(2)}, u32[]{:S(2)}) %collective-permute-start.3) | collective-permute-done | bytes 524320 | tf_op jit(solution)/shard_map/ppermute | solution.py:22
  19.9 1.2 collective-permute-done.2.refs_2_
  21.2 0.8 copy-done.8
  22.0 1.7 %collective-permute-start.7 = (bf16[512,512]{1,0:T(8,128)(2,1)S(1)}, bf16[512,512]{1,0:T(8,128)(2,1)}, u32[]{:S(2)}, u32[]{:S(2)}) collective-permute-start(bf16[512,512]{1,0:T(8,128)(2,1)S(1)} %slice_bitcast_fusion.1), channel_id=1, source_target_pairs={{0,2},{2,0},{64,66},{66,64},{1,3},{3,1},{65,67},{67,65},{4,6},{6,4... | collective-permute-start | bytes 1572872 | tf_op jit(solution)/shard_map/ppermute | solution.py:22
  23.9 0.3 shard_map.19.refs_1_
  24.2 0.4 collective-permute-start.5
  24.6 1.4 %collective-permute-start.6 = (bf16[2,256,512]{2,1,0:T(8,128)(2,1)S(1)}, bf16[2,256,512]{2,1,0:T(8,128)(2,1)S(1)}, u32[]{:S(2)}, u32[]{:S(2)}) collective-permute-start(bf16[2,256,512]{2,1,0:T(8,128)(2,1)S(1)} %shard_map.19.refs_1_), channel_id=1, source_target_pairs={{0,48},{16,32},{32,16},{48,0},{1,49},{17,33},{33,17},{49,1},{2,50}... | collective-permute-start | bytes 1572872 | tf_op jit(solution)/shard_map/ppermute | solution.py:22
  26.0 0.8 copy-done
  26.8 9.7 %collective-permute-done.7.refs_12_.refs_8_ = bf16[512,512]{1,0:T(8,128)(2,1)} collective-permute-done((bf16[512,512]{1,0:T(8,128)(2,1)S(1)}, bf16[512,512]{1,0:T(8,128)(2,1)}, u32[]{:S(2)}, u32[]{:S(2)}) %collective-permute-start.7) | collective-permute-done | bytes 524320 | tf_op jit(solution)/shard_map/ppermute | solution.py:22
  36.6 1.8 %collective-permute-done.5.refs_3_ = bf16[2,256,512]{2,1,0:T(8,128)(2,1)} collective-permute-done((bf16[2,256,512]{2,1,0:T(8,128)(2,1)S(1)}, bf16[2,256,512]{2,1,0:T(8,128)(2,1)}, u32[]{:S(2)}, u32[]{:S(2)}) %collective-permute-start.5) | collective-permute-done | bytes 524320 | tf_op jit(solution)/shard_map/ppermute | solution.py:22
  38.4 1.2 collective-permute-done.6.refs_5_.refs_7_
  39.6 0.4 collective-permute-start.8
  40.0 0.4 copy-done.9
  40.4 1.6 %collective-permute-start.9 = (bf16[2,256,512]{2,1,0:T(8,128)(2,1)}, bf16[2,256,512]{2,1,0:T(8,128)(2,1)}, u32[]{:S(2)}, u32[]{:S(2)}) collective-permute-start(bf16[2,256,512]{2,1,0:T(8,128)(2,1)} %collective-permute-done.5.refs_3_), channel_id=1, source_target_pairs={{0,48},{16,32},{32,16},{48,0},{1,49},{17,33},{33,17},{49,1},{2,50}... | collective-permute-start | bytes 1572872 | tf_op jit(solution)/shard_map/ppermute | solution.py:22
  42.0 3.0 %collective-permute-start.10 = (bf16[2,512,512]{2,1,0:T(8,128)(2,1)S(1)}, bf16[2,512,512]{2,1,0:T(8,128)(2,1)}, u32[]{:S(2)}, u32[]{:S(2)}) collective-permute-start(bf16[2,512,512]{2,1,0:T(8,128)(2,1)S(1)} %get-tuple-element.17.refs_0_.refs_6_.refs_10_.refs_2_), channel_id=1, source_target_pairs={{0,66},{2,64},{64,2},{66,0},{1,67},{3,65},{65,3},{67,1},{4,70},{6,... | collective-permute-start | bytes 3145736 | tf_op jit(solution)/shard_map/ppermute | solution.py:22
  45.0 1.0 copy-done.1
  46.1 1.0 copy-done.4
  47.1 5.5 %shard_map.20 = f32[4,4,17,8,512]{4,3,2,1,0:T(8,128)S(1)} custom-call(s32[1]{0:T(128)} %bitcast.3.where, bf16[2,256,512]{2,1,0:T(8,128)(2,1)S(1)} %copy-done.4, bf16[2,256,512]{2,1,0:T(8,128)(2,1)S(1)} %copy-done.1, bf16[2,256,512]{2,1,0:T(8,128)(2,1)} %copy-done.8, bf16[2,256,512]{2,1,0:T(8,128)(2,1)} %collective-permute-done.5.refs_3_, ...), custom_call_target="tpu_custom_call" | custom-call | flops 3221225472 | bytes 8388608 | tf_op jit(solution)/shard_map/pallas_call | solution.py:146
  52.6 0.5 convert_element_type.33
  53.2 1.7 %collective-permute-done.9.refs_1_.refs_5_ = bf16[2,256,512]{2,1,0:T(8,128)(2,1)} collective-permute-done((bf16[2,256,512]{2,1,0:T(8,128)(2,1)}, bf16[2,256,512]{2,1,0:T(8,128)(2,1)}, u32[]{:S(2)}, u32[]{:S(2)}) %collective-permute-start.9) | collective-permute-done | bytes 524320 | tf_op jit(solution)/shard_map/ppermute | solution.py:22
  54.8 2.9 %shard_map.21 = f32[1,4,17,8,512]{4,3,2,1,0:T(8,128)S(1)} custom-call(s32[1]{0:T(128)} %bitcast.3.where, bf16[2,256,512]{2,1,0:T(8,128)(2,1)} %collective-permute-done.8.refs_0_.refs_4_, bf16[2,256,512]{2,1,0:T(8,128)(2,1)} %collective-permute-done.9.refs_1_.refs_5_, bf16[2,512,512]{2,1,0:T(8,128)(2,1)S(1)} %get-tuple-element.17.refs_0_.refs_6_.refs_10_.refs_2_, ...), custom_call_target="tpu_custom_call" | custom-call | flops 1073741824 | bytes 8388608 | tf_op jit(solution)/shard_map/pallas_call | solution.py:146
  57.9 1.4 %copy-done.7 = f16[4,4,17,8,512]{4,3,2,1,0:T(8,128)(2,1)} copy-done((f16[4,4,17,8,512]{4,3,2,1,0:T(8,128)(2,1)}, f16[4,4,17,8,512]{4,3,2,1,0:T(8,128)(2,1)S(1)}, u32[]{:S(2)}) %copy-start.7) | copy-done | bytes 2228248
  59.3 6.8 %all-to-all-start.1 = ((f16[16,17,8,512]{3,2,1,0:T(8,128)(2,1)}), f16[16,17,8,512]{3,2,1,0:T(8,128)(2,1)}, u32[]{:S(2)}, u32[]{:S(2)}) async-start(f16[16,17,8,512]{3,2,1,0:T(8,128)(2,1)} %bitcast.34), calls=%async_computation.1 | async-start | bytes 4456448 | tf_op jit(solution)/shard_map/all_to_all | solution.py:243
  66.1 1.4 %collective-permute-done.10.refs_10_.refs_14_ = bf16[2,512,512]{2,1,0:T(8,128)(2,1)} collective-permute-done((bf16[2,512,512]{2,1,0:T(8,128)(2,1)S(1)}, bf16[2,512,512]{2,1,0:T(8,128)(2,1)}, u32[]{:S(2)}, u32[]{:S(2)}) %collective-permute-start.10) | collective-permute-done | bytes 1048608 | tf_op jit(solution)/shard_map/ppermute | solution.py:22
  67.5 1.1 slice_bitcast_fusion
  68.5 0.4 collective-permute-start.12
  68.9 2.7 %collective-permute-start.15 = (bf16[512,512]{1,0:T(8,128)(2,1)S(1)}, bf16[512,512]{1,0:T(8,128)(2,1)S(1)}, u32[]{:S(2)}, u32[]{:S(2)}) collective-permute-start(bf16[512,512]{1,0:T(8,128)(2,1)S(1)} %collective-permute-done.1.refs_0_.refs_8_.refs_4_), channel_id=1, source_target_pairs={{0,66},{2,64},{64,2},{66,0},{1,67},{3,65},{65,3},{67,1},{4,70},{6,... | collective-permute-start | bytes 1572872 | tf_op jit(solution)/shard_map/ppermute | solution.py:22
  71.7 8.9 %collective-permute-done.12.refs_8_ = bf16[512,512]{1,0:T(8,128)(2,1)S(1)} collective-permute-done((bf16[512,512]{1,0:T(8,128)(2,1)S(1)}, bf16[512,512]{1,0:T(8,128)(2,1)S(1)}, u32[]{:S(2)}, u32[]{:S(2)}) %collective-permute-start.12) | collective-permute-done | bytes 524320 | tf_op jit(solution)/shard_map/ppermute | solution.py:22
  80.6 1.3 collective-permute-done.15.refs_12_
  81.9 0.6 collective-permute-done.13.refs_9_
  82.5 1.3 collective-permute-done.16.refs_13_
  83.9 6.9 %shard_map.22 = f32[4,4,17,8,512]{4,3,2,1,0:T(8,128)S(1)} custom-call(s32[1]{0:T(128)} %bitcast.3.where, bf16[2,256,512]{2,1,0:T(8,128)(2,1)S(1)} %copy-done.5, bf16[2,256,512]{2,1,0:T(8,128)(2,1)S(1)} %copy-done.2, bf16[2,256,512]{2,1,0:T(8,128)(2,1)} %copy-done.8, bf16[2,256,512]{2,1,0:T(8,128)(2,1)} %collective-permute-done.5.refs_3_, ...), custom_call_target="tpu_custom_call" | custom-call | flops 4294967296 | bytes 8388608 | tf_op jit(solution)/shard_map/pallas_call | solution.py:146
  90.8 1.9 %convert_element_type.35 = f16[4,4,17,8,512]{4,3,2,1,0:T(8,128)(2,1)} convert(f32[4,4,17,8,512]{4,3,2,1,0:T(8,128)S(1)} %shard_map.22) | non-fusion elementwise | flops 1114112 | bytes 6684672 | tf_op jit(solution)/shard_map/convert_element_type | solution.py:242
  92.7 3.2 %all-to-all-done.1 = f16[16,17,8,512]{3,2,1,0:T(8,128)(2,1)} async-done(((f16[16,17,8,512]{3,2,1,0:T(8,128)(2,1)}), f16[16,17,8,512]{3,2,1,0:T(8,128)(2,1)}, u32[]{:S(2)}, u32[]{:S(2)}) %all-to-all-start.1) | async-done | bytes 2228256 | tf_op jit(solution)/shard_map/all_to_all | solution.py:243
  96.0 4.1 %all-to-all-start = ((f16[16,17,8,512]{3,2,1,0:T(8,128)(2,1)}), f16[16,17,8,512]{3,2,1,0:T(8,128)(2,1)S(1)}, u32[]{:S(2)}, u32[]{:S(2)}) async-start(f16[16,17,8,512]{3,2,1,0:T(8,128)(2,1)} %bitcast.7), calls=%async_computation | async-start | bytes 4456448 | tf_op jit(solution)/shard_map/all_to_all | solution.py:243
  100.2 1.0 divide_bitcast_fusion.1
  101.2 2.2 %multiply_reduce_fusion.1 = f32[4,16,8,512]{3,2,1,0:T(8,128)S(1)} fusion(f16[4,4,17,8,512]{4,3,2,1,0:T(8,128)(2,1)} %bitcast.10, f32[4,4,8,512]{3,2,1,0:T(8,128)S(1)} %divide_bitcast_fusion.1), kind=kLoop, calls=%fused_computation.1 | loop fusion | flops 2883584 | bytes 3407872 | tf_op jit(solution)/shard_map/reduce_sum | solution.py:246
  103.5 1.7 %shard_map.23.refs_4_ = f32[64,8192]{1,0:T(8,128)} custom-call(s32[7]{0:T(128)S(1)} %stack.37.where, f32[2,64,512]{2,1,0:T(8,128)S(1)} %bitcast.29, f32[2,64,512]{2,1,0:T(8,128)S(1)} %bitcast.28, f32[2,64,512]{2,1,0:T(8,128)S(1)} %bitcast.27, f32[2,64,512]{2,1,0:T(8,128)S(1)} %bitcast.26), custom_call_target="tpu_custom_call" | custom-call | tf_op jit(solution)/shard_map/pallas_call | solution.py:188
  105.3 26.2 %all-to-all-done = f16[16,17,8,512]{3,2,1,0:T(8,128)(2,1)S(1)} async-done(((f16[16,17,8,512]{3,2,1,0:T(8,128)(2,1)}), f16[16,17,8,512]{3,2,1,0:T(8,128)(2,1)S(1)}, u32[]{:S(2)}, u32[]{:S(2)}) %all-to-all-start) | async-done | bytes 2228256 | tf_op jit(solution)/shard_map/all_to_all | solution.py:243
  131.5 0.5 multiply_reduce_fusion
  132.0 1.6 %shard_map.24 = f32[64,8192]{1,0:T(8,128)} custom-call(s32[7]{0:T(128)S(1)} %stack.33.where, f32[2,64,512]{2,1,0:T(8,128)S(1)} %bitcast.33, f32[2,64,512]{2,1,0:T(8,128)S(1)} %bitcast.32, f32[2,64,512]{2,1,0:T(8,128)S(1)} %bitcast.31, f32[2,64,512]{2,1,0:T(8,128)S(1)} %bitcast.30, f32[64,8192]{1,0:T(8,128)} %shard_map.23.refs_4_), custom_call_target="tpu_custom_call", output_to_operand_aliasing={{}: (5, {})} | custom-call | tf_op jit(solution)/shard_map/pallas_call | solution.py:188
  (32 shorter events, 1.1 us)
Async XLA Ops:
  0.0 1.2 copy-start.6
  1.5 2.7 %collective-permute-start = (bf16[2,512,512]{2,1,0:T(8,128)(2,1)S(1)}, bf16[2,512,512]{2,1,0:T(8,128)(2,1)S(1)}, u32[]{:S(2)}, u32[]{:S(2)}) collective-permute-start(bf16[2,512,512]{2,1,0:T(8,128)(2,1)S(1)} %get-tuple-element.17.refs_0_.refs_6_.refs_10_.refs_2_), channel_id=1, source_target_pairs={{0,1},{1,0},{2,3},{3,2},{4,5},{5,4},{6,7},{7,6},{8,9},{9,8},{10,11... | collective-permute-start | bytes 3145736 | tf_op jit(solution)/shard_map/ppermute | solution.py:18
  1.6 14.3 %collective-permute-start.1 = (bf16[512,512]{1,0:T(8,128)(2,1)S(1)}, bf16[512,512]{1,0:T(8,128)(2,1)S(1)}, u32[]{:S(2)}, u32[]{:S(2)}) collective-permute-start(bf16[512,512]{1,0:T(8,128)(2,1)S(1)} %get-tuple-element.18), channel_id=1, source_target_pairs={{0,2},{2,0},{64,66},{66,64},{1,3},{3,1},{65,67},{67,65},{4,6},{6,4... | collective-permute-start | bytes 1572872 | tf_op jit(solution)/shard_map/ppermute | solution.py:22
  4.6 19.1 %copy-start.3 = (bf16[2,256,512]{2,1,0:T(8,128)(2,1)}, bf16[2,256,512]{2,1,0:T(8,128)(2,1)S(1)}, u32[]{:S(2)}) copy-start(bf16[2,256,512]{2,1,0:T(8,128)(2,1)S(1)} %shard_map.18.refs_0_) | copy-start | bytes 1572868
  4.6 15.4 %collective-permute-start.3 = (bf16[2,256,512]{2,1,0:T(8,128)(2,1)S(1)}, bf16[2,256,512]{2,1,0:T(8,128)(2,1)}, u32[]{:S(2)}, u32[]{:S(2)}) collective-permute-start(bf16[2,256,512]{2,1,0:T(8,128)(2,1)S(1)} %shard_map.18.refs_0_), channel_id=1, source_target_pairs={{0,48},{16,32},{32,16},{48,0},{1,49},{17,33},{33,17},{49,1},{2,50}... | collective-permute-start | bytes 1572872 | tf_op jit(solution)/shard_map/ppermute | solution.py:22
  7.5 13.7 %collective-permute-start.2 = (bf16[2,256,512]{2,1,0:T(8,128)(2,1)S(1)}, bf16[2,256,512]{2,1,0:T(8,128)(2,1)S(1)}, u32[]{:S(2)}, u32[]{:S(2)}) collective-permute-start(bf16[2,256,512]{2,1,0:T(8,128)(2,1)S(1)} %shard_map.18.refs_0_), channel_id=1, source_target_pairs={{0,16},{16,0},{32,48},{48,32},{1,17},{17,1},{33,49},{49,33},{2,18}... | collective-permute-start | bytes 1572872 | tf_op jit(solution)/shard_map/ppermute | solution.py:22
  21.2 0.8 copy-start.8
  22.0 1.9 %collective-permute-start.4 = (bf16[512,512]{1,0:T(8,128)(2,1)S(1)}, bf16[512,512]{1,0:T(8,128)(2,1)S(1)}, u32[]{:S(2)}, u32[]{:S(2)}) collective-permute-start(bf16[512,512]{1,0:T(8,128)(2,1)S(1)} %collective-permute-done.1.refs_0_.refs_8_.refs_4_), channel_id=1, source_target_pairs={{0,1},{1,0},{2,3},{3,2},{4,5},{5,4},{6,7},{7,6},{8,9},{9,8},{10,11... | collective-permute-start | bytes 1572872 | tf_op jit(solution)/shard_map/ppermute | solution.py:18
  22.0 14.5 %collective-permute-start.7 = (bf16[512,512]{1,0:T(8,128)(2,1)S(1)}, bf16[512,512]{1,0:T(8,128)(2,1)}, u32[]{:S(2)}, u32[]{:S(2)}) collective-permute-start(bf16[512,512]{1,0:T(8,128)(2,1)S(1)} %slice_bitcast_fusion.1), channel_id=1, source_target_pairs={{0,2},{2,0},{64,66},{66,64},{1,3},{3,1},{65,67},{67,65},{4,6},{6,4... | collective-permute-start | bytes 1572872 | tf_op jit(solution)/shard_map/ppermute | solution.py:22
  24.2 14.2 %collective-permute-start.5 = (bf16[2,256,512]{2,1,0:T(8,128)(2,1)S(1)}, bf16[2,256,512]{2,1,0:T(8,128)(2,1)}, u32[]{:S(2)}, u32[]{:S(2)}) collective-permute-start(bf16[2,256,512]{2,1,0:T(8,128)(2,1)S(1)} %shard_map.19.refs_1_), channel_id=1, source_target_pairs={{0,16},{16,0},{32,48},{48,32},{1,17},{17,1},{33,49},{49,33},{2,18}... | collective-permute-start | bytes 1572872 | tf_op jit(solution)/shard_map/ppermute | solution.py:22
  24.6 15.0 %collective-permute-start.6 = (bf16[2,256,512]{2,1,0:T(8,128)(2,1)S(1)}, bf16[2,256,512]{2,1,0:T(8,128)(2,1)S(1)}, u32[]{:S(2)}, u32[]{:S(2)}) collective-permute-start(bf16[2,256,512]{2,1,0:T(8,128)(2,1)S(1)} %shard_map.19.refs_1_), channel_id=1, source_target_pairs={{0,48},{16,32},{32,16},{48,0},{1,49},{17,33},{33,17},{49,1},{2,50}... | collective-permute-start | bytes 1572872 | tf_op jit(solution)/shard_map/ppermute | solution.py:22
  26.0 0.8 copy-start
  36.6 8.5 %collective-permute-start.11 = (bf16[512,512]{1,0:T(8,128)(2,1)}, bf16[512,512]{1,0:T(8,128)(2,1)}, u32[]{:S(2)}, u32[]{:S(2)}) collective-permute-start(bf16[512,512]{1,0:T(8,128)(2,1)} %collective-permute-done.7.refs_12_.refs_8_), channel_id=1, source_target_pairs={{0,1},{1,0},{2,3},{3,2},{4,5},{5,4},{6,7},{7,6},{8,9},{9,8},{10,11... | collective-permute-start | bytes 1572872 | tf_op jit(solution)/shard_map/ppermute | solution.py:18
  39.6 0.8 copy-start.9
  39.6 13.6 %collective-permute-start.8 = (bf16[2,256,512]{2,1,0:T(8,128)(2,1)}, bf16[2,256,512]{2,1,0:T(8,128)(2,1)}, u32[]{:S(2)}, u32[]{:S(2)}) collective-permute-start(bf16[2,256,512]{2,1,0:T(8,128)(2,1)} %collective-permute-done.3.refs_4_.refs_6_), channel_id=1, source_target_pairs={{0,16},{16,0},{32,48},{48,32},{1,17},{17,1},{33,49},{49,33},{2,18}... | collective-permute-start | bytes 1572872 | tf_op jit(solution)/shard_map/ppermute | solution.py:22
  40.4 14.4 %collective-permute-start.9 = (bf16[2,256,512]{2,1,0:T(8,128)(2,1)}, bf16[2,256,512]{2,1,0:T(8,128)(2,1)}, u32[]{:S(2)}, u32[]{:S(2)}) collective-permute-start(bf16[2,256,512]{2,1,0:T(8,128)(2,1)} %collective-permute-done.5.refs_3_), channel_id=1, source_target_pairs={{0,48},{16,32},{32,16},{48,0},{1,49},{17,33},{33,17},{49,1},{2,50}... | collective-permute-start | bytes 1572872 | tf_op jit(solution)/shard_map/ppermute | solution.py:22
  42.0 25.5 %collective-permute-start.10 = (bf16[2,512,512]{2,1,0:T(8,128)(2,1)S(1)}, bf16[2,512,512]{2,1,0:T(8,128)(2,1)}, u32[]{:S(2)}, u32[]{:S(2)}) collective-permute-start(bf16[2,512,512]{2,1,0:T(8,128)(2,1)S(1)} %get-tuple-element.17.refs_0_.refs_6_.refs_10_.refs_2_), channel_id=1, source_target_pairs={{0,66},{2,64},{64,2},{66,0},{1,67},{3,65},{65,3},{67,1},{4,70},{6,... | collective-permute-start | bytes 3145736 | tf_op jit(solution)/shard_map/ppermute | solution.py:22
  45.0 1.0 copy-start.1
  46.1 1.0 copy-start.4
  57.9 1.4 %copy-start.7 = (f16[4,4,17,8,512]{4,3,2,1,0:T(8,128)(2,1)}, f16[4,4,17,8,512]{4,3,2,1,0:T(8,128)(2,1)S(1)}, u32[]{:S(2)}) copy-start(f16[4,4,17,8,512]{4,3,2,1,0:T(8,128)(2,1)S(1)} %convert_dynamic-update-slice_fusion) | copy-start | bytes 6684676
  59.3 24.6 %copy-start.2 = (bf16[2,256,512]{2,1,0:T(8,128)(2,1)S(1)}, bf16[2,256,512]{2,1,0:T(8,128)(2,1)}, u32[]{:S(2)}) copy-start(bf16[2,256,512]{2,1,0:T(8,128)(2,1)} %copy-done) | copy-start | bytes 1572868
  59.3 24.6 %copy-start.5 = (bf16[2,256,512]{2,1,0:T(8,128)(2,1)S(1)}, bf16[2,256,512]{2,1,0:T(8,128)(2,1)}, u32[]{:S(2)}) copy-start(bf16[2,256,512]{2,1,0:T(8,128)(2,1)} %copy-done.3) | copy-start | bytes 1572868
  59.3 36.7 %all-to-all-start.1 = ((f16[16,17,8,512]{3,2,1,0:T(8,128)(2,1)}), f16[16,17,8,512]{3,2,1,0:T(8,128)(2,1)}, u32[]{:S(2)}, u32[]{:S(2)}) async-start(f16[16,17,8,512]{3,2,1,0:T(8,128)(2,1)} %bitcast.34), calls=%async_computation.1 | async-start | bytes 4456448 | tf_op jit(solution)/shard_map/all_to_all | solution.py:243
  68.5 12.1 %collective-permute-start.12 = (bf16[512,512]{1,0:T(8,128)(2,1)S(1)}, bf16[512,512]{1,0:T(8,128)(2,1)S(1)}, u32[]{:S(2)}, u32[]{:S(2)}) collective-permute-start(bf16[512,512]{1,0:T(8,128)(2,1)S(1)} %slice_bitcast_fusion), channel_id=1, source_target_pairs={{0,2},{2,0},{64,66},{66,64},{1,3},{3,1},{65,67},{67,65},{4,6},{6,4... | collective-permute-start | bytes 1572872 | tf_op jit(solution)/shard_map/ppermute | solution.py:22
  68.9 13.0 %collective-permute-start.15 = (bf16[512,512]{1,0:T(8,128)(2,1)S(1)}, bf16[512,512]{1,0:T(8,128)(2,1)S(1)}, u32[]{:S(2)}, u32[]{:S(2)}) collective-permute-start(bf16[512,512]{1,0:T(8,128)(2,1)S(1)} %collective-permute-done.1.refs_0_.refs_8_.refs_4_), channel_id=1, source_target_pairs={{0,66},{2,64},{64,2},{66,0},{1,67},{3,65},{65,3},{67,1},{4,70},{6,... | collective-permute-start | bytes 1572872 | tf_op jit(solution)/shard_map/ppermute | solution.py:22
  71.7 12.2 %collective-permute-start.14 = (bf16[2,512,512]{2,1,0:T(8,128)(2,1)}, bf16[2,512,512]{2,1,0:T(8,128)(2,1)S(1)}, u32[]{:S(2)}, u32[]{:S(2)}) collective-permute-start(bf16[2,512,512]{2,1,0:T(8,128)(2,1)} %collective-permute-done.10.refs_10_.refs_14_), channel_id=1, source_target_pairs={{0,1},{1,0},{2,3},{3,2},{4,5},{5,4},{6,7},{7,6},{8,9},{9,8},{10,11... | collective-permute-start | bytes 3145736 | tf_op jit(solution)/shard_map/ppermute | solution.py:18
  80.6 1.9 %collective-permute-start.13 = (bf16[512,512]{1,0:T(8,128)(2,1)S(1)}, bf16[512,512]{1,0:T(8,128)(2,1)S(1)}, u32[]{:S(2)}, u32[]{:S(2)}) collective-permute-start(bf16[512,512]{1,0:T(8,128)(2,1)S(1)} %collective-permute-done.12.refs_8_), channel_id=1, source_target_pairs={{0,1},{1,0},{2,3},{3,2},{4,5},{5,4},{6,7},{7,6},{8,9},{9,8},{10,11... | collective-permute-start | bytes 1572872 | tf_op jit(solution)/shard_map/ppermute | solution.py:18
  81.9 1.9 %collective-permute-start.16 = (bf16[512,512]{1,0:T(8,128)(2,1)S(1)}, bf16[512,512]{1,0:T(8,128)(2,1)S(1)}, u32[]{:S(2)}, u32[]{:S(2)}) collective-permute-start(bf16[512,512]{1,0:T(8,128)(2,1)S(1)} %collective-permute-done.15.refs_12_), channel_id=1, source_target_pairs={{0,1},{1,0},{2,3},{3,2},{4,5},{5,4},{6,7},{7,6},{8,9},{9,8},{10,11... | collective-permute-start | bytes 1572872 | tf_op jit(solution)/shard_map/ppermute | solution.py:18
  96.0 35.5 %all-to-all-start = ((f16[16,17,8,512]{3,2,1,0:T(8,128)(2,1)}), f16[16,17,8,512]{3,2,1,0:T(8,128)(2,1)S(1)}, u32[]{:S(2)}, u32[]{:S(2)}) async-start(f16[16,17,8,512]{3,2,1,0:T(8,128)(2,1)} %bitcast.7), calls=%async_computation | async-start | bytes 4456448 | tf_op jit(solution)/shard_map/all_to_all | solution.py:243
